TPU v7x, 32 devices: a whole 2x2x4 slice. The times are simulated.
32 devices in a mesh: groups: 2 (over y), dp: 4 (over z), tgt: 4 (over x, core).
Axes of the slice: x: 2, y: 2, z: 4, core: 2. Of those that a mesh axis runs over, the one named last changes fastest.
Arguments:
- hidden: bfloat16 [6144, 4096], P(('groups', 'dp', 'tgt')), parts along dimension 0, may hold values from -6 to 6
- cotangent: bfloat16 [6144, 4096], P(('groups', 'dp', 'tgt')), parts along dimension 0, may hold values from -6 to 6
- adapter_down_weight: bfloat16 [4096, 64], replicated, may hold values from -0.09375 to 0.09375
- adapter_up_weight: bfloat16 [64, 4096], replicated, may hold values from -0.75 to 0.75
- width_projection_factor: bfloat16 [4096, 512], replicated, may hold values from -0.09375 to 0.09375
- rank_projection_factor: bfloat16 [64, 8], replicated, may hold values from -0.75 to 0.75
- targets: bfloat16 [8, 768, 8192], P(('groups', 'dp'), 'tgt'), parts along dimension 0, may hold values from -100 to 100
- strata: int32 [768], P(('groups', 'dp', 'tgt')), parts along dimension 0, may hold values from 0 to 31
- keep: int32 [768], P(('groups', 'dp', 'tgt')), parts along dimension 0, may hold values from 0 to 1
- shard_example_count: int32 [32], P(('groups', 'dp', 'tgt')), parts along dimension 0, may hold values from 18 to 24
- stratum_owner_table: int32 [32], replicated, may hold values from 0 to 3, as said below
Outputs:
- selection: float32 [768], P(('groups', 'dp', 'tgt')), parts along dimension 0
There are 2 independent parts, one for each index of `groups`. A program takes and returns all parts, laid end to end along the dimension named above; an argument that names none is the same for every part. Nothing has to cross between parts.
Inputs may be any that keep to these rules, and one draw needn't show every extreme that they name: `stratum_owner_table`: each of the 4 owners holds exactly 8 strata.
All inputs are finite; a program needn't handle non-finite values.
Results may differ from a plain program's by a relative error of at most 0.0029.
Values may be sent and summed in bfloat16 or wider, within the bound.
No kernel may reach another device: no remote copies, remote signals or barrier semaphores. Data moves between devices by JAX's collectives and lax.ppermute only.
A program may use at most 64 MiB of HBM per device.

v0:
```python
import math

import jax
import jax.numpy as jnp
from jax import lax
from jax.sharding import PartitionSpec as P

FEAT = 8192
CAP = 2
TGT = 768
TASKS = 16


epsilon = 1e-06


def contracted_row_sums(row_block, col_block):
    return lax.dot_general(
        row_block, col_block, (((1,), (1,)), ((), ())), preferred_element_type=jnp.float32
    )


def inverse_norms(values):
    widened = values.astype(jnp.float32)
    return lax.rsqrt(jnp.sum(widened * widened, axis=1) + epsilon)


def task_terms(row_block, row_inv, col_block, col_inv, first_index):
    per_task = TGT // TASKS
    products = contracted_row_sums(row_block, col_block)
    aligned = math.sqrt(FEAT) * products * row_inv[:, None] * col_inv[None, :]
    target_ids = (first_index + jnp.arange(col_block.shape[0], dtype=jnp.int32)) // per_task
    task_mask = (target_ids[:, None] == jnp.arange(TASKS, dtype=jnp.int32)[None, :]).astype(
        jnp.float32
    )
    return jnp.dot(jnp.maximum(aligned, 0.0), task_mask, precision=lax.Precision.HIGHEST)


def per_example(values, examples):
    return values.reshape(examples, -1, values.shape[1])


def shards(
    hidden,
    cotangent,
    adapter_down_weight,
    adapter_up_weight,
    width_projection_factor,
    rank_projection_factor,
    targets,
    strata,
    keep,
    shard_example_count,
    stratum_owner_table,
):
    examples = strata.shape[0]
    strata_total = stratum_owner_table.shape[0]
    ordinal = jnp.arange(examples, dtype=jnp.int32)
    usable = ordinal < shard_example_count[0]
    is_live = jnp.logical_and(keep == 1, usable)
    member = strata[:, None] == jnp.arange(strata_total, dtype=jnp.int32)[None, :]
    local_counts = jnp.sum(jnp.logical_and(member, is_live[:, None]).astype(jnp.float32), axis=0)
    counts = lax.psum(local_counts, ("dp", "tgt"))
    down_activation = jnp.dot(
        hidden, adapter_down_weight, preferred_element_type=jnp.float32
    ).astype(jnp.bfloat16)
    up_backward_product = contracted_row_sums(cotangent, adapter_up_weight).astype(jnp.bfloat16)
    wide_hidden = jnp.dot(
        hidden, width_projection_factor, preferred_element_type=jnp.float32
    ).astype(jnp.bfloat16)
    wide_back = jnp.dot(
        cotangent, width_projection_factor, preferred_element_type=jnp.float32
    ).astype(jnp.bfloat16)
    rank_down = jnp.dot(
        down_activation, rank_projection_factor, preferred_element_type=jnp.float32
    ).astype(jnp.bfloat16)
    rank_up = jnp.dot(
        up_backward_product, rank_projection_factor, preferred_element_type=jnp.float32
    ).astype(jnp.bfloat16)
    up_grad = jnp.einsum(
        "esr,esd->erd",
        per_example(rank_down, examples),
        per_example(wide_back, examples),
        preferred_element_type=jnp.float32,
    )
    down_grad = jnp.einsum(
        "esd,esr->edr",
        per_example(wide_hidden, examples),
        per_example(rank_up, examples),
        preferred_element_type=jnp.float32,
    )
    features = jnp.concatenate(
        [up_grad.reshape(examples, -1), down_grad.reshape(examples, -1)], axis=1
    ).astype(jnp.bfloat16)
    owner_of = jnp.sum(jnp.where(member, stratum_owner_table[None, :], 0), axis=1)
    earlier = ordinal[:, None] > ordinal[None, :]
    same_owner = owner_of[:, None] == owner_of[None, :]
    ahead = jnp.logical_and(jnp.logical_and(earlier, same_owner), is_live[None, :])
    slot_rank = jnp.sum(ahead.astype(jnp.int32), axis=1)
    is_sent = jnp.logical_and(is_live, slot_rank < CAP)
    owner_count = lax.axis_size("dp")
    slot_index = owner_of * CAP + slot_rank
    slot_ids = jnp.arange(owner_count * CAP, dtype=jnp.int32)
    dispatch = jnp.logical_and(slot_ids[:, None] == slot_index[None, :], is_sent[None, :])
    outgoing = jnp.dot(
        dispatch.astype(jnp.bfloat16), features, preferred_element_type=jnp.float32
    ).astype(jnp.bfloat16)
    received = lax.all_to_all(
        outgoing.reshape(owner_count, CAP, -1), "dp", split_axis=0, concat_axis=0, tiled=True
    )
    owner_rows = received.reshape(owner_count * CAP, -1)
    own_targets = targets[0]
    target_inv = inverse_norms(own_targets)
    offset = lax.axis_index("tgt") * own_targets.shape[0]
    row_piece = lax.all_gather(owner_rows, "tgt", axis=0, tiled=True)
    partials = task_terms(row_piece, inverse_norms(row_piece), own_targets, target_inv, offset)
    task_sums = lax.psum_scatter(partials, "tgt", scatter_dimension=0, tiled=True)
    raw_owner = jnp.max(task_sums / (TGT // TASKS), axis=1)
    returned = lax.all_to_all(
        raw_owner.reshape(owner_count, CAP), "dp", split_axis=0, concat_axis=0, tiled=True
    ).reshape(owner_count * CAP)
    raw_score = jnp.sum(jnp.where(dispatch, returned[:, None], 0.0), axis=0)
    stratum_count = jnp.sum(jnp.where(member, counts[None, :], 0.0), axis=1)
    weight = jnp.sqrt(jnp.sum(counts) / (strata_total * jnp.maximum(stratum_count, 1.0)))
    return jnp.where(is_sent, raw_score * weight, 0.0)


def solution(mesh):
    return jax.shard_map(
        shards,
        mesh=mesh,
        in_specs=(
            P(("groups", "dp", "tgt"), None),
            P(("groups", "dp", "tgt"), None),
            P(),
            P(),
            P(),
            P(),
            P(("groups", "dp"), "tgt", None),
            P(("groups", "dp", "tgt")),
            P(("groups", "dp", "tgt")),
            P(("groups", "dp", "tgt")),
            P(),
        ),
        out_specs=P(("groups", "dp", "tgt")),
        check_vma=False,
    )
```

profile of v0, /device:TPU:0, one launch (start us, length us, event | category | flops | bytes accessed | tf_op | source)
XLA Modules:
  0.0 93.7 jit_solution(1229232755631329175)
XLA Ops:
  0.0 0.0 copy-start
  0.8 0.7 compare_and_fusion.1
  1.4 0.9 select_reduce_fusion.1
  2.3 0.2 convert_reduce_fusion.1
  2.5 0.7 compare_and_fusion
  3.2 2.3 %fusion.15 = bf16[192,8]{0,1:T(8,128)(2,1)S(1)} fusion(bf16[64,8]{0,1:T(8,128)(2,1)} %param.16, bf16[192,4096]{1,0:T(8,128)(2,1)} %param.12, bf16[64,4096]{1,0:T(8,128)(2,1)} %param.14), kind=kOutput, calls=%fused_computation.17 | convolution fusion | flops 100873728 | bytes 2101248 | tf_op jit(solution)/shard_map/dot_general | solution.py:77
  5.5 0.1 reshape.70
  5.6 0.0 copy-done
  5.6 3.3 %convolution_convert_fusion.1 = bf16[24,512,8]{1,2,0:T(8,128)(2,1)S(1)} fusion(bf16[192,4096]{1,0:T(8,128)(2,1)S(1)} %copy-done, bf16[4096,512]{1,0:T(8,128)(2,1)} %param.15, bf16[24,8,8]{1,0,2:T(8,128)(2,1)S(1)} %reshape.70), kind=kOutput, calls=%fused_computation.4 | convolution fusion | flops 807075840 | bytes 5966848 | tf_op jit(solution)/shard_map/esd,esr->edr/dot_general | solution.py:86
  8.9 0.0 copy-start.2
  8.9 0.8 copy.25
  9.8 0.3 copy.26
  10.1 0.0 copy-done.2
  10.1 0.0 copy-start.1
  10.1 1.9 %fusion.16 = bf16[192,8]{0,1:T(8,128)(2,1)S(1)} fusion(bf16[64,8]{0,1:T(8,128)(2,1)S(1)} %copy-done.2, bf16[192,4096]{1,0:T(8,128)(2,1)S(1)} %copy-done, bf16[4096,64]{0,1:T(8,128)(2,1)} %param.13), kind=kOutput, calls=%fused_computation.18 | convolution fusion | flops 100873728 | bytes 2101248 | tf_op jit(solution)/shard_map/dot_general | solution.py:74
  12.0 0.7 reshape.66
  12.8 0.0 copy-done.1
  12.8 3.3 %convolution_convert_fusion.3 = bf16[24,8,512]{2,1,0:T(8,128)(2,1)S(1)} fusion(bf16[192,4096]{1,0:T(8,128)(2,1)S(1)} %copy-done.1, bf16[4096,512]{1,0:T(8,128)(2,1)} %param.15, bf16[24,8,8]{1,0,2:T(8,128)(2,1)} %reshape.66), kind=kOutput, calls=%fused_computation.6 | convolution fusion | flops 807075840 | bytes 5966848 | tf_op jit(solution)/shard_map/esr,esd->erd/dot_general | solution.py:80
  16.1 0.1 copy.28
  16.2 0.2 convolution_convert_fusion
  16.4 0.7 reshape.72
  17.1 6.3 %all-to-all-start = ((bf16[4,2,8192]{2,1,0:T(2,128)(2,1)}), bf16[4,2,8192]{2,1,0:T(2,128)(2,1)S(1)}, u32[]{:S(2)}, u32[]{:S(2)}) async-start(bf16[4,2,8192]{2,1,0:T(2,128)(2,1)} %reshape.72), calls=%async_computation | async-start | bytes 262144 | tf_op jit(solution)/shard_map/all_to_all | solution.py:108
  23.4 0.7 convert_reduce_fusion
  24.2 0.0 copy-start.3
  24.2 0.0 copy-start.4
  24.2 2.6 %multiply_reduce_fusion = f32[192]{0:T(256)S(1)} fusion(bf16[1,192,8192]{2,1,0:T(8,128)(2,1)} %param.17), kind=kLoop, calls=%fused_computation.1 | loop fusion | flops 4718400 | bytes 3146496 | tf_op jit(solution)/shard_map/reduce_sum | solution.py:25
  26.8 33.1 %psum.7 = f32[32]{0:T(128)S(1)} all-reduce(f32[32]{0:T(128)S(1)} %convert_reduce_fusion), channel_id=1, replica_groups=mesh['groups'=2,'dp'=4,'tgt'=4] {'dp','tgt'}, use_global_device_ids=true, to_apply=%region_8.9 | all-reduce | flops 32 | bytes 256 | tf_op jit(solution)/shard_map/psum | solution.py:63
  59.9 0.0 copy-done.3
  59.9 0.2 select_reduce_fusion
  60.1 0.6 reduce_sum.78
  60.7 0.0 copy-done.4
  60.7 0.6 dynamic-slice
  62.0 0.0 all-to-all-done
  62.0 0.1 reshape.73
  62.0 6.5 %all_gather.3 = bf16[32,8192]{1,0:T(8,128)(2,1)S(1)} all-gather(bf16[8,8192]{1,0:T(8,128)(2,1)S(1)} %reshape.73), channel_id=1, replica_groups=mesh['groups'=2,'dp'=4,'tgt'=4] {'tgt'}, dimensions={0}, use_global_device_ids=true | all-gather | bytes 655360 | tf_op jit(solution)/shard_map/all_gather | solution.py:115
  68.6 0.2 multiply_reduce_fusion.1
  68.8 3.0 %fusion.10 = f32[32,192]{1,0:T(8,128)S(1)} fusion(bf16[32,8192]{1,0:T(8,128)(2,1)S(1)} %all_gather.3, bf16[1,192,8192]{2,1,0:T(8,128)(2,1)} %param.17, f32[192]{0:T(256)S(1)} %add_rsqrt_fusion, f32[32]{0:T(128)S(1)} %rsqrt_multiply_fusion), kind=kOutput, calls=%fused_computation.14 | convolution fusion | flops 100681728 | bytes 3695488 | tf_op jit(solution)/shard_map/dot_general | solution.py:18
  71.8 0.2 fusion.20
  72.0 11.1 %all-reduce = f32[32,16]{1,0:T(8,128)S(1)} all-reduce(f32[32,16]{1,0:T(8,128)S(1)} %fusion.20), channel_id=2, replica_groups=mesh['groups'=2,'dp'=4,'tgt'=4] {'tgt'}, use_global_device_ids=true, to_apply=%region_4.5.clone | all-reduce | flops 512 | bytes 4096
  83.2 0.1 fusion.27
  83.3 0.1 all_to_all.10
  83.4 7.9 %all_to_all.14 = f32[4,1,2]{2,1,0:T(1,128)S(1)} all-to-all(f32[4,1,2]{2,1,0:T(1,128)S(1)} %bitcast.45), channel_id=1, replica_groups=mesh['groups'=2,'dp'=4,'tgt'=4] {'dp'}, dimensions={0} | all-to-all | bytes 64 | tf_op jit(solution)/shard_map/all_to_all | solution.py:119
  91.2 0.5 broadcast.76
  91.7 0.7 reduce.3
  92.4 0.1 broadcast_in_dim.61
  92.5 0.1 select_reduce_fusion.2
  92.6 1.1 %multiply_select_fusion = f32[24]{0:T(128)} fusion(pred[24]{0:T(512)(128)(4,1)S(1)} %compare_and_fusion, f32[24]{0:T(128)S(1)} %select_reduce_fusion.2, f32[24]{0:T(128)S(1)} %select_reduce_fusion, f32[]{:T(128)} %reduce_sum.78), kind=kLoop, calls=%fused_computation.48 | loop fusion | flops 120 | bytes 316 | tf_op jit(solution)/shard_map/jit(_where)/select_n | solution.py:125
  (4 shorter events, 0.0 us)
Async XLA Ops:
  0.0 5.6 %copy-start = (bf16[192,4096]{1,0:T(8,128)(2,1)S(1)}, bf16[192,4096]{1,0:T(8,128)(2,1)}, u32[]{:S(2)}) copy-start(bf16[192,4096]{1,0:T(8,128)(2,1)} %param.11) | copy-start | bytes 4718596
  8.9 1.2 %copy-start.2 = (bf16[64,8]{0,1:T(8,128)(2,1)S(1)}, bf16[64,8]{0,1:T(8,128)(2,1)}, u32[]{:S(2)}) copy-start(bf16[64,8]{0,1:T(8,128)(2,1)} %param.16) | copy-start | bytes 3076
  10.1 2.7 %copy-start.1 = (bf16[192,4096]{1,0:T(8,128)(2,1)S(1)}, bf16[192,4096]{1,0:T(8,128)(2,1)}, u32[]{:S(2)}) copy-start(bf16[192,4096]{1,0:T(8,128)(2,1)} %param.12) | copy-start | bytes 4718596
  17.1 44.9 %all-to-all-start = ((bf16[4,2,8192]{2,1,0:T(2,128)(2,1)}), bf16[4,2,8192]{2,1,0:T(2,128)(2,1)S(1)}, u32[]{:S(2)}, u32[]{:S(2)}) async-start(bf16[4,2,8192]{2,1,0:T(2,128)(2,1)} %reshape.72), calls=%async_computation | async-start | bytes 262144 | tf_op jit(solution)/shard_map/all_to_all | solution.py:108
  24.2 35.8 %copy-start.3 = (s32[24]{0:T(128)S(1)}, s32[24]{0:T(128)}, u32[]{:S(2)}) copy-start(s32[24]{0:T(128)} %param.18) | copy-start | bytes 292
  24.2 36.5 %copy-start.4 = (u32[32]{0:T(128)S(1)}, u32[32]{0:T(128)}, u32[]{:S(2)}) copy-start(u32[32]{0:T(128)} %constant.44) | copy-start | bytes 388
where the time goes:
time: 94.2 us; the launch traced here: 93.7 us
  blocking collectives  58.6 us (62%)
  matrix products  14.3 us (15%)
  other arithmetic  8.73 us (9%)
  starting transfers between devices  6.32 us (7%)
  local copies, waits for them, and re-layouts  4.16 us (4%)
  between operations  1.57 us (2%)
    psum x1, blocking collectives, shards(): counts = lax.psum(local_counts, ('dp', 'tgt'))  33.1 us
    unnamed x1, blocking collectives  11.1 us
    all_to_all x1, blocking collectives, shards(): lax.all_to_all(raw_owner.reshape(owner_count, CAP), 'dp', split_axis=0, c...  7.88 us
    all_gather x1, blocking collectives, shards(): row_piece = lax.all_gather(owner_rows, 'tgt', axis=0, tiled=True)  6.51 us
    all_to_all x1, starting transfers between devices, shards(): lax.all_to_all(outgoing.reshape(owner_count, CAP, -1), 'dp', split_axis=0...  6.32 us
    dot_general x1, matrix products, shards(): jnp.einsum('esr,esd->erd', per_example(rank_down, examples), per_example(...  3.33 us
    dot_general x1, matrix products, shards(): jnp.einsum('esd,esr->edr', per_example(wide_hidden, examples), per_exampl...  3.31 us
    dot_general x1, matrix products, contracted_row_sums(): lax.dot_general(row_block, col_block, (((1,), (1,)), ((), ())), preferred...  2.97 us
  transfers between devices with their start and end apart: 1, of which 0 were waited for; matrix products, arithmetic and copies ran while one was open for 5% of the time, Pallas kernels for 0%

commit v1 on v0

v1 whole, which is shorter than its diff:
```python
import functools
import math

import jax
import jax.numpy as jnp
from jax import lax
from jax.experimental import pallas as pl
from jax.experimental.pallas import tpu as pltpu
from jax.sharding import PartitionSpec as P

FEAT = 8192
CAP = 2
TGT = 768
TASKS = 16
SEQ = 8
CORES = 2
LANES = 128
ROW = 1024
PIECES = FEAT // ROW
GROUP = 8
epsilon = 1e-06
bf16, f32, i32 = jnp.bfloat16, jnp.float32, jnp.int32

ANY = pl.BlockSpec(memory_space=pl.ANY)
VMEM = pl.BlockSpec(memory_space=pltpu.VMEM)


def nn(a, b):
    return jnp.dot(a, b, preferred_element_type=f32)


def nt(a, b):
    return lax.dot_general(a, b, (((1,), (1,)), ((), ())), preferred_element_type=f32)


def iota(shape, dim):
    return lax.broadcasted_iota(i32, shape, dim)


def project_kernel(
    strata, keep, present, table, hidden, cotangent, down_t, up, width, rank_t,
    payload, dispatch, member, notes,
    strata_s, keep_s, present_s, table_s, taken, chosen, x, adapters, width_v, rank_v, spread,
    small_sem, row_sem, weight_sem,
):
    examples, strata_total = strata_s.shape[0], table_s.shape[0]
    slots = x.shape[0] // 2
    owners = slots // CAP
    copies = payload.shape[0] // owners
    rank = down_t.shape[0]
    wide = width.shape[1]
    parts = 4
    depth = width.shape[0] // parts

    smalls = [
        pltpu.make_async_copy(a, b, small_sem.at[n])
        for n, (a, b) in enumerate(
            [(strata, strata_s), (keep, keep_s), (present, present_s), (table, table_s)]
        )
    ]
    weights = [
        pltpu.make_async_copy(rank_t, rank_v, weight_sem.at[0]),
        pltpu.make_async_copy(down_t, adapters.at[pl.ds(0, rank)], weight_sem.at[1]),
        pltpu.make_async_copy(up, adapters.at[pl.ds(rank, rank)], weight_sem.at[2]),
    ] + [
        pltpu.make_async_copy(
            width.at[pl.ds(n * depth, depth)], width_v.at[pl.ds(n * depth, depth)], weight_sem.at[3 + n]
        )
        for n in range(parts)
    ]
    for copy in smalls + weights:
        copy.start()

    for n in range(owners):
        taken[n] = 0
    for n in range(slots + 1):
        chosen[n] = 0
    lane = iota((1, LANES), 1)
    for copy in smalls:
        copy.wait()
    counts = jnp.zeros((1, LANES), f32)
    for e in range(examples):
        stratum = strata_s[e]
        live = jnp.where(jnp.logical_and(keep_s[e] == 1, e < present_s[0]), 1, 0)
        owner = table_s[stratum]
        place = taken[owner]
        taken[owner] = place + live
        slot = jnp.where(jnp.logical_and(live == 1, place < CAP), owner * CAP + place, slots)
        chosen[slot] = e
        counts += jnp.where(lane == stratum, live.astype(f32), 0.0)
        member[e : e + 1, :] = (lane == stratum).astype(f32)
        dispatch[e : e + 1, :] = jnp.where(jnp.logical_and(lane == slot, lane < slots), 1.0, 0.0)
    rows = []
    for n in range(slots):
        rows.append(pltpu.make_async_copy(hidden.at[chosen[n]], x.at[n], row_sem.at[n]))
        rows.append(
            pltpu.make_async_copy(cotangent.at[chosen[n]], x.at[slots + n], row_sem.at[slots + n])
        )
    for copy in rows:
        copy.start()

    half = PIECES // 2
    kr = rank_v.shape[0]
    per_row = ROW // wide
    tokens = GROUP * SEQ
    lines = GROUP * half
    spread[...] = (iota((LANES, ROW), 1) // kr == iota((LANES, ROW), 0)).astype(f32).astype(bf16)
    weights[0].wait()
    up_line = iota((per_row * lines, kr), 0)
    pick_up = (per_row * (up_line % half) + up_line // lines == iota((per_row * lines, kr), 1))
    rank_up_rows = nn(pick_up.astype(f32).astype(bf16), rank_v[...]).astype(bf16)
    pick_down = iota((kr * lines, kr), 0) // lines == iota((kr * lines, kr), 1)
    rank_down_rows = nn(pick_down.astype(f32).astype(bf16), rank_v[...]).astype(bf16)
    up_at, up_token = iota((per_row * lines, tokens), 0), iota((per_row * lines, tokens), 1)
    up_mask = (up_at % lines) // half == up_token // SEQ
    down_at, down_token = iota((kr * lines, half * tokens), 0), iota((kr * lines, half * tokens), 1)
    down_mask = jnp.logical_and(
        (down_at % lines) // half == (down_token % tokens) // SEQ, down_at % half == down_token // tokens
    )
    rank_at = iota((lines, ROW), 1) % kr
    for copy in rows + weights[1:3]:
        copy.wait()

    norms = jnp.zeros((1, LANES), f32)
    for g in range(slots // GROUP):
        projected = jnp.zeros((2 * tokens, wide), f32)
        adapted = jnp.zeros((2 * tokens, 2 * rank), f32)
        for n in range(parts):
            span = pl.ds(n * depth, depth)
            both = jnp.concatenate(
                [
                    x[g * GROUP : (g + 1) * GROUP, :, span].reshape(tokens, depth),
                    x[slots + g * GROUP : slots + (g + 1) * GROUP, :, span].reshape(tokens, depth),
                ],
                axis=0,
            )
            adapted += nt(both, adapters[:, span])
            if g == 0:
                weights[3 + n].wait()
            projected += nn(both, width_v[span, :])
        down_act = adapted[:tokens, :rank].astype(bf16)
        up_back = adapted[tokens:, rank:].astype(bf16)
        wide_hidden = projected[:tokens].astype(bf16)
        wide_back = projected[tokens:].astype(bf16)

        left = jnp.where(up_mask, nt(rank_up_rows, down_act), 0.0).astype(bf16)
        up_grad = nn(left, wide_back)
        up_rows = jnp.concatenate(
            [up_grad[n * lines : (n + 1) * lines] for n in range(per_row)], axis=1
        ).astype(bf16)

        left = nt(rank_down_rows, jnp.concatenate([up_back] * half, axis=0))
        left = jnp.where(down_mask, left, 0.0).astype(bf16)
        stacked = jnp.concatenate(
            [wide_hidden[:, n * LANES : (n + 1) * LANES] for n in range(half)], axis=0
        )
        down_grad = nn(left, stacked).astype(bf16)
        repeated = nn(down_grad, spread[...])
        down_rows = repeated[:lines]
        for n in range(1, kr):
            down_rows = jnp.where(rank_at == n, repeated[n * lines : (n + 1) * lines], down_rows)

        up_rows = up_rows.astype(f32)
        squares = jnp.sum(up_rows * up_rows + down_rows * down_rows, axis=1, keepdims=True)
        slot_of = g * GROUP + iota((lines, LANES), 0) // half
        norms += jnp.sum(
            jnp.where(slot_of == iota((lines, LANES), 1), squares, 0.0), axis=0, keepdims=True
        )
        per_owner = CAP * half
        for n in range(GROUP // CAP):
            owner = g * (GROUP // CAP) + n
            piece = jnp.concatenate(
                [
                    up_rows[n * per_owner : (n + 1) * per_owner],
                    down_rows[n * per_owner : (n + 1) * per_owner],
                ],
                axis=0,
            ).astype(bf16)
            for c in range(copies):
                payload[owner * copies + c] = piece
    notes[...] = jnp.concatenate(
        [lax.rsqrt(norms + epsilon), counts, jnp.zeros((6, LANES), f32)], axis=0
    )


def target_kernel(targets, stacked, inverse, sem):
    copies = [
        pltpu.make_async_copy(
            targets.at[0, :, pl.ds(n * ROW, ROW)], stacked.at[n], sem.at[n]
        )
        for n in range(PIECES)
    ]
    for copy in copies:
        copy.start()
    total = jnp.zeros((targets.shape[1], LANES), f32)
    for n in range(PIECES):
        copies[n].wait()
        for m in range(ROW // LANES):
            part = stacked[n, :, m * LANES : (m + 1) * LANES].astype(f32)
            total += part * part
    scale = math.sqrt(FEAT) / (TGT // TASKS)
    inverse[...] = jnp.broadcast_to(
        scale * lax.rsqrt(jnp.sum(total, axis=1, keepdims=True) + epsilon), inverse.shape
    )


def score_kernel(stacked, inverse, mine, other, notes, back):
    per_task = TGT // TASKS
    half = PIECES // 2
    sources = LANES // (CAP * PIECES)
    own_core = lax.axis_index("core")
    first = lax.axis_index("dp") * CAP
    share = stacked.shape[1]
    line = iota((1, CORES * LANES), 1)
    piece_of = (line // (CAP * half)) % 2 * half + line % half
    inv = inverse[...]
    dst = iota((CORES * sources, LANES), 0)
    lane = iota((CORES * sources, LANES), 1)
    for b in range(mine.shape[0] // sources):
        block = jnp.concatenate(
            [
                mine[b * sources : (b + 1) * sources].reshape(LANES, ROW),
                other[b * sources : (b + 1) * sources].reshape(LANES, ROW),
            ],
            axis=0,
        )
        products = nt(stacked[0], block)
        for n in range(1, PIECES):
            products = jnp.where(piece_of == n, nt(stacked[n], block), products)
        best = []
        for c in range(CORES):
            total = products[:, c * LANES : (c + 1) * LANES]
            for shift in (1, 2, CAP * half):
                total = total + pltpu.roll(total, LANES - shift, 1)
            total = jnp.maximum(total, 0.0) * inv
            top = jnp.sum(total[:per_task], axis=0, keepdims=True)
            for n in range(1, share // per_task):
                top = jnp.maximum(
                    top, jnp.sum(total[n * per_task : (n + 1) * per_task], axis=0, keepdims=True)
                )
            best.append(top)
        table = jnp.where(dst % CORES == own_core, best[0], best[1])
        scores = jnp.zeros((CORES * sources, LANES), f32)
        for n in range(CAP):
            at = lane == dst // CORES * (CAP * PIECES) + n * half
            column = jnp.sum(jnp.where(at, table, 0.0), axis=1, keepdims=True)
            scores = jnp.where(lane == first + n, column, scores)
        for n in range(CORES * sources):
            back[b * CORES * sources + n] = jnp.concatenate(
                [scores[n : n + 1], notes[1:2, :]], axis=1
            )


def finish_kernel(strata_total, returned, dispatch, member, notes, out):
    values = returned[:, 0, :]
    raw = jnp.max(values[:, :LANES], axis=0, keepdims=True) * notes[0:1, :]
    counts = jnp.sum(values[:, LANES:], axis=0, keepdims=True)
    live = jnp.sum(counts, axis=1, keepdims=True)
    weight = jnp.sqrt(live / (strata_total * jnp.maximum(counts, 1.0)))
    picked = jnp.sum(dispatch[...] * raw, axis=1, keepdims=True)
    picked = picked * jnp.sum(member[...] * weight, axis=1, keepdims=True)
    examples = dispatch.shape[0]
    square = iota((examples, LANES), 0) == iota((examples, LANES), 1)
    out[...] = jnp.sum(jnp.where(square, picked, 0.0), axis=0)[:examples]


def shards(
    hidden,
    cotangent,
    adapter_down_weight,
    adapter_up_weight,
    width_projection_factor,
    rank_projection_factor,
    targets,
    strata,
    keep,
    shard_example_count,
    stratum_owner_table,
):
    examples = strata.shape[0]
    strata_total = stratum_owner_table.shape[0]
    owners, columns = lax.axis_size("dp"), lax.axis_size("x")
    slots = owners * CAP
    model, wide = width_projection_factor.shape
    rank, kr = rank_projection_factor.shape
    share = targets.shape[1]
    chips = owners * columns

    payload, dispatch, member, notes = pl.pallas_call(
        project_kernel,
        out_shape=(
            jax.ShapeDtypeStruct((chips, CAP * PIECES, ROW), bf16),
            jax.ShapeDtypeStruct((examples, LANES), f32),
            jax.ShapeDtypeStruct((examples, LANES), f32),
            jax.ShapeDtypeStruct((8, LANES), f32),
        ),
        in_specs=[ANY] * 10,
        out_specs=(VMEM,) * 4,
        scratch_shapes=[
            pltpu.SMEM((examples,), i32),
            pltpu.SMEM((examples,), i32),
            pltpu.SMEM((1,), i32),
            pltpu.SMEM((strata_total,), i32),
            pltpu.SMEM((owners,), i32),
            pltpu.SMEM((slots + 1,), i32),
            pltpu.VMEM((2 * slots, SEQ, model), bf16),
            pltpu.VMEM((2 * rank, model), bf16),
            pltpu.VMEM((model, wide), bf16),
            pltpu.VMEM((kr, rank), bf16),
            pltpu.VMEM((LANES, ROW), bf16),
            pltpu.SemaphoreType.DMA((4,)),
            pltpu.SemaphoreType.DMA((2 * slots,)),
            pltpu.SemaphoreType.DMA((7,)),
        ],
        compiler_params=pltpu.CompilerParams(vmem_limit_bytes=40 * 2**20),
        name="project",
    )(
        strata,
        keep,
        shard_example_count,
        stratum_owner_table,
        hidden.reshape(examples, SEQ, model),
        cotangent.reshape(examples, SEQ, model),
        adapter_down_weight.T,
        adapter_up_weight,
        width_projection_factor,
        rank_projection_factor.T,
    )
    stacked, inverse = pl.pallas_call(
        target_kernel,
        out_shape=(
            jax.ShapeDtypeStruct((PIECES, share, ROW), bf16),
            jax.ShapeDtypeStruct((share, LANES), f32),
        ),
        in_specs=[ANY],
        out_specs=(VMEM, VMEM),
        scratch_shapes=[pltpu.SemaphoreType.DMA((PIECES,))],
        compiler_params=pltpu.CompilerParams(vmem_limit_bytes=20 * 2**20),
        cost_estimate=pl.CostEstimate(flops=4 * share * FEAT, bytes_accessed=4 * share * FEAT, transcendentals=0),
        name="target_norms",
    )(targets)
    mine = lax.all_to_all(payload, ("dp", "x"), split_axis=0, concat_axis=0, tiled=True)
    other = lax.ppermute(mine, "core", [(n, (n + 1) % CORES) for n in range(CORES)])
    back = pl.pallas_call(
        score_kernel,
        out_shape=jax.ShapeDtypeStruct((chips * CORES, 1, 2 * LANES), f32),
        in_specs=[VMEM] * 5,
        out_specs=VMEM,
        compiler_params=pltpu.CompilerParams(vmem_limit_bytes=40 * 2**20),
        name="score",
    )(stacked, inverse, mine, other, notes)
    returned = lax.all_to_all(back, ("dp", "x", "core"), split_axis=0, concat_axis=0, tiled=True)
    return pl.pallas_call(
        functools.partial(finish_kernel, strata_total),
        out_shape=jax.ShapeDtypeStruct((examples,), f32),
        in_specs=[VMEM] * 4,
        out_specs=VMEM,
        name="finish",
    )(returned, dispatch, member, notes)


def solution(mesh):
    sizes = [mesh.shape[name] for name in ("groups", "dp", "tgt")]
    fine = jax.sharding.Mesh(
        mesh.devices.reshape(sizes[0], sizes[1], sizes[2] // CORES, CORES),
        ("groups", "dp", "x", "core"),
    )
    every = P(("groups", "dp", "x", "core"))
    whole = P()
    return jax.shard_map(
        shards,
        mesh=fine,
        in_specs=(
            every, every, whole, whole, whole, whole,
            P(("groups", "dp"), ("x", "core"), None),
            every, every, every, whole,
        ),
        out_specs=every,
        check_vma=False,
    )
```

time: 94.2 us -> 46.8 us (0.50)
  blocking collectives: 58.6 us -> 26.1 us
  matrix products: 14.3 us -> 0 us
  Pallas kernels: 0 us -> 9.49 us
  other arithmetic: 8.73 us -> 0 us
  starting transfers between devices: 6.32 us -> 0.01 us
  local copies, waits for them, and re-layouts: 4.16 us -> 9.74 us
    psum x1 -> x0, blocking collectives: 33.1 us -> none  [shards(): counts = lax.psum(local_counts, ('dp', 'tgt'))]
    all_to_all x1 -> x2, blocking collectives: 7.88 us -> 26.1 us  [the longest x1 16 us: shards(): lax.all_to_all(payload, ('dp', 'x'), split_axis=0, concat_axis=0, tiled=T...]
    dot_general x7 -> x0, matrix products: 14.3 us -> none  [the longest x1 3.33 us: shards(): jnp.einsum('esr,esd->erd', per_example(rank_down, examples), per_example(...]
    unnamed x1 -> x0, blocking collectives: 11.1 us -> none
    pallas_call x0 -> x4, Pallas kernels: none -> 9.49 us  [the longest x1 5.01 us: shards(): pl.pallas_call(project_kernel, out_shape=(jax.ShapeDtypeStruct((chips, CA...]
    unnamed x12 -> x26, local copies, waits for them, and re-layouts: 0.68 us -> 9.74 us
    all_gather x1 -> x0, blocking collectives: 6.51 us -> none  [shards(): row_piece = lax.all_gather(owner_rows, 'tgt', axis=0, tiled=True)]
    all_to_all x1 -> x0, starting transfers between devices: 6.32 us -> none  [shards(): lax.all_to_all(outgoing.reshape(owner_count, CAP, -1), 'dp', split_axis=0...]
  transfers between devices with their start and end apart: 1 -> 1, of which waited for: 0 -> 1; matrix products, arithmetic and copies ran while one was open for 5% -> 0% of each run, Pallas kernels for 0% -> 3%
where the time goes in v1:
time: 46.8 us; the launch traced here: 46.3 us
  blocking collectives  26.1 us (56%)
  local copies, waits for them, and re-layouts  9.74 us (21%)
  Pallas kernels  9.49 us (20%)
  between operations  0.74 us (2%)
    all_to_all x1, blocking collectives, shards(): lax.all_to_all(payload, ('dp', 'x'), split_axis=0, concat_axis=0, tiled=T...  16 us
    all_to_all x1, blocking collectives, shards(): lax.all_to_all(back, ('dp', 'x', 'core'), split_axis=0, concat_axis=0, ti...  10.1 us
    unnamed x26, local copies, waits for them, and re-layouts  9.74 us
    pallas_call x1, Pallas kernels, shards(): pl.pallas_call(project_kernel, out_shape=(jax.ShapeDtypeStruct((chips, CA...  5.01 us
    pallas_call x1, Pallas kernels, shards(): pl.pallas_call(score_kernel, out_shape=jax.ShapeDtypeStruct((chips * CORE...  1.82 us
    pallas_call x1, Pallas kernels, shards(): pl.pallas_call(functools.partial(finish_kernel, strata_total), out_shape=...  1.44 us
    pallas_call x1, Pallas kernels, shards(): pl.pallas_call(target_kernel, out_shape=(jax.ShapeDtypeStruct((PIECES, sh...  1.22 us
  transfers between devices with their start and end apart: 1, of which 1 were waited for; matrix products, arithmetic and copies ran while one was open for 0% of the time, Pallas kernels for 3%

profile of v1, /device:TPU:0, one launch (start us, length us, event | category | flops | bytes accessed | tf_op | source)
XLA Modules:
  0.0 46.3 jit_solution(3476237600986213917)
XLA Ops:
  0.7 0.0 copy-start
  0.7 2.2 %copy-done = bf16[4096,512]{1,0:T(8,128)(2,1)S(1)} copy-done((bf16[4096,512]{1,0:T(8,128)(2,1)S(1)}, bf16[4096,512]{1,0:T(8,128)(2,1)}, u32[]{:S(2)}) %copy-start) | copy-done | bytes 4194328
  2.8 0.0 copy-start.2
  2.8 1.4 %copy-done.2 = bf16[192,4096]{1,0:T(8,128)(2,1)S(1)} copy-done((bf16[192,4096]{1,0:T(8,128)(2,1)S(1)}, bf16[192,4096]{1,0:T(8,128)(2,1)}, u32[]{:S(2)}) %copy-start.2) | copy-done | bytes 1572888
  4.2 0.0 copy-start.3
  4.3 1.4 %copy-done.3 = bf16[192,4096]{1,0:T(8,128)(2,1)S(1)} copy-done((bf16[192,4096]{1,0:T(8,128)(2,1)S(1)}, bf16[192,4096]{1,0:T(8,128)(2,1)}, u32[]{:S(2)}) %copy-start.3) | copy-done | bytes 1572888
  5.7 0.0 copy-start.4
  5.7 1.0 %copy-done.4 = bf16[4096,64]{0,1:T(8,128)(2,1)S(1)} copy-done((bf16[4096,64]{0,1:T(8,128)(2,1)S(1)}, bf16[4096,64]{0,1:T(8,128)(2,1)}, u32[]{:S(2)}) %copy-start.4) | copy-done | bytes 524312
  6.7 0.0 copy-start.5
  6.7 1.0 %copy-done.5 = bf16[64,4096]{1,0:T(8,128)(2,1)S(1)} copy-done((bf16[64,4096]{1,0:T(8,128)(2,1)S(1)}, bf16[64,4096]{1,0:T(8,128)(2,1)}, u32[]{:S(2)}) %copy-start.5) | copy-done | bytes 524312
  7.7 0.0 copy-start.9
  7.7 0.7 %copy-done.9 = bf16[64,8]{0,1:T(8,128)(2,1)S(1)} copy-done((bf16[64,8]{0,1:T(8,128)(2,1)S(1)}, bf16[64,8]{0,1:T(8,128)(2,1)}, u32[]{:S(2)}) %copy-start.9) | copy-done | bytes 1048
  8.4 0.0 copy-start.10
  8.4 0.7 %copy-done.10 = s32[24]{0:T(128)S(1)} copy-done((s32[24]{0:T(128)S(1)}, s32[24]{0:T(128)}, u32[]{:S(2)}) %copy-start.10) | copy-done | bytes 120
  9.1 0.0 copy-start.11
  9.1 0.7 %copy-done.11 = s32[24]{0:T(128)S(1)} copy-done((s32[24]{0:T(128)S(1)}, s32[24]{0:T(128)}, u32[]{:S(2)}) %copy-start.11) | copy-done | bytes 120
  9.7 0.0 copy-start.12
  9.7 0.7 %copy-done.12 = s32[32]{0:T(128)S(1)} copy-done((s32[32]{0:T(128)S(1)}, s32[32]{0:T(128)}, u32[]{:S(2)}) %copy-start.12) | copy-done | bytes 152
  10.4 0.0 copy-start.1
  10.4 5.0 %project.1 = (bf16[8,16,1024]{2,1,0:T(8,128)(2,1)S(1)}, f32[24,128]{1,0:T(8,128)S(1)}, f32[24,128]{1,0:T(8,128)S(1)}, f32[8,128]{1,0:T(8,128)S(1)}) custom-call(s32[24]{0:T(128)S(1)} %copy-done.10, s32[24]{0:T(128)S(1)} %copy-done.11, s32[1]{0:T(128)S(6)} %copy.12.present, s32[32]{0:T(128)S(1)} %copy-done.12, bf16[24,8,4096]{2,1,0:T(8,128)(2,1)S(1)} %bitcast.4, ...), custom_call_target="tpu_custom_call" | custom-call | tf_op jit(solution)/shard_map/project/pallas_call | solution.py:289
  15.4 0.0 copy-start.6
  15.4 0.0 copy-start.7
  15.4 0.0 copy-start.8
  15.4 16.0 %all_to_all.10.mine = bf16[8,16,1024]{2,1,0:T(8,128)(2,1)S(1)} all-to-all(bf16[8,16,1024]{2,1,0:T(8,128)(2,1)S(1)} %get-tuple-element.13), channel_id=1, replica_groups=mesh['groups'=2,'dp'=4,'x'=2,'core'=2] {'dp','x'}, dimensions={0} | all-to-all | bytes 524288 | tf_op jit(solution)/shard_map/all_to_all | solution.py:342
  31.4 0.0 collective-permute-start
  31.4 0.0 copy-done.1
  31.4 1.2 %target_norms.1 = (bf16[8,192,1024]{2,1,0:T(8,128)(2,1)S(1)}, f32[192,128]{1,0:T(8,128)S(1)}) custom-call(bf16[1,192,8192]{2,1,0:T(8,128)(2,1)S(1)} %copy-done.1), custom_call_target="tpu_custom_call" | custom-call | flops 6291456 | bytes 6291456 | tf_op jit(solution)/shard_map/target_norms/pallas_call | solution.py:329
  32.6 0.3 collective-permute-done.other
  32.9 1.8 %score.1 = f32[16,1,256]{2,1,0:T(1,128)S(1)} custom-call(bf16[8,192,1024]{2,1,0:T(8,128)(2,1)S(1)} %get-tuple-element.11.stacked, f32[192,128]{1,0:T(8,128)S(1)} %get-tuple-element.12.inverse, bf16[8,16,1024]{2,1,0:T(8,128)(2,1)S(1)} %all_to_all.10.mine, bf16[8,16,1024]{2,1,0:T(8,128)(2,1)S(1)} %collective-permute-done.other, ...), custom_call_target="tpu_custom_call" | custom-call | tf_op jit(solution)/shard_map/score/pallas_call | solution.py:344
  34.8 0.0 copy-done.6
  34.8 0.0 copy-done.7
  34.8 0.0 copy-done.8
  34.8 10.1 %all_to_all.11.returned = f32[16,1,256]{2,1,0:T(1,128)} all-to-all(f32[16,1,256]{2,1,0:T(1,128)S(1)} %score.1), channel_id=1, replica_groups=mesh['groups'=2,'dp'=4,'x'=2,'core'=2] {'dp','x','core'}, dimensions={0} | all-to-all | bytes 32768 | tf_op jit(solution)/shard_map/all_to_all | solution.py:352
  44.9 1.4 %finish.1 = f32[24]{0:T(128)} custom-call(f32[16,1,256]{2,1,0:T(1,128)} %all_to_all.11.returned, f32[24,128]{1,0:T(8,128)} %copy-done.7, f32[24,128]{1,0:T(8,128)} %copy-done.8, f32[8,128]{1,0:T(8,128)} %copy-done.6), custom_call_target="tpu_custom_call" | custom-call | tf_op jit(solution)/shard_map/finish/pallas_call | solution.py:353
Async XLA Ops:
  0.7 2.2 %copy-start = (bf16[4096,512]{1,0:T(8,128)(2,1)S(1)}, bf16[4096,512]{1,0:T(8,128)(2,1)}, u32[]{:S(2)}) copy-start(bf16[4096,512]{1,0:T(8,128)(2,1)} %width.1) | copy-start | bytes 12582916
  2.8 1.4 %copy-start.2 = (bf16[192,4096]{1,0:T(8,128)(2,1)S(1)}, bf16[192,4096]{1,0:T(8,128)(2,1)}, u32[]{:S(2)}) copy-start(bf16[192,4096]{1,0:T(8,128)(2,1)} %param.11) | copy-start | bytes 4718596
  4.2 1.4 %copy-start.3 = (bf16[192,4096]{1,0:T(8,128)(2,1)S(1)}, bf16[192,4096]{1,0:T(8,128)(2,1)}, u32[]{:S(2)}) copy-start(bf16[192,4096]{1,0:T(8,128)(2,1)} %param.12) | copy-start | bytes 4718596
  5.7 1.0 %copy-start.4 = (bf16[4096,64]{0,1:T(8,128)(2,1)S(1)}, bf16[4096,64]{0,1:T(8,128)(2,1)}, u32[]{:S(2)}) copy-start(bf16[4096,64]{0,1:T(8,128)(2,1)} %param.13) | copy-start | bytes 1572868
  6.7 1.0 %copy-start.5 = (bf16[64,4096]{1,0:T(8,128)(2,1)S(1)}, bf16[64,4096]{1,0:T(8,128)(2,1)}, u32[]{:S(2)}) copy-start(bf16[64,4096]{1,0:T(8,128)(2,1)} %up.1) | copy-start | bytes 1572868
  7.7 0.7 %copy-start.9 = (bf16[64,8]{0,1:T(8,128)(2,1)S(1)}, bf16[64,8]{0,1:T(8,128)(2,1)}, u32[]{:S(2)}) copy-start(bf16[64,8]{0,1:T(8,128)(2,1)} %param.16) | copy-start | bytes 3076
  8.4 0.7 %copy-start.10 = (s32[24]{0:T(128)S(1)}, s32[24]{0:T(128)}, u32[]{:S(2)}) copy-start(s32[24]{0:T(128)} %strata.1) | copy-start | bytes 292
  9.1 0.7 %copy-start.11 = (s32[24]{0:T(128)S(1)}, s32[24]{0:T(128)}, u32[]{:S(2)}) copy-start(s32[24]{0:T(128)} %keep.1) | copy-start | bytes 292
  9.7 0.7 %copy-start.12 = (s32[32]{0:T(128)S(1)}, s32[32]{0:T(128)}, u32[]{:S(2)}) copy-start(s32[32]{0:T(128)} %table.1) | copy-start | bytes 388
  10.4 21.0 %copy-start.1 = (bf16[1,192,8192]{2,1,0:T(8,128)(2,1)S(1)}, bf16[1,192,8192]{2,1,0:T(8,128)(2,1)}, u32[]{:S(2)}) copy-start(bf16[1,192,8192]{2,1,0:T(8,128)(2,1)} %targets.1) | copy-start | bytes 9437188
  15.4 19.4 %copy-start.6 = (f32[8,128]{1,0:T(8,128)}, f32[8,128]{1,0:T(8,128)S(1)}, u32[]{:S(2)}) copy-start(f32[8,128]{1,0:T(8,128)S(1)} %get-tuple-element.14.notes) | copy-start | bytes 12292
  15.4 19.4 %copy-start.7 = (f32[24,128]{1,0:T(8,128)}, f32[24,128]{1,0:T(8,128)S(1)}, u32[]{:S(2)}) copy-start(f32[24,128]{1,0:T(8,128)S(1)} %get-tuple-element.15.dispatch) | copy-start | bytes 36868
  15.4 19.4 %copy-start.8 = (f32[24,128]{1,0:T(8,128)}, f32[24,128]{1,0:T(8,128)S(1)}, u32[]{:S(2)}) copy-start(f32[24,128]{1,0:T(8,128)S(1)} %get-tuple-element.16.member) | copy-start | bytes 36868
  31.4 1.5 %collective-permute-start = (bf16[8,16,1024]{2,1,0:T(8,128)(2,1)S(1)}, bf16[8,16,1024]{2,1,0:T(8,128)(2,1)S(1)}, u32[]{:S(2)}, u32[]{:S(2)}) collective-permute-start(bf16[8,16,1024]{2,1,0:T(8,128)(2,1)S(1)} %all_to_all.10.mine), channel_id=1, source_target_pairs={{0,1},{1,0},{2,3},{3,2},{4,5},{5,4},{6,7},{7,6},{8,9},{9,8},{10,11... | collective-permute-start | bytes 786440 | tf_op jit(solution)/shard_map/ppermute | solution.py:343

commit v2 on v1

--- a/solution.py
+++ b/solution.py
@@ -21,7 +21,7 @@
 epsilon = 1e-06
 bf16, f32, i32 = jnp.bfloat16, jnp.float32, jnp.int32
 
-ANY = pl.BlockSpec(memory_space=pl.ANY)
+HBM = pl.BlockSpec(memory_space=pltpu.HBM)
 VMEM = pl.BlockSpec(memory_space=pltpu.VMEM)
 
 
@@ -33,14 +33,18 @@
     return lax.dot_general(a, b, (((1,), (1,)), ((), ())), preferred_element_type=f32)
 
 
+def in_hbm(*arrays):
+    return [pltpu.with_memory_space_constraint(a, pltpu.HBM) for a in arrays]
+
+
 def iota(shape, dim):
     return lax.broadcasted_iota(i32, shape, dim)
 
 
 def project_kernel(
-    strata, keep, present, table, hidden, cotangent, down_t, up, width, rank_t,
+    present, strata, keep, table, hidden, cotangent, down_t, up, width, rank_t,
     payload, dispatch, member, notes,
-    strata_s, keep_s, present_s, table_s, taken, chosen, x, adapters, width_v, rank_v, spread,
+    strata_s, keep_s, table_s, taken, chosen, x, adapters, width_v, rank_v, spread,
     small_sem, row_sem, weight_sem,
 ):
     examples, strata_total = strata_s.shape[0], table_s.shape[0]
@@ -55,7 +59,7 @@
     smalls = [
         pltpu.make_async_copy(a, b, small_sem.at[n])
         for n, (a, b) in enumerate(
-            [(strata, strata_s), (keep, keep_s), (present, present_s), (table, table_s)]
+            [(strata, strata_s), (keep, keep_s), (table, table_s)]
         )
     ]
     weights = [
@@ -81,7 +85,7 @@
     counts = jnp.zeros((1, LANES), f32)
     for e in range(examples):
         stratum = strata_s[e]
-        live = jnp.where(jnp.logical_and(keep_s[e] == 1, e < present_s[0]), 1, 0)
+        live = jnp.where(jnp.logical_and(keep_s[e] == 1, e < present[0]), 1, 0)
         owner = table_s[stratum]
         place = taken[owner]
         taken[owner] = place + live
@@ -294,12 +298,11 @@
             jax.ShapeDtypeStruct((examples, LANES), f32),
             jax.ShapeDtypeStruct((8, LANES), f32),
         ),
-        in_specs=[ANY] * 10,
+        in_specs=[pl.BlockSpec(memory_space=pltpu.SMEM)] + [HBM] * 9,
         out_specs=(VMEM,) * 4,
         scratch_shapes=[
             pltpu.SMEM((examples,), i32),
             pltpu.SMEM((examples,), i32),
-            pltpu.SMEM((1,), i32),
             pltpu.SMEM((strata_total,), i32),
             pltpu.SMEM((owners,), i32),
             pltpu.SMEM((slots + 1,), i32),
@@ -308,23 +311,25 @@
             pltpu.VMEM((model, wide), bf16),
             pltpu.VMEM((kr, rank), bf16),
             pltpu.VMEM((LANES, ROW), bf16),
-            pltpu.SemaphoreType.DMA((4,)),
+            pltpu.SemaphoreType.DMA((3,)),
             pltpu.SemaphoreType.DMA((2 * slots,)),
             pltpu.SemaphoreType.DMA((7,)),
         ],
         compiler_params=pltpu.CompilerParams(vmem_limit_bytes=40 * 2**20),
         name="project",
     )(
-        strata,
-        keep,
         shard_example_count,
-        stratum_owner_table,
-        hidden.reshape(examples, SEQ, model),
-        cotangent.reshape(examples, SEQ, model),
-        adapter_down_weight.T,
-        adapter_up_weight,
-        width_projection_factor,
-        rank_projection_factor.T,
+        *in_hbm(
+            strata,
+            keep,
+            stratum_owner_table,
+            hidden.reshape(examples, SEQ, model),
+            cotangent.reshape(examples, SEQ, model),
+            adapter_down_weight.T,
+            adapter_up_weight,
+            width_projection_factor,
+            rank_projection_factor.T,
+        )
     )
     stacked, inverse = pl.pallas_call(
         target_kernel,
@@ -332,13 +337,13 @@
             jax.ShapeDtypeStruct((PIECES, share, ROW), bf16),
             jax.ShapeDtypeStruct((share, LANES), f32),
         ),
-        in_specs=[ANY],
+        in_specs=[HBM],
         out_specs=(VMEM, VMEM),
         scratch_shapes=[pltpu.SemaphoreType.DMA((PIECES,))],
         compiler_params=pltpu.CompilerParams(vmem_limit_bytes=20 * 2**20),
         cost_estimate=pl.CostEstimate(flops=4 * share * FEAT, bytes_accessed=4 * share * FEAT, transcendentals=0),
         name="target_norms",
-    )(targets)
+    )(*in_hbm(targets))
     mine = lax.all_to_all(payload, ("dp", "x"), split_axis=0, concat_axis=0, tiled=True)
     other = lax.ppermute(mine, "core", [(n, (n + 1) % CORES) for n in range(CORES)])
     back = pl.pallas_call(

time: 46.8 us -> 38.1 us (0.81)
  local copies, waits for them, and re-layouts: 9.74 us -> 0.01 us
  Pallas kernels: 9.49 us -> 10.9 us
    unnamed x26 -> x6, local copies, waits for them, and re-layouts: 9.74 us -> 0.01 us
    pallas_call x1, Pallas kernels: 1.22 us -> 2.07 us  [shards(): pl.pallas_call(target_kernel, out_shape=(jax.ShapeDtypeStruct((PIECES, sh...]
    pallas_call x1, Pallas kernels: 5.01 us -> 5.6 us  [shards(): pl.pallas_call(project_kernel, out_shape=(jax.ShapeDtypeStruct((chips, CA...]
  transfers between devices with their start and end apart: 1 -> 1, of which waited for: 1 -> 0; matrix products, arithmetic and copies ran while one was open for 0% -> 0% of each run, Pallas kernels for 3% -> 5%
where the time goes in v2:
time: 38.1 us; the launch traced here: 37.8 us
  blocking collectives  26.2 us (69%)
  Pallas kernels  10.9 us (29%)
  between operations  0.72 us (2%)
    all_to_all x1, blocking collectives, shards(): lax.all_to_all(payload, ('dp', 'x'), split_axis=0, concat_axis=0, tiled=T...  16 us
    all_to_all x1, blocking collectives, shards(): lax.all_to_all(back, ('dp', 'x', 'core'), split_axis=0, concat_axis=0, ti...  10.2 us
    pallas_call x1, Pallas kernels, shards(): pl.pallas_call(project_kernel, out_shape=(jax.ShapeDtypeStruct((chips, CA...  5.6 us
    pallas_call x1, Pallas kernels, shards(): pl.pallas_call(target_kernel, out_shape=(jax.ShapeDtypeStruct((PIECES, sh...  2.07 us
    pallas_call x1, Pallas kernels, shards(): pl.pallas_call(score_kernel, out_shape=jax.ShapeDtypeStruct((chips * CORE...  1.82 us
    pallas_call x1, Pallas kernels, shards(): pl.pallas_call(functools.partial(finish_kernel, strata_total), out_shape=...  1.44 us
  transfers between devices with their start and end apart: 1, of which 0 were waited for; matrix products, arithmetic and copies ran while one was open for 0% of the time, Pallas kernels for 5%

profile of v2, /device:TPU:0, one launch (start us, length us, event | category | flops | bytes accessed | tf_op | source)
XLA Modules:
  0.0 37.8 jit_solution(12380957175488596247)
XLA Ops:
  0.7 5.6 %project.1 = (bf16[8,16,1024]{2,1,0:T(8,128)(2,1)S(1)}, f32[24,128]{1,0:T(8,128)S(1)}, f32[24,128]{1,0:T(8,128)S(1)}, f32[8,128]{1,0:T(8,128)S(1)}) custom-call(s32[1]{0:T(128)S(6)} %copy.12.present, s32[24]{0:T(128)} %strata.1, s32[24]{0:T(128)} %keep.1, s32[32]{0:T(128)} %table.1, bf16[24,8,4096]{2,1,0:T(8,128)(2,1)} %bitcast.4, ...), custom_call_target="tpu_custom_call" | custom-call | tf_op jit(solution)/shard_map/project/pallas_call | solution.py:293
  6.3 0.0 copy-start.1
  6.3 0.0 copy-start.2
  6.3 0.0 copy-start
  6.3 16.0 %all_to_all.10.mine = bf16[8,16,1024]{2,1,0:T(8,128)(2,1)S(1)} all-to-all(bf16[8,16,1024]{2,1,0:T(8,128)(2,1)S(1)} %get-tuple-element.13), channel_id=1, replica_groups=mesh['groups'=2,'dp'=4,'x'=2,'core'=2] {'dp','x'}, dimensions={0} | all-to-all | bytes 524288 | tf_op jit(solution)/shard_map/all_to_all | solution.py:347
  22.3 0.0 copy-done.1
  22.3 0.0 copy-done.2
  22.3 0.0 collective-permute-start
  22.3 2.1 %target_norms.1 = (bf16[8,192,1024]{2,1,0:T(8,128)(2,1)S(1)}, f32[192,128]{1,0:T(8,128)S(1)}) custom-call(bf16[1,192,8192]{2,1,0:T(8,128)(2,1)} %targets.1), custom_call_target="tpu_custom_call" | custom-call | flops 6291456 | bytes 6291456 | tf_op jit(solution)/shard_map/target_norms/pallas_call | solution.py:334
  24.3 0.0 collective-permute-done.other
  24.4 1.8 %score.1 = f32[16,1,256]{2,1,0:T(1,128)S(1)} custom-call(bf16[8,192,1024]{2,1,0:T(8,128)(2,1)S(1)} %get-tuple-element.11.stacked, f32[192,128]{1,0:T(8,128)S(1)} %get-tuple-element.12.inverse, bf16[8,16,1024]{2,1,0:T(8,128)(2,1)S(1)} %all_to_all.10.mine, bf16[8,16,1024]{2,1,0:T(8,128)(2,1)S(1)} %collective-permute-done.other, ...), custom_call_target="tpu_custom_call" | custom-call | tf_op jit(solution)/shard_map/score/pallas_call | solution.py:349
  26.2 0.0 copy-done
  26.2 10.2 %all_to_all.11.returned = f32[16,1,256]{2,1,0:T(1,128)} all-to-all(f32[16,1,256]{2,1,0:T(1,128)S(1)} %score.1), channel_id=1, replica_groups=mesh['groups'=2,'dp'=4,'x'=2,'core'=2] {'dp','x','core'}, dimensions={0} | all-to-all | bytes 32768 | tf_op jit(solution)/shard_map/all_to_all | solution.py:357
  36.4 1.4 %finish.1 = f32[24]{0:T(128)} custom-call(f32[16,1,256]{2,1,0:T(1,128)} %all_to_all.11.returned, f32[24,128]{1,0:T(8,128)} %copy-done.1, f32[24,128]{1,0:T(8,128)} %copy-done.2, f32[8,128]{1,0:T(8,128)} %copy-done), custom_call_target="tpu_custom_call" | custom-call | tf_op jit(solution)/shard_map/finish/pallas_call | solution.py:358
Async XLA Ops:
  6.3 16.0 %copy-start.1 = (f32[24,128]{1,0:T(8,128)}, f32[24,128]{1,0:T(8,128)S(1)}, u32[]{:S(2)}) copy-start(f32[24,128]{1,0:T(8,128)S(1)} %get-tuple-element.15.dispatch) | copy-start | bytes 36868
  6.3 16.0 %copy-start.2 = (f32[24,128]{1,0:T(8,128)}, f32[24,128]{1,0:T(8,128)S(1)}, u32[]{:S(2)}) copy-start(f32[24,128]{1,0:T(8,128)S(1)} %get-tuple-element.16.member) | copy-start | bytes 36868
  6.3 19.9 %copy-start = (f32[8,128]{1,0:T(8,128)}, f32[8,128]{1,0:T(8,128)S(1)}, u32[]{:S(2)}) copy-start(f32[8,128]{1,0:T(8,128)S(1)} %get-tuple-element.14.notes) | copy-start | bytes 12292
  22.3 2.1 %collective-permute-start = (bf16[8,16,1024]{2,1,0:T(8,128)(2,1)S(1)}, bf16[8,16,1024]{2,1,0:T(8,128)(2,1)S(1)}, u32[]{:S(2)}, u32[]{:S(2)}) collective-permute-start(bf16[8,16,1024]{2,1,0:T(8,128)(2,1)S(1)} %all_to_all.10.mine), channel_id=1, source_target_pairs={{0,1},{1,0},{2,3},{3,2},{4,5},{5,4},{6,7},{7,6},{8,9},{9,8},{10,11... | collective-permute-start | bytes 786440 | tf_op jit(solution)/shard_map/ppermute | solution.py:348

commit v3 on v2

--- a/solution.py
+++ b/solution.py
@@ -44,7 +44,7 @@
 def project_kernel(
     present, strata, keep, table, hidden, cotangent, down_t, up, width, rank_t,
     payload, dispatch, member, notes,
-    strata_s, keep_s, table_s, taken, chosen, x, adapters, width_v, rank_v, spread,
+    strata_s, keep_s, table_s, taken, chosen, x, adapters, adapters_t, width_v, rank_v, spread,
     small_sem, row_sem, weight_sem,
 ):
     examples, strata_total = strata_s.shape[0], table_s.shape[0]
@@ -53,7 +53,8 @@
     copies = payload.shape[0] // owners
     rank = down_t.shape[0]
     wide = width.shape[1]
-    parts = 4
+    parts = 2
+    early = 1
     depth = width.shape[0] // parts
 
     smalls = [
@@ -72,17 +73,17 @@
         )
         for n in range(parts)
     ]
-    for copy in smalls + weights:
+    for copy in smalls + weights[: 3 + early]:
         copy.start()
 
     for n in range(owners):
         taken[n] = 0
     for n in range(slots + 1):
         chosen[n] = 0
-    lane = iota((1, LANES), 1)
+    lane = iota((1, notes.shape[1]), 1)
     for copy in smalls:
         copy.wait()
-    counts = jnp.zeros((1, LANES), f32)
+    counts = jnp.zeros(lane.shape, f32)
     for e in range(examples):
         stratum = strata_s[e]
         live = jnp.where(jnp.logical_and(keep_s[e] == 1, e < present[0]), 1, 0)
@@ -91,8 +92,8 @@
         taken[owner] = place + live
         slot = jnp.where(jnp.logical_and(live == 1, place < CAP), owner * CAP + place, slots)
         chosen[slot] = e
-        counts += jnp.where(lane == stratum, live.astype(f32), 0.0)
-        member[e : e + 1, :] = (lane == stratum).astype(f32)
+        counts += jnp.where(lane == slots + stratum, live.astype(f32), 0.0)
+        member[e : e + 1, :] = (lane == slots + stratum).astype(f32)
         dispatch[e : e + 1, :] = jnp.where(jnp.logical_and(lane == slot, lane < slots), 1.0, 0.0)
     rows = []
     for n in range(slots):
@@ -100,7 +101,7 @@
         rows.append(
             pltpu.make_async_copy(cotangent.at[chosen[n]], x.at[slots + n], row_sem.at[slots + n])
         )
-    for copy in rows:
+    for copy in rows + weights[3 + early :]:
         copy.start()
 
     half = PIECES // 2
@@ -122,26 +123,31 @@
         (down_at % lines) // half == (down_token % tokens) // SEQ, down_at % half == down_token // tokens
     )
     rank_at = iota((lines, ROW), 1) % kr
-    for copy in rows + weights[1:3]:
+    for copy in weights[1:3]:
         copy.wait()
-
-    norms = jnp.zeros((1, LANES), f32)
+    adapters_t[...] = adapters[...].T
+    for copy in rows:
+        copy.wait()
+
+    norms = jnp.zeros(lane.shape, f32)
     for g in range(slots // GROUP):
-        projected = jnp.zeros((2 * tokens, wide), f32)
-        adapted = jnp.zeros((2 * tokens, 2 * rank), f32)
-        for n in range(parts):
-            span = pl.ds(n * depth, depth)
-            both = jnp.concatenate(
+        model = x.shape[2]
+        def both(lo, size):
+            return jnp.concatenate(
                 [
-                    x[g * GROUP : (g + 1) * GROUP, :, span].reshape(tokens, depth),
-                    x[slots + g * GROUP : slots + (g + 1) * GROUP, :, span].reshape(tokens, depth),
+                    x[g * GROUP : (g + 1) * GROUP, :, lo : lo + size].reshape(tokens, size),
+                    x[slots + g * GROUP : slots + (g + 1) * GROUP, :, lo : lo + size].reshape(tokens, size),
                 ],
                 axis=0,
             )
-            adapted += nt(both, adapters[:, span])
+
+        adapted = nn(both(0, model), adapters_t[...])
+        for n in range(parts):
             if g == 0:
                 weights[3 + n].wait()
-            projected += nn(both, width_v[span, :])
+            span = pl.ds(n * depth, depth)
+            part = nn(both(n * depth, depth), width_v[span, :])
+            projected = part if n == 0 else projected + part
         down_act = adapted[:tokens, :rank].astype(bf16)
         up_back = adapted[tokens:, rank:].astype(bf16)
         wide_hidden = projected[:tokens].astype(bf16)
@@ -166,10 +172,9 @@
 
         up_rows = up_rows.astype(f32)
         squares = jnp.sum(up_rows * up_rows + down_rows * down_rows, axis=1, keepdims=True)
-        slot_of = g * GROUP + iota((lines, LANES), 0) // half
-        norms += jnp.sum(
-            jnp.where(slot_of == iota((lines, LANES), 1), squares, 0.0), axis=0, keepdims=True
-        )
+        at = (lines, notes.shape[1])
+        slot_of = g * GROUP + iota(at, 0) // half
+        norms += jnp.sum(jnp.where(slot_of == iota(at, 1), squares, 0.0), axis=0, keepdims=True)
         per_owner = CAP * half
         for n in range(GROUP // CAP):
             owner = g * (GROUP // CAP) + n
@@ -181,9 +186,9 @@
                 axis=0,
             ).astype(bf16)
             for c in range(copies):
-                payload[owner * copies + c] = piece
+                payload[c * owners + owner] = piece
     notes[...] = jnp.concatenate(
-        [lax.rsqrt(norms + epsilon), counts, jnp.zeros((6, LANES), f32)], axis=0
+        [lax.rsqrt(norms + epsilon), counts, jnp.zeros((6, notes.shape[1]), f32)], axis=0
     )
 
 
@@ -228,9 +233,10 @@
             ],
             axis=0,
         )
-        products = nt(stacked[0], block)
+        whole = nt(stacked[...].reshape(PIECES * share, ROW), block)
+        products = whole[:share]
         for n in range(1, PIECES):
-            products = jnp.where(piece_of == n, nt(stacked[n], block), products)
+            products = jnp.where(piece_of == n, whole[n * share : (n + 1) * share], products)
         best = []
         for c in range(CORES):
             total = products[:, c * LANES : (c + 1) * LANES]
@@ -244,25 +250,25 @@
                 )
             best.append(top)
         table = jnp.where(dst % CORES == own_core, best[0], best[1])
-        scores = jnp.zeros((CORES * sources, LANES), f32)
+        scores = jnp.broadcast_to(notes[1:2, :], (CORES * sources, notes.shape[1]))
         for n in range(CAP):
             at = lane == dst // CORES * (CAP * PIECES) + n * half
             column = jnp.sum(jnp.where(at, table, 0.0), axis=1, keepdims=True)
-            scores = jnp.where(lane == first + n, column, scores)
+            scores = jnp.where(iota(scores.shape, 1) == first + n, column, scores)
         for n in range(CORES * sources):
-            back[b * CORES * sources + n] = jnp.concatenate(
-                [scores[n : n + 1], notes[1:2, :]], axis=1
-            )
-
-
-def finish_kernel(strata_total, returned, dispatch, member, notes, out):
+            back[b * CORES * sources + n] = scores[n : n + 1]
+
+
+def finish_kernel(slots, strata_total, returned, dispatch, member, notes, out):
     values = returned[:, 0, :]
-    raw = jnp.max(values[:, :LANES], axis=0, keepdims=True) * notes[0:1, :]
-    counts = jnp.sum(values[:, LANES:], axis=0, keepdims=True)
-    live = jnp.sum(counts, axis=1, keepdims=True)
-    weight = jnp.sqrt(live / (strata_total * jnp.maximum(counts, 1.0)))
+    raw = jnp.max(values, axis=0, keepdims=True) * notes[0:1, :]
+    counts = jnp.sum(values, axis=0, keepdims=True)
+    held = iota(counts.shape, 1)
+    held = jnp.logical_and(held >= slots, held < slots + strata_total)
+    live = jnp.sum(jnp.where(held, counts, 0.0), axis=1, keepdims=True)
+    weight = lax.rsqrt(strata_total * jnp.maximum(counts, 1.0))
     picked = jnp.sum(dispatch[...] * raw, axis=1, keepdims=True)
-    picked = picked * jnp.sum(member[...] * weight, axis=1, keepdims=True)
+    picked = picked * jnp.sum(member[...] * weight, axis=1, keepdims=True) * jnp.sqrt(live)
     examples = dispatch.shape[0]
     square = iota((examples, LANES), 0) == iota((examples, LANES), 1)
     out[...] = jnp.sum(jnp.where(square, picked, 0.0), axis=0)[:examples]
@@ -289,14 +295,15 @@
     rank, kr = rank_projection_factor.shape
     share = targets.shape[1]
     chips = owners * columns
+    lanes = -(-(slots + strata_total) // LANES) * LANES
 
     payload, dispatch, member, notes = pl.pallas_call(
         project_kernel,
         out_shape=(
             jax.ShapeDtypeStruct((chips, CAP * PIECES, ROW), bf16),
-            jax.ShapeDtypeStruct((examples, LANES), f32),
-            jax.ShapeDtypeStruct((examples, LANES), f32),
-            jax.ShapeDtypeStruct((8, LANES), f32),
+            jax.ShapeDtypeStruct((examples, lanes), f32),
+            jax.ShapeDtypeStruct((examples, lanes), f32),
+            jax.ShapeDtypeStruct((8, lanes), f32),
         ),
         in_specs=[pl.BlockSpec(memory_space=pltpu.SMEM)] + [HBM] * 9,
         out_specs=(VMEM,) * 4,
@@ -308,6 +315,7 @@
             pltpu.SMEM((slots + 1,), i32),
             pltpu.VMEM((2 * slots, SEQ, model), bf16),
             pltpu.VMEM((2 * rank, model), bf16),
+            pltpu.VMEM((model, 2 * rank), bf16),
             pltpu.VMEM((model, wide), bf16),
             pltpu.VMEM((kr, rank), bf16),
             pltpu.VMEM((LANES, ROW), bf16),
@@ -331,35 +339,37 @@
             rank_projection_factor.T,
         )
     )
+    payload, targets = lax.optimization_barrier((payload, targets))
     stacked, inverse = pl.pallas_call(
         target_kernel,
         out_shape=(
             jax.ShapeDtypeStruct((PIECES, share, ROW), bf16),
             jax.ShapeDtypeStruct((share, LANES), f32),
         ),
-        in_specs=[HBM],
+        in_specs=[pl.BlockSpec(memory_space=pl.ANY)],
         out_specs=(VMEM, VMEM),
         scratch_shapes=[pltpu.SemaphoreType.DMA((PIECES,))],
         compiler_params=pltpu.CompilerParams(vmem_limit_bytes=20 * 2**20),
         cost_estimate=pl.CostEstimate(flops=4 * share * FEAT, bytes_accessed=4 * share * FEAT, transcendentals=0),
         name="target_norms",
-    )(*in_hbm(targets))
-    mine = lax.all_to_all(payload, ("dp", "x"), split_axis=0, concat_axis=0, tiled=True)
+    )(targets)
+    mine = lax.all_to_all(payload, ("x", "dp"), split_axis=0, concat_axis=0, tiled=True)
     other = lax.ppermute(mine, "core", [(n, (n + 1) % CORES) for n in range(CORES)])
     back = pl.pallas_call(
         score_kernel,
-        out_shape=jax.ShapeDtypeStruct((chips * CORES, 1, 2 * LANES), f32),
+        out_shape=jax.ShapeDtypeStruct((chips * CORES, 1, lanes), f32),
         in_specs=[VMEM] * 5,
         out_specs=VMEM,
         compiler_params=pltpu.CompilerParams(vmem_limit_bytes=40 * 2**20),
         name="score",
     )(stacked, inverse, mine, other, notes)
-    returned = lax.all_to_all(back, ("dp", "x", "core"), split_axis=0, concat_axis=0, tiled=True)
+    returned = lax.all_to_all(back, ("x", "dp", "core"), split_axis=0, concat_axis=0, tiled=True)
     return pl.pallas_call(
-        functools.partial(finish_kernel, strata_total),
+        functools.partial(finish_kernel, slots, strata_total),
         out_shape=jax.ShapeDtypeStruct((examples,), f32),
         in_specs=[VMEM] * 4,
         out_specs=VMEM,
+        compiler_params=pltpu.CompilerParams(vmem_limit_bytes=4 * 2**20),
         name="finish",
     )(returned, dispatch, member, notes)
 

time: 38.1 us -> 35 us (0.919)
  Pallas kernels: 10.9 us -> 8.08 us
  blocking collectives: 26.2 us -> 25.8 us
    pallas_call x1, Pallas kernels: 1.44 us -> 0.63 us  [shards(): pl.pallas_call(functools.partial(finish_kernel, slots, strata_total), out...]
    pallas_call x1, Pallas kernels: 2.07 us -> 1.28 us  [shards(): pl.pallas_call(target_kernel, out_shape=(jax.ShapeDtypeStruct((PIECES, sh...]
    pallas_call x1, Pallas kernels: 5.6 us -> 4.84 us  [shards(): pl.pallas_call(project_kernel, out_shape=(jax.ShapeDtypeStruct((chips, CA...]
    pallas_call x1, Pallas kernels: 1.82 us -> 1.34 us  [shards(): pl.pallas_call(score_kernel, out_shape=jax.ShapeDtypeStruct((chips * CORE...]
  transfers between devices with their start and end apart: 1 -> 1, of which waited for: 0 -> 1; matrix products, arithmetic and copies ran while one was open for 0% -> 0% of each run, Pallas kernels for 5% -> 4%
where the time goes in v3:
time: 35 us; the launch traced here: 34.8 us
  blocking collectives  25.8 us (74%)
  Pallas kernels  8.08 us (23%)
  between operations  0.68 us (2%)
    all_to_all x1, blocking collectives, shards(): lax.all_to_all(payload, ('x', 'dp'), split_axis=0, concat_axis=0, tiled=T...  16.8 us
    all_to_all x1, blocking collectives, shards(): lax.all_to_all(back, ('x', 'dp', 'core'), split_axis=0, concat_axis=0, ti...  8.97 us
    pallas_call x1, Pallas kernels, shards(): pl.pallas_call(project_kernel, out_shape=(jax.ShapeDtypeStruct((chips, CA...  4.84 us
    pallas_call x1, Pallas kernels, shards(): pl.pallas_call(score_kernel, out_shape=jax.ShapeDtypeStruct((chips * CORE...  1.34 us
    pallas_call x1, Pallas kernels, shards(): pl.pallas_call(target_kernel, out_shape=(jax.ShapeDtypeStruct((PIECES, sh...  1.28 us
  transfers between devices with their start and end apart: 1, of which 1 were waited for; matrix products, arithmetic and copies ran while one was open for 0% of the time, Pallas kernels for 4%

profile of v3, /device:TPU:0, one launch (start us, length us, event | category | flops | bytes accessed | tf_op | source)
XLA Modules:
  0.0 34.8 jit_solution(13973247979509512850)
XLA Ops:
  0.7 0.0 copy-start
  0.7 4.8 %project.1 = (bf16[8,16,1024]{2,1,0:T(8,128)(2,1)S(1)}, f32[24,128]{1,0:T(8,128)S(1)}, f32[24,128]{1,0:T(8,128)S(1)}, f32[8,128]{1,0:T(8,128)S(1)}) custom-call(s32[1]{0:T(128)S(6)} %copy.12.present, s32[24]{0:T(128)} %strata.1, s32[24]{0:T(128)} %keep.1, s32[32]{0:T(128)} %table.1, bf16[24,8,4096]{2,1,0:T(8,128)(2,1)} %bitcast.4, ...), custom_call_target="tpu_custom_call" | custom-call | tf_op jit(solution)/shard_map/project/pallas_call | solution.py:300
  5.5 16.8 %all_to_all.10.mine = bf16[8,16,1024]{2,1,0:T(8,128)(2,1)S(1)} all-to-all(bf16[8,16,1024]{2,1,0:T(8,128)(2,1)S(1)} %get-tuple-element.17), channel_id=1, replica_groups=mesh['groups'=2,'dp'=4,'x'=2,'core'=2] {'x','dp'}, dimensions={0} | all-to-all | bytes 524288 | tf_op jit(solution)/shard_map/all_to_all | solution.py:356
  22.3 0.0 collective-permute-start
  22.3 0.0 copy-done
  22.3 1.3 %target_norms.1 = (bf16[8,192,1024]{2,1,0:T(8,128)(2,1)S(1)}, f32[192,128]{1,0:T(8,128)S(1)}) custom-call(bf16[1,192,8192]{2,1,0:T(8,128)(2,1)S(1)} %copy-done), custom_call_target="tpu_custom_call" | custom-call | flops 6291456 | bytes 6291456 | tf_op jit(solution)/shard_map/target_norms/pallas_call | solution.py:343
  23.6 0.2 collective-permute-done.other
  23.9 1.3 %score.1 = f32[16,1,128]{2,1,0:T(1,128)S(1)} custom-call(bf16[8,192,1024]{2,1,0:T(8,128)(2,1)S(1)} %get-tuple-element.15.stacked, f32[192,128]{1,0:T(8,128)S(1)} %get-tuple-element.16.inverse, bf16[8,16,1024]{2,1,0:T(8,128)(2,1)S(1)} %all_to_all.10.mine, bf16[8,16,1024]{2,1,0:T(8,128)(2,1)S(1)} %collective-permute-done.other, ...), custom_call_target="tpu_custom_call" | custom-call | tf_op jit(solution)/shard_map/score/pallas_call | solution.py:358
  25.2 9.0 %all_to_all.11.returned = f32[16,1,128]{2,1,0:T(1,128)S(1)} all-to-all(f32[16,1,128]{2,1,0:T(1,128)S(1)} %score.1), channel_id=1, replica_groups=mesh['groups'=2,'dp'=4,'x'=2,'core'=2] {'x','dp','core'}, dimensions={0} | all-to-all | bytes 16384 | tf_op jit(solution)/shard_map/all_to_all | solution.py:366
  34.2 0.6 %finish.1 = f32[24]{0:T(128)} custom-call(f32[16,1,128]{2,1,0:T(1,128)S(1)} %all_to_all.11.returned, f32[24,128]{1,0:T(8,128)S(1)} %get-tuple-element.19.dispatch, f32[24,128]{1,0:T(8,128)S(1)} %get-tuple-element.20.member, f32[8,128]{1,0:T(8,128)S(1)} %get-tuple-element.18.notes), custom_call_target="tpu_custom_call" | custom-call | tf_op jit(solution)/shard_map/finish/pallas_call | solution.py:367
Async XLA Ops:
  0.7 21.7 %copy-start = (bf16[1,192,8192]{2,1,0:T(8,128)(2,1)S(1)}, bf16[1,192,8192]{2,1,0:T(8,128)(2,1)}, u32[]{:S(2)}) copy-start(bf16[1,192,8192]{2,1,0:T(8,128)(2,1)} %targets) | copy-start | bytes 9437188
  22.3 1.5 %collective-permute-start = (bf16[8,16,1024]{2,1,0:T(8,128)(2,1)S(1)}, bf16[8,16,1024]{2,1,0:T(8,128)(2,1)S(1)}, u32[]{:S(2)}, u32[]{:S(2)}) collective-permute-start(bf16[8,16,1024]{2,1,0:T(8,128)(2,1)S(1)} %all_to_all.10.mine), channel_id=1, source_target_pairs={{0,1},{1,0},{2,3},{3,2},{4,5},{5,4},{6,7},{7,6},{8,9},{9,8},{10,11... | collective-permute-start | bytes 786440 | tf_op jit(solution)/shard_map/ppermute | solution.py:357

commit v4 on v3

--- a/solution.py
+++ b/solution.py
@@ -42,7 +42,7 @@
 
 
 def project_kernel(
-    present, strata, keep, table, hidden, cotangent, down_t, up, width, rank_t,
+    place_of, present, strata, keep, table, hidden, cotangent, down_t, up, width, rank_t,
     payload, dispatch, member, notes,
     strata_s, keep_s, table_s, taken, chosen, x, adapters, adapters_t, width_v, rank_v, spread,
     small_sem, row_sem, weight_sem,
@@ -50,7 +50,6 @@
     examples, strata_total = strata_s.shape[0], table_s.shape[0]
     slots = x.shape[0] // 2
     owners = slots // CAP
-    copies = payload.shape[0] // owners
     rank = down_t.shape[0]
     wide = width.shape[1]
     parts = 2
@@ -95,6 +94,7 @@
         counts += jnp.where(lane == slots + stratum, live.astype(f32), 0.0)
         member[e : e + 1, :] = (lane == slots + stratum).astype(f32)
         dispatch[e : e + 1, :] = jnp.where(jnp.logical_and(lane == slot, lane < slots), 1.0, 0.0)
+    notes[...] = jnp.broadcast_to(counts, notes.shape)
     rows = []
     for n in range(slots):
         rows.append(pltpu.make_async_copy(hidden.at[chosen[n]], x.at[n], row_sem.at[n]))
@@ -129,7 +129,6 @@
     for copy in rows:
         copy.wait()
 
-    norms = jnp.zeros(lane.shape, f32)
     for g in range(slots // GROUP):
         model = x.shape[2]
         def both(lo, size):
@@ -142,39 +141,32 @@
             )
 
         adapted = nn(both(0, model), adapters_t[...])
+        down_act = adapted[:tokens, :rank].astype(bf16)
+        up_back = adapted[tokens:, rank:].astype(bf16)
+        left_up = jnp.where(up_mask, nt(rank_up_rows, down_act), 0.0).astype(bf16)
+        left_down = nt(rank_down_rows, jnp.concatenate([up_back] * half, axis=0))
+        left_down = jnp.where(down_mask, left_down, 0.0).astype(bf16)
         for n in range(parts):
             if g == 0:
                 weights[3 + n].wait()
             span = pl.ds(n * depth, depth)
             part = nn(both(n * depth, depth), width_v[span, :])
             projected = part if n == 0 else projected + part
-        down_act = adapted[:tokens, :rank].astype(bf16)
-        up_back = adapted[tokens:, rank:].astype(bf16)
         wide_hidden = projected[:tokens].astype(bf16)
         wide_back = projected[tokens:].astype(bf16)
-
-        left = jnp.where(up_mask, nt(rank_up_rows, down_act), 0.0).astype(bf16)
-        up_grad = nn(left, wide_back)
+        stacked = jnp.concatenate(
+            [wide_hidden[:, n * LANES : (n + 1) * LANES] for n in range(half)], axis=0
+        )
+        down_grad = nn(left_down, stacked).astype(bf16)
+        up_grad = nn(left_up, wide_back)
         up_rows = jnp.concatenate(
             [up_grad[n * lines : (n + 1) * lines] for n in range(per_row)], axis=1
-        ).astype(bf16)
-
-        left = nt(rank_down_rows, jnp.concatenate([up_back] * half, axis=0))
-        left = jnp.where(down_mask, left, 0.0).astype(bf16)
-        stacked = jnp.concatenate(
-            [wide_hidden[:, n * LANES : (n + 1) * LANES] for n in range(half)], axis=0
-        )
-        down_grad = nn(left, stacked).astype(bf16)
+        )
         repeated = nn(down_grad, spread[...])
         down_rows = repeated[:lines]
         for n in range(1, kr):
             down_rows = jnp.where(rank_at == n, repeated[n * lines : (n + 1) * lines], down_rows)
 
-        up_rows = up_rows.astype(f32)
-        squares = jnp.sum(up_rows * up_rows + down_rows * down_rows, axis=1, keepdims=True)
-        at = (lines, notes.shape[1])
-        slot_of = g * GROUP + iota(at, 0) // half
-        norms += jnp.sum(jnp.where(slot_of == iota(at, 1), squares, 0.0), axis=0, keepdims=True)
         per_owner = CAP * half
         for n in range(GROUP // CAP):
             owner = g * (GROUP // CAP) + n
@@ -185,14 +177,11 @@
                 ],
                 axis=0,
             ).astype(bf16)
-            for c in range(copies):
-                payload[c * owners + owner] = piece
-    notes[...] = jnp.concatenate(
-        [lax.rsqrt(norms + epsilon), counts, jnp.zeros((6, notes.shape[1]), f32)], axis=0
-    )
-
-
-def target_kernel(targets, stacked, inverse, sem):
+            for at in place_of(owner):
+                payload[at] = piece
+
+
+def norm_kernel(slots, direct, targets, payload, stacked, inverse, row_inverse, sem):
     copies = [
         pltpu.make_async_copy(
             targets.at[0, :, pl.ds(n * ROW, ROW)], stacked.at[n], sem.at[n]
@@ -211,28 +200,71 @@
     inverse[...] = jnp.broadcast_to(
         scale * lax.rsqrt(jnp.sum(total, axis=1, keepdims=True) + epsilon), inverse.shape
     )
-
-
-def score_kernel(stacked, inverse, mine, other, notes, back):
+    owners, pieces = slots // CAP, payload.shape[1]
+    step = payload.shape[0] // owners
+    values = jnp.concatenate([payload[n * step] for n in range(owners)], axis=0).astype(f32)
+    squares = jnp.sum(values * values, axis=1, keepdims=True)
+    at = (owners * pieces, row_inverse.shape[1])
+    line = iota(at, 0)
+    owner = line // pieces
+    if direct:
+        owner = jnp.bitwise_xor(owner, lax.axis_index("dp"))
+    slot = owner * CAP + line % pieces % (pieces // 2) // (PIECES // 2)
+    squares = jnp.sum(jnp.where(slot == iota(at, 1), squares, 0.0), axis=0, keepdims=True)
+    row_inverse[...] = jnp.broadcast_to(lax.rsqrt(squares + epsilon), row_inverse.shape)
+
+
+def direct_groups(payload, other, *arrived):
+    d, x, core = (lax.axis_index(name) for name in ("dp", "x", "core"))
+    columns = lax.axis_size("x")
+
+    def place(k, across, on):
+        return (jnp.bitwise_xor(d, k) * columns + jnp.bitwise_xor(x, across)) * CORES + on
+
+    pieces = CAP * PIECES
+    groups = [(payload[0], place(0, 0, core)), (other[0], place(0, 0, 1 - core))]
+    arrived, from_core = arrived[:-1], arrived[-1]
+    for on, mine in ((core, True), (1 - core, False)):
+        start = 0
+        for k, ref in zip(direct_order(lax.axis_size("dp")), arrived):
+            span = ref.shape[0]
+            rows = ref[...] if mine else from_core[start : start + span]
+            start += span
+            if k == 0:
+                groups.append((rows, place(0, 1, on)))
+            else:
+                groups.append((rows[:pieces], place(k, on, on)))
+                groups.append((rows[pieces:], place(k, on, 1 - on)))
+    return groups
+
+
+def gathered_groups(mine, other):
+    core = lax.axis_index("core")
+    sources = mine.shape[0]
+    groups = []
+    step = LANES // (CAP * PIECES)
+    for b in range(0, sources, step):
+        groups += [(mine[n], n * CORES + core) for n in range(b, b + step)]
+        groups += [(other[n], n * CORES + 1 - core) for n in range(b, b + step)]
+    return groups
+
+
+def score_kernel(groups_of, stacked, inverse, notes, *refs):
+    back = refs[-1]
     per_task = TGT // TASKS
     half = PIECES // 2
-    sources = LANES // (CAP * PIECES)
-    own_core = lax.axis_index("core")
     first = lax.axis_index("dp") * CAP
     share = stacked.shape[1]
     line = iota((1, CORES * LANES), 1)
     piece_of = (line // (CAP * half)) % 2 * half + line % half
     inv = inverse[...]
-    dst = iota((CORES * sources, LANES), 0)
-    lane = iota((CORES * sources, LANES), 1)
-    for b in range(mine.shape[0] // sources):
-        block = jnp.concatenate(
-            [
-                mine[b * sources : (b + 1) * sources].reshape(LANES, ROW),
-                other[b * sources : (b + 1) * sources].reshape(LANES, ROW),
-            ],
-            axis=0,
-        )
+    pieces = CAP * PIECES
+    per_block = CORES * LANES // pieces
+    source = iota((per_block, LANES), 0)
+    lane = iota((per_block, LANES), 1)
+    groups = groups_of(*refs[:-1])
+    for b in range(0, len(groups), per_block):
+        block = jnp.concatenate([rows for rows, _ in groups[b : b + per_block]], axis=0)
         whole = nt(stacked[...].reshape(PIECES * share, ROW), block)
         products = whole[:share]
         for n in range(1, PIECES):
@@ -249,19 +281,19 @@
                     top, jnp.sum(total[n * per_task : (n + 1) * per_task], axis=0, keepdims=True)
                 )
             best.append(top)
-        table = jnp.where(dst % CORES == own_core, best[0], best[1])
-        scores = jnp.broadcast_to(notes[1:2, :], (CORES * sources, notes.shape[1]))
+        table = jnp.where(source < per_block // CORES, best[0], best[1])
+        scores = jnp.broadcast_to(notes[0:1, :], (per_block, notes.shape[1]))
         for n in range(CAP):
-            at = lane == dst // CORES * (CAP * PIECES) + n * half
+            at = lane == source % (per_block // CORES) * pieces + n * half
             column = jnp.sum(jnp.where(at, table, 0.0), axis=1, keepdims=True)
             scores = jnp.where(iota(scores.shape, 1) == first + n, column, scores)
-        for n in range(CORES * sources):
-            back[b * CORES * sources + n] = scores[n : n + 1]
-
-
-def finish_kernel(slots, strata_total, returned, dispatch, member, notes, out):
+        for n in range(per_block):
+            back[groups[b + n][1]] = scores[n : n + 1]
+
+
+def finish_kernel(slots, strata_total, returned, dispatch, member, row_inverse, out):
     values = returned[:, 0, :]
-    raw = jnp.max(values, axis=0, keepdims=True) * notes[0:1, :]
+    raw = jnp.max(values, axis=0, keepdims=True) * row_inverse[0:1, :]
     counts = jnp.sum(values, axis=0, keepdims=True)
     held = iota(counts.shape, 1)
     held = jnp.logical_and(held >= slots, held < slots + strata_total)
@@ -272,6 +304,29 @@
     examples = dispatch.shape[0]
     square = iota((examples, LANES), 0) == iota((examples, LANES), 1)
     out[...] = jnp.sum(jnp.where(square, picked, 0.0), axis=0)[:examples]
+
+
+def direct_order(owners):
+    return list(range(owners - 1, -1, -1))
+
+
+def direct_rows(payload, owners, columns):
+    swap = [(n, n ^ 1) for n in range(CORES)]
+    other = lax.ppermute(payload, "core", swap)
+    arrived = []
+    for k in direct_order(owners):
+        pairs = []
+        for d in range(owners):
+            for x in range(columns):
+                for c in range(CORES):
+                    to = (d ^ k, x ^ (1 if k == 0 else c), c)
+                    pairs.append(
+                        ((d * columns + x) * CORES + c, (to[0] * columns + to[1]) * CORES + to[2])
+                    )
+        rows = payload[0] if k == 0 else jnp.concatenate([payload[k], other[k]], axis=0)
+        arrived.append(lax.ppermute(rows, ("dp", "x", "core"), pairs))
+    from_core = lax.ppermute(jnp.concatenate(arrived, axis=0), "core", swap)
+    return [payload, other] + arrived + [from_core]
 
 
 def shards(
@@ -295,12 +350,19 @@
     rank, kr = rank_projection_factor.shape
     share = targets.shape[1]
     chips = owners * columns
+    direct = columns == 2 and owners in (2, 4)
+
+    def places(owner):
+        if direct:
+            return [jnp.bitwise_xor(lax.axis_index("dp"), owner)]
+        return [owner * columns + n for n in range(columns)]
+
     lanes = -(-(slots + strata_total) // LANES) * LANES
 
     payload, dispatch, member, notes = pl.pallas_call(
-        project_kernel,
+        functools.partial(project_kernel, places),
         out_shape=(
-            jax.ShapeDtypeStruct((chips, CAP * PIECES, ROW), bf16),
+            jax.ShapeDtypeStruct((owners if direct else chips, CAP * PIECES, ROW), bf16),
             jax.ShapeDtypeStruct((examples, lanes), f32),
             jax.ShapeDtypeStruct((examples, lanes), f32),
             jax.ShapeDtypeStruct((8, lanes), f32),
@@ -339,31 +401,34 @@
             rank_projection_factor.T,
         )
     )
-    payload, targets = lax.optimization_barrier((payload, targets))
-    stacked, inverse = pl.pallas_call(
-        target_kernel,
+    stacked, inverse, row_inverse = pl.pallas_call(
+        functools.partial(norm_kernel, slots, direct),
         out_shape=(
             jax.ShapeDtypeStruct((PIECES, share, ROW), bf16),
             jax.ShapeDtypeStruct((share, LANES), f32),
+            jax.ShapeDtypeStruct((8, lanes), f32),
         ),
-        in_specs=[pl.BlockSpec(memory_space=pl.ANY)],
-        out_specs=(VMEM, VMEM),
+        in_specs=[pl.BlockSpec(memory_space=pl.ANY), VMEM],
+        out_specs=(VMEM, VMEM, VMEM),
         scratch_shapes=[pltpu.SemaphoreType.DMA((PIECES,))],
         compiler_params=pltpu.CompilerParams(vmem_limit_bytes=20 * 2**20),
         cost_estimate=pl.CostEstimate(flops=4 * share * FEAT, bytes_accessed=4 * share * FEAT, transcendentals=0),
-        name="target_norms",
-    )(targets)
-    mine = lax.all_to_all(payload, ("x", "dp"), split_axis=0, concat_axis=0, tiled=True)
-    other = lax.ppermute(mine, "core", [(n, (n + 1) % CORES) for n in range(CORES)])
+        name="norms",
+    )(targets, payload)
+    if direct:
+        rows = direct_rows(payload, owners, columns)
+    else:
+        mine = lax.all_to_all(payload, ("dp", "x"), split_axis=0, concat_axis=0, tiled=True)
+        rows = [mine, lax.ppermute(mine, "core", [(n, n ^ 1) for n in range(CORES)])]
     back = pl.pallas_call(
-        score_kernel,
+        functools.partial(score_kernel, direct_groups if direct else gathered_groups),
         out_shape=jax.ShapeDtypeStruct((chips * CORES, 1, lanes), f32),
-        in_specs=[VMEM] * 5,
+        in_specs=[VMEM] * (3 + len(rows)),
         out_specs=VMEM,
         compiler_params=pltpu.CompilerParams(vmem_limit_bytes=40 * 2**20),
         name="score",
-    )(stacked, inverse, mine, other, notes)
-    returned = lax.all_to_all(back, ("x", "dp", "core"), split_axis=0, concat_axis=0, tiled=True)
+    )(stacked, inverse, notes, *rows)
+    returned = lax.all_to_all(back, ("dp", "x", "core"), split_axis=0, concat_axis=0, tiled=True)
     return pl.pallas_call(
         functools.partial(finish_kernel, slots, strata_total),
         out_shape=jax.ShapeDtypeStruct((examples,), f32),
@@ -371,7 +436,7 @@
         out_specs=VMEM,
         compiler_params=pltpu.CompilerParams(vmem_limit_bytes=4 * 2**20),
         name="finish",
-    )(returned, dispatch, member, notes)
+    )(returned, dispatch, member, row_inverse)
 
 
 def solution(mesh):

time: 35 us -> 33.1 us (0.946)
  blocking collectives: 25.8 us -> 10.8 us
  starting transfers between devices: 0.01 us -> 8.19 us
  waiting for transfers between devices: 0.24 us -> 5.16 us
    all_to_all x2 -> x1, blocking collectives: 25.8 us -> 10.8 us  [shards(): lax.all_to_all(back, ('dp', 'x', 'core'), split_axis=0, concat_axis=0, ti...]
    ppermute x1 -> x6, starting transfers between devices: 0.01 us -> 8.19 us  [the longest x4 7.27 us: direct_rows(): arrived.append(lax.ppermute(rows, ('dp', 'x', 'core'), pairs))]
    ppermute x1 -> x6, waiting for transfers between devices: 0.24 us -> 5.16 us  [the longest x4 4.19 us: direct_rows(): arrived.append(lax.ppermute(rows, ('dp', 'x', 'core'), pairs))]
  transfers between devices with their start and end apart: 1 -> 6, of which waited for: 1 -> 3; matrix products, arithmetic and copies ran while one was open for 0% -> 0% of each run, Pallas kernels for 4% -> 4%
where the time goes in v4:
time: 33.1 us; the launch traced here: 32.9 us
  blocking collectives  10.8 us (33%)
  starting transfers between devices  8.19 us (25%)
  Pallas kernels  7.99 us (24%)
  waiting for transfers between devices  5.16 us (16%)
  between operations  0.72 us (2%)
    all_to_all x1, blocking collectives, shards(): lax.all_to_all(back, ('dp', 'x', 'core'), split_axis=0, concat_axis=0, ti...  10.8 us
    ppermute x4, starting transfers between devices, direct_rows(): arrived.append(lax.ppermute(rows, ('dp', 'x', 'core'), pairs))  7.27 us
    pallas_call x1, Pallas kernels, shards(): pl.pallas_call(functools.partial(project_kernel, places), out_shape=(jax....  4.72 us
    ppermute x4, waiting for transfers between devices, direct_rows(): arrived.append(lax.ppermute(rows, ('dp', 'x', 'core'), pairs))  4.19 us
    pallas_call x1, Pallas kernels, shards(): pl.pallas_call(functools.partial(score_kernel, direct_groups if direct el...  1.35 us
    pallas_call x1, Pallas kernels, shards(): pl.pallas_call(functools.partial(norm_kernel, slots, direct), out_shape=(...  1.29 us
    ppermute x1, waiting for transfers between devices, direct_rows(): other = lax.ppermute(payload, 'core', swap)  0.97 us
  transfers between devices with their start and end apart: 6, of which 3 were waited for; matrix products, arithmetic and copies ran while one was open for 0% of the time, Pallas kernels for 4%

profile of v4, /device:TPU:0, one launch (start us, length us, event | category | flops | bytes accessed | tf_op | source)
XLA Modules:
  0.0 32.9 jit_solution(4626916136326711323)
XLA Ops:
  0.7 0.0 copy-start
  0.7 4.7 %project.1 = (bf16[4,16,1024]{2,1,0:T(8,128)(2,1)S(1)}, f32[24,128]{1,0:T(8,128)S(1)}, f32[24,128]{1,0:T(8,128)S(1)}, f32[8,128]{1,0:T(8,128)S(1)}) custom-call(s32[1]{0:T(128)S(6)} %copy.12.present, s32[24]{0:T(128)} %strata.1, s32[24]{0:T(128)} %keep.1, s32[32]{0:T(128)} %table.1, bf16[24,8,4096]{2,1,0:T(8,128)(2,1)} %bitcast.18, ...), custom_call_target="tpu_custom_call" | custom-call | tf_op jit(solution)/shard_map/project/pallas_call | solution.py:362
  5.4 0.4 %collective-permute-start = (bf16[4,16,1024]{2,1,0:T(8,128)(2,1)S(1)}, bf16[4,16,1024]{2,1,0:T(8,128)(2,1)S(1)}, u32[]{:S(2)}, u32[]{:S(2)}) collective-permute-start(bf16[4,16,1024]{2,1,0:T(8,128)(2,1)S(1)} %get-tuple-element.12.payload.refs_0_), channel_id=1, source_target_pairs={{0,1},{1,0},{2,3},{3,2},{4,5},{5,4},{6,7},{7,6},{8,9},{9,8},{10,11... | collective-permute-start | bytes 393224 | tf_op jit(solution)/shard_map/ppermute | solution.py:315
  5.8 1.0 %collective-permute-done.refs_1_ = bf16[4,16,1024]{2,1,0:T(8,128)(2,1)S(1)} collective-permute-done((bf16[4,16,1024]{2,1,0:T(8,128)(2,1)S(1)}, bf16[4,16,1024]{2,1,0:T(8,128)(2,1)S(1)}, u32[]{:S(2)}, u32[]{:S(2)}) %collective-permute-start) | collective-permute-done | bytes 131104 | tf_op jit(solution)/shard_map/ppermute | solution.py:315
  6.8 5.0 %collective-permute-start.1 = (bf16[32,1024]{1,0:T(8,128)(2,1)S(1)}, bf16[32,1024]{1,0:T(8,128)(2,1)S(1)}, u32[]{:S(2)}, u32[]{:S(2)}) collective-permute-start(bf16[32,1024]{1,0:T(8,128)(2,1)S(1)} %pad_maximum_fusion.1), channel_id=1, source_target_pairs={{0,12},{1,15},{2,14},{3,13},{4,8},{5,11},{6,10},{7,9},{8,4},{9,7},... | collective-permute-start | bytes 196616 | tf_op jit(solution)/shard_map/ppermute | solution.py:327
  11.8 0.0 collective-permute-start.2
  11.9 0.6 %collective-permute-start.3 = (bf16[32,1024]{1,0:T(8,128)(2,1)S(1)}, bf16[32,1024]{1,0:T(8,128)(2,1)S(1)}, u32[]{:S(2)}, u32[]{:S(2)}) collective-permute-start(bf16[32,1024]{1,0:T(8,128)(2,1)S(1)} %pad_maximum_fusion.3), channel_id=1, source_target_pairs={{0,4},{1,7},{2,6},{3,5},{4,0},{5,3},{6,2},{7,1},{8,12},{9,15},{10,... | collective-permute-start | bytes 196616 | tf_op jit(solution)/shard_map/ppermute | solution.py:327
  12.5 1.6 %collective-permute-start.4 = (bf16[16,1024]{1,0:T(8,128)(2,1)S(1)}, bf16[16,1024]{1,0:T(8,128)(2,1)S(1)}, u32[]{:S(2)}, u32[]{:S(2)}) collective-permute-start(bf16[16,1024]{1,0:T(8,128)(2,1)S(1)} %get-tuple-element.19), channel_id=1, source_target_pairs={{0,2},{1,3},{2,0},{3,1},{4,6},{5,7},{6,4},{7,5},{8,10},{9,11},{10,... | collective-permute-start | bytes 98312 | tf_op jit(solution)/shard_map/ppermute | solution.py:327
  14.1 2.9 %collective-permute-done.4.refs_5_ = bf16[16,1024]{1,0:T(8,128)(2,1)S(1)} collective-permute-done((bf16[16,1024]{1,0:T(8,128)(2,1)S(1)}, bf16[16,1024]{1,0:T(8,128)(2,1)S(1)}, u32[]{:S(2)}, u32[]{:S(2)}) %collective-permute-start.4) | collective-permute-done | bytes 32800 | tf_op jit(solution)/shard_map/ppermute | solution.py:327
  17.1 0.0 collective-permute-done.1.refs_2_
  17.1 1.3 %collective-permute-done.2.refs_3_ = bf16[32,1024]{1,0:T(8,128)(2,1)S(1)} collective-permute-done((bf16[32,1024]{1,0:T(8,128)(2,1)S(1)}, bf16[32,1024]{1,0:T(8,128)(2,1)S(1)}, u32[]{:S(2)}, u32[]{:S(2)}) %collective-permute-start.2) | collective-permute-done | bytes 65568 | tf_op jit(solution)/shard_map/ppermute | solution.py:327
  18.3 0.0 collective-permute-done.3.refs_4_
  18.3 0.5 %collective-permute-start.5 = (bf16[112,1024]{1,0:T(8,128)(2,1)S(1)}, bf16[112,1024]{1,0:T(8,128)(2,1)S(1)}, u32[]{:S(2)}, u32[]{:S(2)}) collective-permute-start(bf16[112,1024]{1,0:T(8,128)(2,1)S(1)} %pad_maximum_fusion), channel_id=1, source_target_pairs={{0,1},{1,0},{2,3},{3,2},{4,5},{5,4},{6,7},{7,6},{8,9},{9,8},{10,11... | collective-permute-start | bytes 688136 | tf_op jit(solution)/shard_map/ppermute | solution.py:328
  18.8 0.0 copy-done
  18.8 1.3 %norms.1 = (bf16[8,192,1024]{2,1,0:T(8,128)(2,1)S(1)}, f32[192,128]{1,0:T(8,128)S(1)}, f32[8,128]{1,0:T(8,128)S(1)}) custom-call(bf16[1,192,8192]{2,1,0:T(8,128)(2,1)S(1)} %copy-done, bf16[4,16,1024]{2,1,0:T(8,128)(2,1)S(1)} %get-tuple-element.12.payload.refs_0_), custom_call_target="tpu_custom_call" | custom-call | flops 6291456 | bytes 6291456 | tf_op jit(solution)/shard_map/norms/pallas_call | solution.py:404
  20.1 0.0 collective-permute-done.5.refs_6_
  20.1 1.4 %score.1 = f32[16,1,128]{2,1,0:T(1,128)S(1)} custom-call(bf16[8,192,1024]{2,1,0:T(8,128)(2,1)S(1)} %get-tuple-element.13.stacked, f32[192,128]{1,0:T(8,128)S(1)} %get-tuple-element.14.inverse, f32[8,128]{1,0:T(8,128)S(1)} %get-tuple-element.15.notes, bf16[4,16,1024]{2,1,0:T(8,128)(2,1)S(1)} %get-tuple-element.12.payload.refs_0_, ...), custom_call_target="tpu_custom_call" | custom-call | tf_op jit(solution)/shard_map/score/pallas_call | solution.py:423
  21.5 10.8 %all_to_all.5.returned = f32[16,1,128]{2,1,0:T(1,128)S(1)} all-to-all(f32[16,1,128]{2,1,0:T(1,128)S(1)} %score.1), channel_id=1, replica_groups=mesh['groups'=2,'dp'=4,'x'=2,'core'=2] {'dp','x','core'}, dimensions={0} | all-to-all | bytes 16384 | tf_op jit(solution)/shard_map/all_to_all | solution.py:431
  32.3 0.6 %finish.1 = f32[24]{0:T(128)} custom-call(f32[16,1,128]{2,1,0:T(1,128)S(1)} %all_to_all.5.returned, f32[24,128]{1,0:T(8,128)S(1)} %get-tuple-element.16.dispatch, f32[24,128]{1,0:T(8,128)S(1)} %get-tuple-element.17.member, f32[8,128]{1,0:T(8,128)S(1)} %get-tuple-element.18.row_inverse), custom_call_target="tpu_custom_call" | custom-call | tf_op jit(solution)/shard_map/finish/pallas_call | solution.py:432
  (6 shorter events, 0.1 us)
Async XLA Ops:
  0.7 18.2 %copy-start = (bf16[1,192,8192]{2,1,0:T(8,128)(2,1)S(1)}, bf16[1,192,8192]{2,1,0:T(8,128)(2,1)}, u32[]{:S(2)}) copy-start(bf16[1,192,8192]{2,1,0:T(8,128)(2,1)} %targets.1) | copy-start | bytes 9437188
  5.4 1.4 %collective-permute-start = (bf16[4,16,1024]{2,1,0:T(8,128)(2,1)S(1)}, bf16[4,16,1024]{2,1,0:T(8,128)(2,1)S(1)}, u32[]{:S(2)}, u32[]{:S(2)}) collective-permute-start(bf16[4,16,1024]{2,1,0:T(8,128)(2,1)S(1)} %get-tuple-element.12.payload.refs_0_), channel_id=1, source_target_pairs={{0,1},{1,0},{2,3},{3,2},{4,5},{5,4},{6,7},{7,6},{8,9},{9,8},{10,11... | collective-permute-start | bytes 393224 | tf_op jit(solution)/shard_map/ppermute | solution.py:315
  6.8 10.2 %collective-permute-start.1 = (bf16[32,1024]{1,0:T(8,128)(2,1)S(1)}, bf16[32,1024]{1,0:T(8,128)(2,1)S(1)}, u32[]{:S(2)}, u32[]{:S(2)}) collective-permute-start(bf16[32,1024]{1,0:T(8,128)(2,1)S(1)} %pad_maximum_fusion.1), channel_id=1, source_target_pairs={{0,12},{1,15},{2,14},{3,13},{4,8},{5,11},{6,10},{7,9},{8,4},{9,7},... | collective-permute-start | bytes 196616 | tf_op jit(solution)/shard_map/ppermute | solution.py:327
  11.8 6.5 %collective-permute-start.2 = (bf16[32,1024]{1,0:T(8,128)(2,1)S(1)}, bf16[32,1024]{1,0:T(8,128)(2,1)S(1)}, u32[]{:S(2)}, u32[]{:S(2)}) collective-permute-start(bf16[32,1024]{1,0:T(8,128)(2,1)S(1)} %pad_maximum_fusion.2), channel_id=1, source_target_pairs={{0,8},{1,11},{2,10},{3,9},{4,12},{5,15},{6,14},{7,13},{8,0},{9,3},... | collective-permute-start | bytes 196616 | tf_op jit(solution)/shard_map/ppermute | solution.py:327
  11.9 6.5 %collective-permute-start.3 = (bf16[32,1024]{1,0:T(8,128)(2,1)S(1)}, bf16[32,1024]{1,0:T(8,128)(2,1)S(1)}, u32[]{:S(2)}, u32[]{:S(2)}) collective-permute-start(bf16[32,1024]{1,0:T(8,128)(2,1)S(1)} %pad_maximum_fusion.3), channel_id=1, source_target_pairs={{0,4},{1,7},{2,6},{3,5},{4,0},{5,3},{6,2},{7,1},{8,12},{9,15},{10,... | collective-permute-start | bytes 196616 | tf_op jit(solution)/shard_map/ppermute | solution.py:327
  12.5 4.6 %collective-permute-start.4 = (bf16[16,1024]{1,0:T(8,128)(2,1)S(1)}, bf16[16,1024]{1,0:T(8,128)(2,1)S(1)}, u32[]{:S(2)}, u32[]{:S(2)}) collective-permute-start(bf16[16,1024]{1,0:T(8,128)(2,1)S(1)} %get-tuple-element.19), channel_id=1, source_target_pairs={{0,2},{1,3},{2,0},{3,1},{4,6},{5,7},{6,4},{7,5},{8,10},{9,11},{10,... | collective-permute-start | bytes 98312 | tf_op jit(solution)/shard_map/ppermute | solution.py:327
  18.3 1.8 %collective-permute-start.5 = (bf16[112,1024]{1,0:T(8,128)(2,1)S(1)}, bf16[112,1024]{1,0:T(8,128)(2,1)S(1)}, u32[]{:S(2)}, u32[]{:S(2)}) collective-permute-start(bf16[112,1024]{1,0:T(8,128)(2,1)S(1)} %pad_maximum_fusion), channel_id=1, source_target_pairs={{0,1},{1,0},{2,3},{3,2},{4,5},{5,4},{6,7},{7,6},{8,9},{9,8},{10,11... | collective-permute-start | bytes 688136 | tf_op jit(solution)/shard_map/ppermute | solution.py:328

commit v5 on v4

--- a/solution.py
+++ b/solution.py
@@ -42,8 +42,8 @@
 
 
 def project_kernel(
-    place_of, present, strata, keep, table, hidden, cotangent, down_t, up, width, rank_t,
-    payload, dispatch, member, notes,
+    place_of, strata, keep, table, hidden, cotangent, down_t, up, width, rank_t,
+    payload, dispatch, member,
     strata_s, keep_s, table_s, taken, chosen, x, adapters, adapters_t, width_v, rank_v, spread,
     small_sem, row_sem, weight_sem,
 ):
@@ -79,22 +79,19 @@
         taken[n] = 0
     for n in range(slots + 1):
         chosen[n] = 0
-    lane = iota((1, notes.shape[1]), 1)
+    lane = iota((1, member.shape[1]), 1)
     for copy in smalls:
         copy.wait()
-    counts = jnp.zeros(lane.shape, f32)
     for e in range(examples):
         stratum = strata_s[e]
-        live = jnp.where(jnp.logical_and(keep_s[e] == 1, e < present[0]), 1, 0)
+        live = jnp.where(keep_s[e] == 1, 1, 0)
         owner = table_s[stratum]
         place = taken[owner]
         taken[owner] = place + live
         slot = jnp.where(jnp.logical_and(live == 1, place < CAP), owner * CAP + place, slots)
         chosen[slot] = e
-        counts += jnp.where(lane == slots + stratum, live.astype(f32), 0.0)
-        member[e : e + 1, :] = (lane == slots + stratum).astype(f32)
+        member[e : e + 1, :] = jnp.where(lane == slots + stratum, live.astype(f32), 0.0)
         dispatch[e : e + 1, :] = jnp.where(jnp.logical_and(lane == slot, lane < slots), 1.0, 0.0)
-    notes[...] = jnp.broadcast_to(counts, notes.shape)
     rows = []
     for n in range(slots):
         rows.append(pltpu.make_async_copy(hidden.at[chosen[n]], x.at[n], row_sem.at[n]))
@@ -181,7 +178,10 @@
                 payload[at] = piece
 
 
-def norm_kernel(slots, direct, targets, payload, stacked, inverse, row_inverse, sem):
+def norm_kernel(
+    slots, direct, present, targets, payload, dispatch, member,
+    stacked, inverse, picks, counts, sem,
+):
     copies = [
         pltpu.make_async_copy(
             targets.at[0, :, pl.ds(n * ROW, ROW)], stacked.at[n], sem.at[n]
@@ -204,14 +204,17 @@
     step = payload.shape[0] // owners
     values = jnp.concatenate([payload[n * step] for n in range(owners)], axis=0).astype(f32)
     squares = jnp.sum(values * values, axis=1, keepdims=True)
-    at = (owners * pieces, row_inverse.shape[1])
+    at = (owners * pieces, picks.shape[1])
     line = iota(at, 0)
     owner = line // pieces
     if direct:
         owner = jnp.bitwise_xor(owner, lax.axis_index("dp"))
     slot = owner * CAP + line % pieces % (pieces // 2) // (PIECES // 2)
     squares = jnp.sum(jnp.where(slot == iota(at, 1), squares, 0.0), axis=0, keepdims=True)
-    row_inverse[...] = jnp.broadcast_to(lax.rsqrt(squares + epsilon), row_inverse.shape)
+    used = iota(picks.shape, 0) < present[0]
+    picks[...] = jnp.where(used, dispatch[...] * lax.rsqrt(squares + epsilon), 0.0)
+    held = jnp.sum(jnp.where(used, member[...], 0.0), axis=0, keepdims=True)
+    counts[...] = jnp.broadcast_to(held, counts.shape)
 
 
 def direct_groups(payload, other, *arrived):
@@ -249,7 +252,7 @@
     return groups
 
 
-def score_kernel(groups_of, stacked, inverse, notes, *refs):
+def score_kernel(groups_of, stacked, inverse, counts, *refs):
     back = refs[-1]
     per_task = TGT // TASKS
     half = PIECES // 2
@@ -282,7 +285,7 @@
                 )
             best.append(top)
         table = jnp.where(source < per_block // CORES, best[0], best[1])
-        scores = jnp.broadcast_to(notes[0:1, :], (per_block, notes.shape[1]))
+        scores = jnp.broadcast_to(counts[0:1, :], (per_block, counts.shape[1]))
         for n in range(CAP):
             at = lane == source % (per_block // CORES) * pieces + n * half
             column = jnp.sum(jnp.where(at, table, 0.0), axis=1, keepdims=True)
@@ -291,26 +294,26 @@
             back[groups[b + n][1]] = scores[n : n + 1]
 
 
-def finish_kernel(slots, strata_total, returned, dispatch, member, row_inverse, out):
+def finish_kernel(slots, strata_total, returned, picks, member, out):
     values = returned[:, 0, :]
-    raw = jnp.max(values, axis=0, keepdims=True) * row_inverse[0:1, :]
+    raw = jnp.max(values, axis=0, keepdims=True)
     counts = jnp.sum(values, axis=0, keepdims=True)
     held = iota(counts.shape, 1)
     held = jnp.logical_and(held >= slots, held < slots + strata_total)
     live = jnp.sum(jnp.where(held, counts, 0.0), axis=1, keepdims=True)
     weight = lax.rsqrt(strata_total * jnp.maximum(counts, 1.0))
-    picked = jnp.sum(dispatch[...] * raw, axis=1, keepdims=True)
+    picked = jnp.sum(picks[...] * raw, axis=1, keepdims=True)
     picked = picked * jnp.sum(member[...] * weight, axis=1, keepdims=True) * jnp.sqrt(live)
-    examples = dispatch.shape[0]
+    examples = picks.shape[0]
     square = iota((examples, LANES), 0) == iota((examples, LANES), 1)
     out[...] = jnp.sum(jnp.where(square, picked, 0.0), axis=0)[:examples]
 
 
 def direct_order(owners):
-    return list(range(owners - 1, -1, -1))
-
-
-def direct_rows(payload, owners, columns):
+    return [2, 1, 3, 0] if owners == 4 else [1, 0]
+
+
+def direct_rows(payload, owners, columns, norms):
     swap = [(n, n ^ 1) for n in range(CORES)]
     other = lax.ppermute(payload, "core", swap)
     arrived = []
@@ -325,8 +328,9 @@
                     )
         rows = payload[0] if k == 0 else jnp.concatenate([payload[k], other[k]], axis=0)
         arrived.append(lax.ppermute(rows, ("dp", "x", "core"), pairs))
+    arrived, norms = lax.optimization_barrier((arrived, norms))
     from_core = lax.ppermute(jnp.concatenate(arrived, axis=0), "core", swap)
-    return [payload, other] + arrived + [from_core]
+    return [payload, other] + arrived + [from_core], norms
 
 
 def shards(
@@ -359,16 +363,15 @@
 
     lanes = -(-(slots + strata_total) // LANES) * LANES
 
-    payload, dispatch, member, notes = pl.pallas_call(
+    payload, dispatch, member = pl.pallas_call(
         functools.partial(project_kernel, places),
         out_shape=(
             jax.ShapeDtypeStruct((owners if direct else chips, CAP * PIECES, ROW), bf16),
             jax.ShapeDtypeStruct((examples, lanes), f32),
             jax.ShapeDtypeStruct((examples, lanes), f32),
-            jax.ShapeDtypeStruct((8, lanes), f32),
         ),
-        in_specs=[pl.BlockSpec(memory_space=pltpu.SMEM)] + [HBM] * 9,
-        out_specs=(VMEM,) * 4,
+        in_specs=[HBM] * 9,
+        out_specs=(VMEM,) * 3,
         scratch_shapes=[
             pltpu.SMEM((examples,), i32),
             pltpu.SMEM((examples,), i32),
@@ -388,7 +391,6 @@
         compiler_params=pltpu.CompilerParams(vmem_limit_bytes=40 * 2**20),
         name="project",
     )(
-        shard_example_count,
         *in_hbm(
             strata,
             keep,
@@ -401,22 +403,25 @@
             rank_projection_factor.T,
         )
     )
-    stacked, inverse, row_inverse = pl.pallas_call(
+    stacked, inverse, picks, counts = pl.pallas_call(
         functools.partial(norm_kernel, slots, direct),
         out_shape=(
             jax.ShapeDtypeStruct((PIECES, share, ROW), bf16),
             jax.ShapeDtypeStruct((share, LANES), f32),
+            jax.ShapeDtypeStruct((examples, lanes), f32),
             jax.ShapeDtypeStruct((8, lanes), f32),
         ),
-        in_specs=[pl.BlockSpec(memory_space=pl.ANY), VMEM],
-        out_specs=(VMEM, VMEM, VMEM),
+        in_specs=[
+            pl.BlockSpec(memory_space=pltpu.SMEM), pl.BlockSpec(memory_space=pl.ANY), VMEM, VMEM, VMEM
+        ],
+        out_specs=(VMEM,) * 4,
         scratch_shapes=[pltpu.SemaphoreType.DMA((PIECES,))],
         compiler_params=pltpu.CompilerParams(vmem_limit_bytes=20 * 2**20),
         cost_estimate=pl.CostEstimate(flops=4 * share * FEAT, bytes_accessed=4 * share * FEAT, transcendentals=0),
         name="norms",
-    )(targets, payload)
+    )(shard_example_count, targets, payload, dispatch, member)
     if direct:
-        rows = direct_rows(payload, owners, columns)
+        rows, (stacked, inverse, picks, counts) = direct_rows(payload, owners, columns, (stacked, inverse, picks, counts))
     else:
         mine = lax.all_to_all(payload, ("dp", "x"), split_axis=0, concat_axis=0, tiled=True)
         rows = [mine, lax.ppermute(mine, "core", [(n, n ^ 1) for n in range(CORES)])]
@@ -427,16 +432,16 @@
         out_specs=VMEM,
         compiler_params=pltpu.CompilerParams(vmem_limit_bytes=40 * 2**20),
         name="score",
-    )(stacked, inverse, notes, *rows)
+    )(stacked, inverse, counts, *rows)
     returned = lax.all_to_all(back, ("dp", "x", "core"), split_axis=0, concat_axis=0, tiled=True)
     return pl.pallas_call(
         functools.partial(finish_kernel, slots, strata_total),
         out_shape=jax.ShapeDtypeStruct((examples,), f32),
-        in_specs=[VMEM] * 4,
+        in_specs=[VMEM] * 3,
         out_specs=VMEM,
         compiler_params=pltpu.CompilerParams(vmem_limit_bytes=4 * 2**20),
         name="finish",
-    )(returned, dispatch, member, row_inverse)
+    )(returned, picks, member)
 
 
 def solution(mesh):

time: 33.1 us -> 32 us (0.967)
  blocking collectives: 10.8 us -> 10.2 us
    ppermute x4, waiting for transfers between devices: 4.19 us -> 2.76 us  [direct_rows(): arrived.append(lax.ppermute(rows, ('dp', 'x', 'core'), pairs))]
    ppermute x1, waiting for transfers between devices: 0.01 us -> 1.35 us  [direct_rows(): from_core = lax.ppermute(jnp.concatenate(arrived, axis=0), 'core', swap)]
    all_to_all x1, blocking collectives: 10.8 us -> 10.2 us  [shards(): lax.all_to_all(back, ('dp', 'x', 'core'), split_axis=0, concat_axis=0, ti...]
  transfers between devices with their start and end apart: 6 -> 6, of which waited for: 3 -> 4; matrix products, arithmetic and copies ran while one was open for 0% -> 0% of each run, Pallas kernels for 4% -> 4%
where the time goes in v5:
time: 32 us; the launch traced here: 31.9 us
  blocking collectives  10.2 us (32%)
  starting transfers between devices  8.02 us (25%)
  Pallas kernels  7.83 us (24%)
  waiting for transfers between devices  5.09 us (16%)
  between operations  0.71 us (2%)
    all_to_all x1, blocking collectives, shards(): lax.all_to_all(back, ('dp', 'x', 'core'), split_axis=0, concat_axis=0, ti...  10.2 us
    ppermute x4, starting transfers between devices, direct_rows(): arrived.append(lax.ppermute(rows, ('dp', 'x', 'core'), pairs))  7.17 us
    pallas_call x1, Pallas kernels, shards(): pl.pallas_call(functools.partial(project_kernel, places), out_shape=(jax....  4.62 us
    ppermute x4, waiting for transfers between devices, direct_rows(): arrived.append(lax.ppermute(rows, ('dp', 'x', 'core'), pairs))  2.76 us
    ppermute x1, waiting for transfers between devices, direct_rows(): from_core = lax.ppermute(jnp.concatenate(arrived, axis=0), 'core', swap)  1.35 us
    pallas_call x1, Pallas kernels, shards(): pl.pallas_call(functools.partial(score_kernel, direct_groups if direct el...  1.33 us
    pallas_call x1, Pallas kernels, shards(): pl.pallas_call(functools.partial(norm_kernel, slots, direct), out_shape=(...  1.26 us
    ppermute x1, waiting for transfers between devices, direct_rows(): other = lax.ppermute(payload, 'core', swap)  0.97 us
  transfers between devices with their start and end apart: 6, of which 4 were waited for; matrix products, arithmetic and copies ran while one was open for 0% of the time, Pallas kernels for 4%

profile of v5, /device:TPU:0, one launch (start us, length us, event | category | flops | bytes accessed | tf_op | source)
XLA Modules:
  0.0 31.9 jit_solution(16253123322317908989)
XLA Ops:
  0.0 0.0 copy-start
  0.0 4.6 %project.1 = (bf16[4,16,1024]{2,1,0:T(8,128)(2,1)S(1)}, f32[24,128]{1,0:T(8,128)S(1)}, f32[24,128]{1,0:T(8,128)S(1)}) custom-call(s32[24]{0:T(128)} %strata.1, s32[24]{0:T(128)} %keep.1, s32[32]{0:T(128)} %table.1, bf16[24,8,4096]{2,1,0:T(8,128)(2,1)} %bitcast.18, bf16[24,8,4096]{2,1,0:T(8,128)(2,1)} %bitcast.19, bf16[64,4096]{1,0:T(8,128)(2,1)} %bitcast.20, ...), custom_call_target="tpu_custom_call" | custom-call | tf_op jit(solution)/shard_map/project/pallas_call | solution.py:366
  4.6 0.7 %collective-permute-start = (bf16[4,16,1024]{2,1,0:T(8,128)(2,1)S(1)}, bf16[4,16,1024]{2,1,0:T(8,128)(2,1)S(1)}, u32[]{:S(2)}, u32[]{:S(2)}) collective-permute-start(bf16[4,16,1024]{2,1,0:T(8,128)(2,1)S(1)} %get-tuple-element.20.payload.refs_0_), channel_id=1, source_target_pairs={{0,1},{1,0},{2,3},{3,2},{4,5},{5,4},{6,7},{7,6},{8,9},{9,8},{10,11... | collective-permute-start | bytes 393224 | tf_op jit(solution)/shard_map/ppermute | solution.py:318
  5.3 1.0 %collective-permute-done.refs_1_ = bf16[4,16,1024]{2,1,0:T(8,128)(2,1)S(1)} collective-permute-done((bf16[4,16,1024]{2,1,0:T(8,128)(2,1)S(1)}, bf16[4,16,1024]{2,1,0:T(8,128)(2,1)S(1)}, u32[]{:S(2)}, u32[]{:S(2)}) %collective-permute-start) | collective-permute-done | bytes 131104 | tf_op jit(solution)/shard_map/ppermute | solution.py:318
  6.3 3.9 %collective-permute-start.1 = (bf16[32,1024]{1,0:T(8,128)(2,1)S(1)}, bf16[32,1024]{1,0:T(8,128)(2,1)S(1)}, u32[]{:S(2)}, u32[]{:S(2)}) collective-permute-start(bf16[32,1024]{1,0:T(8,128)(2,1)S(1)} %pad_maximum_fusion.1), channel_id=1, source_target_pairs={{0,8},{1,11},{2,10},{3,9},{4,12},{5,15},{6,14},{7,13},{8,0},{9,3},... | collective-permute-start | bytes 196616 | tf_op jit(solution)/shard_map/ppermute | solution.py:330
  10.2 1.6 %collective-permute-start.2 = (bf16[32,1024]{1,0:T(8,128)(2,1)S(1)}, bf16[32,1024]{1,0:T(8,128)(2,1)S(1)}, u32[]{:S(2)}, u32[]{:S(2)}) collective-permute-start(bf16[32,1024]{1,0:T(8,128)(2,1)S(1)} %pad_maximum_fusion.2), channel_id=1, source_target_pairs={{0,4},{1,7},{2,6},{3,5},{4,0},{5,3},{6,2},{7,1},{8,12},{9,15},{10,... | collective-permute-start | bytes 196616 | tf_op jit(solution)/shard_map/ppermute | solution.py:330
  11.8 0.0 collective-permute-start.3
  11.8 1.7 %collective-permute-start.4 = (bf16[16,1024]{1,0:T(8,128)(2,1)S(1)}, bf16[16,1024]{1,0:T(8,128)(2,1)S(1)}, u32[]{:S(2)}, u32[]{:S(2)}) collective-permute-start(bf16[16,1024]{1,0:T(8,128)(2,1)S(1)} %get-tuple-element.35), channel_id=1, source_target_pairs={{0,2},{1,3},{2,0},{3,1},{4,6},{5,7},{6,4},{7,5},{8,10},{9,11},{10,... | collective-permute-start | bytes 98312 | tf_op jit(solution)/shard_map/ppermute | solution.py:330
  14.1 0.0 copy-done
  14.1 1.3 %norms.1 = (bf16[8,192,1024]{2,1,0:T(8,128)(2,1)S(1)}, f32[192,128]{1,0:T(8,128)S(1)}, f32[24,128]{1,0:T(8,128)S(1)}, f32[8,128]{1,0:T(8,128)S(1)}) custom-call(s32[1]{0:T(128)S(6)} %copy.12.present, bf16[1,192,8192]{2,1,0:T(8,128)(2,1)S(1)} %copy-done, bf16[4,16,1024]{2,1,0:T(8,128)(2,1)S(1)} %get-tuple-element.20.payload.refs_0_, ...), custom_call_target="tpu_custom_call" | custom-call | flops 6291456 | bytes 6291456 | tf_op jit(solution)/shard_map/norms/pallas_call | solution.py:406
  15.4 0.8 %collective-permute-done.4.refs_5_ = bf16[16,1024]{1,0:T(8,128)(2,1)S(1)} collective-permute-done((bf16[16,1024]{1,0:T(8,128)(2,1)S(1)}, bf16[16,1024]{1,0:T(8,128)(2,1)S(1)}, u32[]{:S(2)}, u32[]{:S(2)}) %collective-permute-start.4) | collective-permute-done | bytes 32800 | tf_op jit(solution)/shard_map/ppermute | solution.py:330
  16.2 0.0 collective-permute-done.1.refs_2_
  16.3 0.0 collective-permute-done.2.refs_3_
  16.3 1.9 %collective-permute-done.3.refs_4_ = bf16[32,1024]{1,0:T(8,128)(2,1)S(1)} collective-permute-done((bf16[32,1024]{1,0:T(8,128)(2,1)S(1)}, bf16[32,1024]{1,0:T(8,128)(2,1)S(1)}, u32[]{:S(2)}, u32[]{:S(2)}) %collective-permute-start.3) | collective-permute-done | bytes 65568 | tf_op jit(solution)/shard_map/ppermute | solution.py:330
  18.2 0.2 collective-permute-start.5
  18.4 1.4 %collective-permute-done.5.refs_6_ = bf16[112,1024]{1,0:T(8,128)(2,1)S(1)} collective-permute-done((bf16[112,1024]{1,0:T(8,128)(2,1)S(1)}, bf16[112,1024]{1,0:T(8,128)(2,1)S(1)}, u32[]{:S(2)}, u32[]{:S(2)}) %collective-permute-start.5) | collective-permute-done | bytes 229408 | tf_op jit(solution)/shard_map/ppermute | solution.py:332
  19.7 1.3 %score.1 = f32[16,1,128]{2,1,0:T(1,128)S(1)} custom-call(bf16[8,192,1024]{2,1,0:T(8,128)(2,1)S(1)} %get-tuple-element.27.stacked, f32[192,128]{1,0:T(8,128)S(1)} %get-tuple-element.28.inverse, f32[8,128]{1,0:T(8,128)S(1)} %get-tuple-element.29.counts, bf16[4,16,1024]{2,1,0:T(8,128)(2,1)S(1)} %get-tuple-element.20.payload.refs_0_, ...), custom_call_target="tpu_custom_call" | custom-call | tf_op jit(solution)/shard_map/score/pallas_call | solution.py:428
  21.1 10.2 %all_to_all.5.returned = f32[16,1,128]{2,1,0:T(1,128)S(1)} all-to-all(f32[16,1,128]{2,1,0:T(1,128)S(1)} %score.1), channel_id=1, replica_groups=mesh['groups'=2,'dp'=4,'x'=2,'core'=2] {'dp','x','core'}, dimensions={0} | all-to-all | bytes 16384 | tf_op jit(solution)/shard_map/all_to_all | solution.py:436
  31.2 0.6 %finish.1 = f32[24]{0:T(128)} custom-call(f32[16,1,128]{2,1,0:T(1,128)S(1)} %all_to_all.5.returned, f32[24,128]{1,0:T(8,128)S(1)} %get-tuple-element.34.picks, f32[24,128]{1,0:T(8,128)S(1)} %get-tuple-element.22.member), custom_call_target="tpu_custom_call" | custom-call | tf_op jit(solution)/shard_map/finish/pallas_call | solution.py:437
  (6 shorter events, 0.0 us)
Async XLA Ops:
  0.0 14.1 %copy-start = (bf16[1,192,8192]{2,1,0:T(8,128)(2,1)S(1)}, bf16[1,192,8192]{2,1,0:T(8,128)(2,1)}, u32[]{:S(2)}) copy-start(bf16[1,192,8192]{2,1,0:T(8,128)(2,1)} %targets.1) | copy-start | bytes 9437188
  4.6 1.6 %collective-permute-start = (bf16[4,16,1024]{2,1,0:T(8,128)(2,1)S(1)}, bf16[4,16,1024]{2,1,0:T(8,128)(2,1)S(1)}, u32[]{:S(2)}, u32[]{:S(2)}) collective-permute-start(bf16[4,16,1024]{2,1,0:T(8,128)(2,1)S(1)} %get-tuple-element.20.payload.refs_0_), channel_id=1, source_target_pairs={{0,1},{1,0},{2,3},{3,2},{4,5},{5,4},{6,7},{7,6},{8,9},{9,8},{10,11... | collective-permute-start | bytes 393224 | tf_op jit(solution)/shard_map/ppermute | solution.py:318
  6.3 10.0 %collective-permute-start.1 = (bf16[32,1024]{1,0:T(8,128)(2,1)S(1)}, bf16[32,1024]{1,0:T(8,128)(2,1)S(1)}, u32[]{:S(2)}, u32[]{:S(2)}) collective-permute-start(bf16[32,1024]{1,0:T(8,128)(2,1)S(1)} %pad_maximum_fusion.1), channel_id=1, source_target_pairs={{0,8},{1,11},{2,10},{3,9},{4,12},{5,15},{6,14},{7,13},{8,0},{9,3},... | collective-permute-start | bytes 196616 | tf_op jit(solution)/shard_map/ppermute | solution.py:330
  10.2 6.1 %collective-permute-start.2 = (bf16[32,1024]{1,0:T(8,128)(2,1)S(1)}, bf16[32,1024]{1,0:T(8,128)(2,1)S(1)}, u32[]{:S(2)}, u32[]{:S(2)}) collective-permute-start(bf16[32,1024]{1,0:T(8,128)(2,1)S(1)} %pad_maximum_fusion.2), channel_id=1, source_target_pairs={{0,4},{1,7},{2,6},{3,5},{4,0},{5,3},{6,2},{7,1},{8,12},{9,15},{10,... | collective-permute-start | bytes 196616 | tf_op jit(solution)/shard_map/ppermute | solution.py:330
  11.8 6.4 %collective-permute-start.3 = (bf16[32,1024]{1,0:T(8,128)(2,1)S(1)}, bf16[32,1024]{1,0:T(8,128)(2,1)S(1)}, u32[]{:S(2)}, u32[]{:S(2)}) collective-permute-start(bf16[32,1024]{1,0:T(8,128)(2,1)S(1)} %pad_maximum_fusion.3), channel_id=1, source_target_pairs={{0,12},{1,15},{2,14},{3,13},{4,8},{5,11},{6,10},{7,9},{8,4},{9,7},... | collective-permute-start | bytes 196616 | tf_op jit(solution)/shard_map/ppermute | solution.py:330
  11.8 4.5 %collective-permute-start.4 = (bf16[16,1024]{1,0:T(8,128)(2,1)S(1)}, bf16[16,1024]{1,0:T(8,128)(2,1)S(1)}, u32[]{:S(2)}, u32[]{:S(2)}) collective-permute-start(bf16[16,1024]{1,0:T(8,128)(2,1)S(1)} %get-tuple-element.35), channel_id=1, source_target_pairs={{0,2},{1,3},{2,0},{3,1},{4,6},{5,7},{6,4},{7,5},{8,10},{9,11},{10,... | collective-permute-start | bytes 98312 | tf_op jit(solution)/shard_map/ppermute | solution.py:330
  18.2 1.6 %collective-permute-start.5 = (bf16[112,1024]{1,0:T(8,128)(2,1)S(1)}, bf16[112,1024]{1,0:T(8,128)(2,1)S(1)}, u32[]{:S(2)}, u32[]{:S(2)}) collective-permute-start(bf16[112,1024]{1,0:T(8,128)(2,1)S(1)} %pad_maximum_fusion), channel_id=1, source_target_pairs={{0,1},{1,0},{2,3},{3,2},{4,5},{5,4},{6,7},{7,6},{8,9},{9,8},{10,11... | collective-permute-start | bytes 688136 | tf_op jit(solution)/shard_map/ppermute | solution.py:332

commit v6 on v5

--- a/solution.py
+++ b/solution.py
@@ -137,18 +137,19 @@
                 axis=0,
             )
 
-        adapted = nn(both(0, model), adapters_t[...])
-        down_act = adapted[:tokens, :rank].astype(bf16)
-        up_back = adapted[tokens:, rank:].astype(bf16)
-        left_up = jnp.where(up_mask, nt(rank_up_rows, down_act), 0.0).astype(bf16)
-        left_down = nt(rank_down_rows, jnp.concatenate([up_back] * half, axis=0))
-        left_down = jnp.where(down_mask, left_down, 0.0).astype(bf16)
         for n in range(parts):
             if g == 0:
                 weights[3 + n].wait()
             span = pl.ds(n * depth, depth)
             part = nn(both(n * depth, depth), width_v[span, :])
             projected = part if n == 0 else projected + part
+            if n == 0:
+                adapted = nn(both(0, model), adapters_t[...])
+                down_act = adapted[:tokens, :rank].astype(bf16)
+                up_back = adapted[tokens:, rank:].astype(bf16)
+                left_up = jnp.where(up_mask, nt(rank_up_rows, down_act), 0.0).astype(bf16)
+                left_down = nt(rank_down_rows, jnp.concatenate([up_back] * half, axis=0))
+                left_down = jnp.where(down_mask, left_down, 0.0).astype(bf16)
         wide_hidden = projected[:tokens].astype(bf16)
         wide_back = projected[tokens:].astype(bf16)
         stacked = jnp.concatenate(
@@ -310,7 +311,7 @@
 
 
 def direct_order(owners):
-    return [2, 1, 3, 0] if owners == 4 else [1, 0]
+    return [2, 1, 0, 3] if owners == 4 else [1, 0]
 
 
 def direct_rows(payload, owners, columns, norms):
@@ -412,14 +413,14 @@
             jax.ShapeDtypeStruct((8, lanes), f32),
         ),
         in_specs=[
-            pl.BlockSpec(memory_space=pltpu.SMEM), pl.BlockSpec(memory_space=pl.ANY), VMEM, VMEM, VMEM
+            pl.BlockSpec(memory_space=pltpu.SMEM), HBM, VMEM, VMEM, VMEM
         ],
         out_specs=(VMEM,) * 4,
         scratch_shapes=[pltpu.SemaphoreType.DMA((PIECES,))],
         compiler_params=pltpu.CompilerParams(vmem_limit_bytes=20 * 2**20),
         cost_estimate=pl.CostEstimate(flops=4 * share * FEAT, bytes_accessed=4 * share * FEAT, transcendentals=0),
         name="norms",
-    )(shard_example_count, targets, payload, dispatch, member)
+    )(shard_example_count, *in_hbm(targets), payload, dispatch, member)
     if direct:
         rows, (stacked, inverse, picks, counts) = direct_rows(payload, owners, columns, (stacked, inverse, picks, counts))
     else:

time: 32 us -> 31.9 us (level)
  waiting for transfers between devices: 5.09 us -> 4.29 us
  Pallas kernels: 7.83 us -> 8.48 us
    pallas_call x1, Pallas kernels: 1.26 us -> 2.09 us  [shards(): pl.pallas_call(functools.partial(norm_kernel, slots, direct), out_shape=(...]
    ppermute x4, waiting for transfers between devices: 2.76 us -> 1.96 us  [direct_rows(): arrived.append(lax.ppermute(rows, ('dp', 'x', 'core'), pairs))]
  transfers between devices with their start and end apart: 6 -> 6, of which waited for: 4 -> 3; matrix products, arithmetic and copies ran while one was open for 0% -> 0% of each run, Pallas kernels for 4% -> 7%
where the time goes in v6:
time: 31.9 us; the launch traced here: 31.7 us
  blocking collectives  10.2 us (32%)
  Pallas kernels  8.48 us (27%)
  starting transfers between devices  8.02 us (25%)
  waiting for transfers between devices  4.29 us (13%)
  between operations  0.7 us (2%)
    all_to_all x1, blocking collectives, shards(): lax.all_to_all(back, ('dp', 'x', 'core'), split_axis=0, concat_axis=0, ti...  10.2 us
    ppermute x4, starting transfers between devices, direct_rows(): arrived.append(lax.ppermute(rows, ('dp', 'x', 'core'), pairs))  7.3 us
    pallas_call x1, Pallas kernels, shards(): pl.pallas_call(functools.partial(project_kernel, places), out_shape=(jax....  4.44 us
    pallas_call x1, Pallas kernels, shards(): pl.pallas_call(functools.partial(norm_kernel, slots, direct), out_shape=(...  2.09 us
    ppermute x4, waiting for transfers between devices, direct_rows(): arrived.append(lax.ppermute(rows, ('dp', 'x', 'core'), pairs))  1.96 us
    ppermute x1, waiting for transfers between devices, direct_rows(): from_core = lax.ppermute(jnp.concatenate(arrived, axis=0), 'core', swap)  1.35 us
    pallas_call x1, Pallas kernels, shards(): pl.pallas_call(functools.partial(score_kernel, direct_groups if direct el...  1.33 us
    ppermute x1, waiting for transfers between devices, direct_rows(): other = lax.ppermute(payload, 'core', swap)  0.97 us
  transfers between devices with their start and end apart: 6, of which 3 were waited for; matrix products, arithmetic and copies ran while one was open for 0% of the time, Pallas kernels for 7%

profile of v6, /device:TPU:0, one launch (start us, length us, event | category | flops | bytes accessed | tf_op | source)
XLA Modules:
  0.0 31.7 jit_solution(12025433914352515250)
XLA Ops:
  0.0 4.4 %project.1 = (bf16[4,16,1024]{2,1,0:T(8,128)(2,1)S(1)}, f32[24,128]{1,0:T(8,128)S(1)}, f32[24,128]{1,0:T(8,128)S(1)}) custom-call(s32[24]{0:T(128)} %strata.1, s32[24]{0:T(128)} %keep.1, s32[32]{0:T(128)} %table.1, bf16[24,8,4096]{2,1,0:T(8,128)(2,1)} %bitcast.18, bf16[24,8,4096]{2,1,0:T(8,128)(2,1)} %bitcast.19, bf16[64,4096]{1,0:T(8,128)(2,1)} %bitcast.20, ...), custom_call_target="tpu_custom_call" | custom-call | tf_op jit(solution)/shard_map/project/pallas_call | solution.py:367
  4.5 0.5 %collective-permute-start = (bf16[4,16,1024]{2,1,0:T(8,128)(2,1)S(1)}, bf16[4,16,1024]{2,1,0:T(8,128)(2,1)S(1)}, u32[]{:S(2)}, u32[]{:S(2)}) collective-permute-start(bf16[4,16,1024]{2,1,0:T(8,128)(2,1)S(1)} %get-tuple-element.20.payload.refs_0_), channel_id=1, source_target_pairs={{0,1},{1,0},{2,3},{3,2},{4,5},{5,4},{6,7},{7,6},{8,9},{9,8},{10,11... | collective-permute-start | bytes 393224 | tf_op jit(solution)/shard_map/ppermute | solution.py:319
  5.0 1.0 %collective-permute-done.refs_1_ = bf16[4,16,1024]{2,1,0:T(8,128)(2,1)S(1)} collective-permute-done((bf16[4,16,1024]{2,1,0:T(8,128)(2,1)S(1)}, bf16[4,16,1024]{2,1,0:T(8,128)(2,1)S(1)}, u32[]{:S(2)}, u32[]{:S(2)}) %collective-permute-start) | collective-permute-done | bytes 131104 | tf_op jit(solution)/shard_map/ppermute | solution.py:319
  6.0 4.0 %collective-permute-start.1 = (bf16[32,1024]{1,0:T(8,128)(2,1)S(1)}, bf16[32,1024]{1,0:T(8,128)(2,1)S(1)}, u32[]{:S(2)}, u32[]{:S(2)}) collective-permute-start(bf16[32,1024]{1,0:T(8,128)(2,1)S(1)} %pad_maximum_fusion.1), channel_id=1, source_target_pairs={{0,8},{1,11},{2,10},{3,9},{4,12},{5,15},{6,14},{7,13},{8,0},{9,3},... | collective-permute-start | bytes 196616 | tf_op jit(solution)/shard_map/ppermute | solution.py:331
  10.0 1.6 %collective-permute-start.2 = (bf16[32,1024]{1,0:T(8,128)(2,1)S(1)}, bf16[32,1024]{1,0:T(8,128)(2,1)S(1)}, u32[]{:S(2)}, u32[]{:S(2)}) collective-permute-start(bf16[32,1024]{1,0:T(8,128)(2,1)S(1)} %pad_maximum_fusion.2), channel_id=1, source_target_pairs={{0,4},{1,7},{2,6},{3,5},{4,0},{5,3},{6,2},{7,1},{8,12},{9,15},{10,... | collective-permute-start | bytes 196616 | tf_op jit(solution)/shard_map/ppermute | solution.py:331
  11.6 0.0 collective-permute-start.4
  11.6 1.7 %collective-permute-start.3 = (bf16[16,1024]{1,0:T(8,128)(2,1)S(1)}, bf16[16,1024]{1,0:T(8,128)(2,1)S(1)}, u32[]{:S(2)}, u32[]{:S(2)}) collective-permute-start(bf16[16,1024]{1,0:T(8,128)(2,1)S(1)} %get-tuple-element.36), channel_id=1, source_target_pairs={{0,2},{1,3},{2,0},{3,1},{4,6},{5,7},{6,4},{7,5},{8,10},{9,11},{10,... | collective-permute-start | bytes 98312 | tf_op jit(solution)/shard_map/ppermute | solution.py:331
  13.9 2.1 %norms.1 = (bf16[8,192,1024]{2,1,0:T(8,128)(2,1)S(1)}, f32[192,128]{1,0:T(8,128)S(1)}, f32[24,128]{1,0:T(8,128)S(1)}, f32[8,128]{1,0:T(8,128)S(1)}) custom-call(s32[1]{0:T(128)S(6)} %copy.12.present, bf16[1,192,8192]{2,1,0:T(8,128)(2,1)} %targets.1, bf16[4,16,1024]{2,1,0:T(8,128)(2,1)S(1)} %get-tuple-element.20.payload.refs_0_, ...), custom_call_target="tpu_custom_call" | custom-call | flops 6291456 | bytes 6291456 | tf_op jit(solution)/shard_map/norms/pallas_call | solution.py:407
  16.0 0.0 collective-permute-done.3.refs_4_
  16.1 0.0 collective-permute-done.1.refs_2_
  16.1 0.0 collective-permute-done.2.refs_3_
  16.1 1.9 %collective-permute-done.4.refs_5_ = bf16[32,1024]{1,0:T(8,128)(2,1)S(1)} collective-permute-done((bf16[32,1024]{1,0:T(8,128)(2,1)S(1)}, bf16[32,1024]{1,0:T(8,128)(2,1)S(1)}, u32[]{:S(2)}, u32[]{:S(2)}) %collective-permute-start.4) | collective-permute-done | bytes 65568 | tf_op jit(solution)/shard_map/ppermute | solution.py:331
  18.0 0.2 collective-permute-start.5
  18.2 1.4 %collective-permute-done.5.refs_6_ = bf16[112,1024]{1,0:T(8,128)(2,1)S(1)} collective-permute-done((bf16[112,1024]{1,0:T(8,128)(2,1)S(1)}, bf16[112,1024]{1,0:T(8,128)(2,1)S(1)}, u32[]{:S(2)}, u32[]{:S(2)}) %collective-permute-start.5) | collective-permute-done | bytes 229408 | tf_op jit(solution)/shard_map/ppermute | solution.py:333
  19.6 1.3 %score.1 = f32[16,1,128]{2,1,0:T(1,128)S(1)} custom-call(bf16[8,192,1024]{2,1,0:T(8,128)(2,1)S(1)} %get-tuple-element.27.stacked, f32[192,128]{1,0:T(8,128)S(1)} %get-tuple-element.28.inverse, f32[8,128]{1,0:T(8,128)S(1)} %get-tuple-element.29.counts, bf16[4,16,1024]{2,1,0:T(8,128)(2,1)S(1)} %get-tuple-element.20.payload.refs_0_, ...), custom_call_target="tpu_custom_call" | custom-call | tf_op jit(solution)/shard_map/score/pallas_call | solution.py:429
  20.9 10.2 %all_to_all.5.returned = f32[16,1,128]{2,1,0:T(1,128)S(1)} all-to-all(f32[16,1,128]{2,1,0:T(1,128)S(1)} %score.1), channel_id=1, replica_groups=mesh['groups'=2,'dp'=4,'x'=2,'core'=2] {'dp','x','core'}, dimensions={0} | all-to-all | bytes 16384 | tf_op jit(solution)/shard_map/all_to_all | solution.py:437
  31.1 0.6 %finish.1 = f32[24]{0:T(128)} custom-call(f32[16,1,128]{2,1,0:T(1,128)S(1)} %all_to_all.5.returned, f32[24,128]{1,0:T(8,128)S(1)} %get-tuple-element.34.picks, f32[24,128]{1,0:T(8,128)S(1)} %get-tuple-element.22.member), custom_call_target="tpu_custom_call" | custom-call | tf_op jit(solution)/shard_map/finish/pallas_call | solution.py:438
  (6 shorter events, 0.0 us)
Async XLA Ops:
  4.5 1.5 %collective-permute-start = (bf16[4,16,1024]{2,1,0:T(8,128)(2,1)S(1)}, bf16[4,16,1024]{2,1,0:T(8,128)(2,1)S(1)}, u32[]{:S(2)}, u32[]{:S(2)}) collective-permute-start(bf16[4,16,1024]{2,1,0:T(8,128)(2,1)S(1)} %get-tuple-element.20.payload.refs_0_), channel_id=1, source_target_pairs={{0,1},{1,0},{2,3},{3,2},{4,5},{5,4},{6,7},{7,6},{8,9},{9,8},{10,11... | collective-permute-start | bytes 393224 | tf_op jit(solution)/shard_map/ppermute | solution.py:319
  6.0 10.1 %collective-permute-start.1 = (bf16[32,1024]{1,0:T(8,128)(2,1)S(1)}, bf16[32,1024]{1,0:T(8,128)(2,1)S(1)}, u32[]{:S(2)}, u32[]{:S(2)}) collective-permute-start(bf16[32,1024]{1,0:T(8,128)(2,1)S(1)} %pad_maximum_fusion.1), channel_id=1, source_target_pairs={{0,8},{1,11},{2,10},{3,9},{4,12},{5,15},{6,14},{7,13},{8,0},{9,3},... | collective-permute-start | bytes 196616 | tf_op jit(solution)/shard_map/ppermute | solution.py:331
  10.0 6.1 %collective-permute-start.2 = (bf16[32,1024]{1,0:T(8,128)(2,1)S(1)}, bf16[32,1024]{1,0:T(8,128)(2,1)S(1)}, u32[]{:S(2)}, u32[]{:S(2)}) collective-permute-start(bf16[32,1024]{1,0:T(8,128)(2,1)S(1)} %pad_maximum_fusion.2), channel_id=1, source_target_pairs={{0,4},{1,7},{2,6},{3,5},{4,0},{5,3},{6,2},{7,1},{8,12},{9,15},{10,... | collective-permute-start | bytes 196616 | tf_op jit(solution)/shard_map/ppermute | solution.py:331
  11.6 6.4 %collective-permute-start.4 = (bf16[32,1024]{1,0:T(8,128)(2,1)S(1)}, bf16[32,1024]{1,0:T(8,128)(2,1)S(1)}, u32[]{:S(2)}, u32[]{:S(2)}) collective-permute-start(bf16[32,1024]{1,0:T(8,128)(2,1)S(1)} %pad_maximum_fusion.3), channel_id=1, source_target_pairs={{0,12},{1,15},{2,14},{3,13},{4,8},{5,11},{6,10},{7,9},{8,4},{9,7},... | collective-permute-start | bytes 196616 | tf_op jit(solution)/shard_map/ppermute | solution.py:331
  11.6 4.5 %collective-permute-start.3 = (bf16[16,1024]{1,0:T(8,128)(2,1)S(1)}, bf16[16,1024]{1,0:T(8,128)(2,1)S(1)}, u32[]{:S(2)}, u32[]{:S(2)}) collective-permute-start(bf16[16,1024]{1,0:T(8,128)(2,1)S(1)} %get-tuple-element.36), channel_id=1, source_target_pairs={{0,2},{1,3},{2,0},{3,1},{4,6},{5,7},{6,4},{7,5},{8,10},{9,11},{10,... | collective-permute-start | bytes 98312 | tf_op jit(solution)/shard_map/ppermute | solution.py:331
  18.0 1.6 %collective-permute-start.5 = (bf16[112,1024]{1,0:T(8,128)(2,1)S(1)}, bf16[112,1024]{1,0:T(8,128)(2,1)S(1)}, u32[]{:S(2)}, u32[]{:S(2)}) collective-permute-start(bf16[112,1024]{1,0:T(8,128)(2,1)S(1)} %pad_maximum_fusion), channel_id=1, source_target_pairs={{0,1},{1,0},{2,3},{3,2},{4,5},{5,4},{6,7},{7,6},{8,9},{9,8},{10,11... | collective-permute-start | bytes 688136 | tf_op jit(solution)/shard_map/ppermute | solution.py:333

commit v7 on v6

--- a/solution.py
+++ b/solution.py
@@ -14,6 +14,7 @@
 TASKS = 16
 SEQ = 8
 CORES = 2
+SWAP = [(0, 1), (1, 0)]
 LANES = 128
 ROW = 1024
 PIECES = FEAT // ROW
@@ -295,8 +296,14 @@
             back[groups[b + n][1]] = scores[n : n + 1]
 
 
-def finish_kernel(slots, strata_total, returned, picks, member, out):
-    values = returned[:, 0, :]
+def finish_kernel(slots, strata_total, direct, picks, member, *refs):
+    returned, out = refs[:-1], refs[-1]
+    if direct:
+        d, x, core = (lax.axis_index(name) for name in ("dp", "x", "core"))
+        place = (d * lax.axis_size("x") + x) * CORES + core
+        values = jnp.concatenate([ref[place] for ref in returned], axis=0)
+    else:
+        values = returned[0][:, 0, :]
     raw = jnp.max(values, axis=0, keepdims=True)
     counts = jnp.sum(values, axis=0, keepdims=True)
     held = iota(counts.shape, 1)
@@ -314,23 +321,37 @@
     return [2, 1, 0, 3] if owners == 4 else [1, 0]
 
 
+def direct_pairs(k, owners, columns):
+    pairs = []
+    for d in range(owners):
+        for x in range(columns):
+            for c in range(CORES):
+                to = (d ^ k, x ^ (1 if k == 0 else c), c)
+                pairs.append(
+                    ((d * columns + x) * CORES + c, (to[0] * columns + to[1]) * CORES + to[2])
+                )
+    return pairs
+
+
+def direct_return(back, owners, columns, slots):
+    def merge(a, b):
+        return jnp.where(iota(a.shape, 2) < slots, jnp.maximum(a, b), a + b)
+
+    chip = merge(back, lax.ppermute(back, "core", SWAP))
+    order = [3, 1, 2, 0] if owners == 4 else [1, 0]
+    got = [lax.ppermute(chip, ("dp", "x", "core"), direct_pairs(k, owners, columns)) for k in order]
+    far = functools.reduce(merge, [part for k, part in zip(order, got) if k > 0])
+    return [chip, got[order.index(0)], far, lax.ppermute(far, "core", SWAP)]
+
+
 def direct_rows(payload, owners, columns, norms):
-    swap = [(n, n ^ 1) for n in range(CORES)]
-    other = lax.ppermute(payload, "core", swap)
+    other = lax.ppermute(payload, "core", SWAP)
     arrived = []
     for k in direct_order(owners):
-        pairs = []
-        for d in range(owners):
-            for x in range(columns):
-                for c in range(CORES):
-                    to = (d ^ k, x ^ (1 if k == 0 else c), c)
-                    pairs.append(
-                        ((d * columns + x) * CORES + c, (to[0] * columns + to[1]) * CORES + to[2])
-                    )
         rows = payload[0] if k == 0 else jnp.concatenate([payload[k], other[k]], axis=0)
-        arrived.append(lax.ppermute(rows, ("dp", "x", "core"), pairs))
+        arrived.append(lax.ppermute(rows, ("dp", "x", "core"), direct_pairs(k, owners, columns)))
     arrived, norms = lax.optimization_barrier((arrived, norms))
-    from_core = lax.ppermute(jnp.concatenate(arrived, axis=0), "core", swap)
+    from_core = lax.ppermute(jnp.concatenate(arrived, axis=0), "core", SWAP)
     return [payload, other] + arrived + [from_core], norms
 
 
@@ -425,7 +446,7 @@
         rows, (stacked, inverse, picks, counts) = direct_rows(payload, owners, columns, (stacked, inverse, picks, counts))
     else:
         mine = lax.all_to_all(payload, ("dp", "x"), split_axis=0, concat_axis=0, tiled=True)
-        rows = [mine, lax.ppermute(mine, "core", [(n, n ^ 1) for n in range(CORES)])]
+        rows = [mine, lax.ppermute(mine, "core", SWAP)]
     back = pl.pallas_call(
         functools.partial(score_kernel, direct_groups if direct else gathered_groups),
         out_shape=jax.ShapeDtypeStruct((chips * CORES, 1, lanes), f32),
@@ -434,15 +455,20 @@
         compiler_params=pltpu.CompilerParams(vmem_limit_bytes=40 * 2**20),
         name="score",
     )(stacked, inverse, counts, *rows)
-    returned = lax.all_to_all(back, ("dp", "x", "core"), split_axis=0, concat_axis=0, tiled=True)
+    if direct:
+        returned = direct_return(back, owners, columns, slots)
+    else:
+        returned = [
+            lax.all_to_all(back, ("dp", "x", "core"), split_axis=0, concat_axis=0, tiled=True)
+        ]
     return pl.pallas_call(
-        functools.partial(finish_kernel, slots, strata_total),
+        functools.partial(finish_kernel, slots, strata_total, direct),
         out_shape=jax.ShapeDtypeStruct((examples,), f32),
-        in_specs=[VMEM] * 3,
+        in_specs=[VMEM] * (2 + len(returned)),
         out_specs=VMEM,
         compiler_params=pltpu.CompilerParams(vmem_limit_bytes=4 * 2**20),
         name="finish",
-    )(returned, picks, member)
+    )(picks, member, *returned)
 
 
 def solution(mesh):

time: 31.9 us -> 31.4 us (0.984)
  blocking collectives: 10.2 us -> 0 us
  starting transfers between devices: 8.02 us -> 15.1 us
  waiting for transfers between devices: 4.29 us -> 6.84 us
    all_to_all x1 -> x0, blocking collectives: 10.2 us -> none  [shards(): lax.all_to_all(back, ('dp', 'x', 'core'), split_axis=0, concat_axis=0, ti...]
    ppermute x6 -> x12, starting transfers between devices: 8.02 us -> 15.1 us  [the longest x4 7.3 us: direct_rows(): lax.ppermute(rows, ('dp', 'x', 'core'), direct_pairs(k, owners, columns))]
    ppermute x6 -> x12, waiting for transfers between devices: 4.29 us -> 6.84 us  [the longest x4 2.11 us: direct_return(): lax.ppermute(chip, ('dp', 'x', 'core'), direct_pairs(k, owners, columns))]
  transfers between devices with their start and end apart: 6 -> 12, of which waited for: 3 -> 8; matrix products, arithmetic and copies ran while one was open for 0% -> 0% of each run, Pallas kernels for 7% -> 7%
where the time goes in v7:
time: 31.4 us; the launch traced here: 31.2 us
  starting transfers between devices  15.1 us (48%)
  Pallas kernels  8.48 us (27%)
  waiting for transfers between devices  6.84 us (22%)
  between operations  0.72 us (2%)
    ppermute x4, starting transfers between devices, direct_rows(): lax.ppermute(rows, ('dp', 'x', 'core'), direct_pairs(k, owners, columns))  7.3 us
    ppermute x4, starting transfers between devices, direct_return(): lax.ppermute(chip, ('dp', 'x', 'core'), direct_pairs(k, owners, columns))  4.85 us
    pallas_call x1, Pallas kernels, shards(): pl.pallas_call(functools.partial(project_kernel, places), out_shape=(jax....  4.44 us
    ppermute x4, waiting for transfers between devices, direct_return(): lax.ppermute(chip, ('dp', 'x', 'core'), direct_pairs(k, owners, columns))  2.11 us
    pallas_call x1, Pallas kernels, shards(): pl.pallas_call(functools.partial(norm_kernel, slots, direct), out_shape=(...  2.09 us
    ppermute x1, starting transfers between devices, direct_rows(): from_core = lax.ppermute(jnp.concatenate(arrived, axis=0), 'core', SWAP)  1.62 us
    pallas_call x1, Pallas kernels, shards(): pl.pallas_call(functools.partial(score_kernel, direct_groups if direct el...  1.33 us
    ppermute x4, waiting for transfers between devices, direct_rows(): lax.ppermute(rows, ('dp', 'x', 'core'), direct_pairs(k, owners, columns))  1.14 us
  transfers between devices with their start and end apart: 12, of which 8 were waited for; matrix products, arithmetic and copies ran while one was open for 0% of the time, Pallas kernels for 7%

profile of v7, /device:TPU:0, one launch (start us, length us, event | category | flops | bytes accessed | tf_op | source)
XLA Modules:
  0.0 31.2 jit_solution(10301122254237029394)
XLA Ops:
  0.0 4.4 %project.1 = (bf16[4,16,1024]{2,1,0:T(8,128)(2,1)S(1)}, f32[24,128]{1,0:T(8,128)S(1)}, f32[24,128]{1,0:T(8,128)S(1)}) custom-call(s32[24]{0:T(128)} %strata.1, s32[24]{0:T(128)} %keep.1, s32[32]{0:T(128)} %table.1, bf16[24,8,4096]{2,1,0:T(8,128)(2,1)} %bitcast.18, bf16[24,8,4096]{2,1,0:T(8,128)(2,1)} %bitcast.19, bf16[64,4096]{1,0:T(8,128)(2,1)} %bitcast.20, ...), custom_call_target="tpu_custom_call" | custom-call | tf_op jit(solution)/shard_map/project/pallas_call | solution.py:388
  4.5 0.5 %collective-permute-start = (bf16[4,16,1024]{2,1,0:T(8,128)(2,1)S(1)}, bf16[4,16,1024]{2,1,0:T(8,128)(2,1)S(1)}, u32[]{:S(2)}, u32[]{:S(2)}) collective-permute-start(bf16[4,16,1024]{2,1,0:T(8,128)(2,1)S(1)} %get-tuple-element.20.payload.refs_0_), channel_id=1, source_target_pairs={{0,1},{1,0},{2,3},{3,2},{4,5},{5,4},{6,7},{7,6},{8,9},{9,8},{10,11... | collective-permute-start | bytes 393224 | tf_op jit(solution)/shard_map/ppermute | solution.py:348
  5.0 1.0 %collective-permute-done.refs_1_ = bf16[4,16,1024]{2,1,0:T(8,128)(2,1)S(1)} collective-permute-done((bf16[4,16,1024]{2,1,0:T(8,128)(2,1)S(1)}, bf16[4,16,1024]{2,1,0:T(8,128)(2,1)S(1)}, u32[]{:S(2)}, u32[]{:S(2)}) %collective-permute-start) | collective-permute-done | bytes 131104 | tf_op jit(solution)/shard_map/ppermute | solution.py:348
  6.0 5.0 %collective-permute-start.4 = (bf16[32,1024]{1,0:T(8,128)(2,1)S(1)}, bf16[32,1024]{1,0:T(8,128)(2,1)S(1)}, u32[]{:S(2)}, u32[]{:S(2)}) collective-permute-start(bf16[32,1024]{1,0:T(8,128)(2,1)S(1)} %pad_maximum_fusion.3), channel_id=1, source_target_pairs={{0,12},{1,15},{2,14},{3,13},{4,8},{5,11},{6,10},{7,9},{8,4},{9,7},... | collective-permute-start | bytes 196616 | tf_op jit(solution)/shard_map/ppermute | solution.py:352
  11.0 0.0 collective-permute-start.2
  11.0 0.6 %collective-permute-start.1 = (bf16[32,1024]{1,0:T(8,128)(2,1)S(1)}, bf16[32,1024]{1,0:T(8,128)(2,1)S(1)}, u32[]{:S(2)}, u32[]{:S(2)}) collective-permute-start(bf16[32,1024]{1,0:T(8,128)(2,1)S(1)} %pad_maximum_fusion.1), channel_id=1, source_target_pairs={{0,8},{1,11},{2,10},{3,9},{4,12},{5,15},{6,14},{7,13},{8,0},{9,3},... | collective-permute-start | bytes 196616 | tf_op jit(solution)/shard_map/ppermute | solution.py:352
  11.7 1.6 %collective-permute-start.3 = (bf16[16,1024]{1,0:T(8,128)(2,1)S(1)}, bf16[16,1024]{1,0:T(8,128)(2,1)S(1)}, u32[]{:S(2)}, u32[]{:S(2)}) collective-permute-start(bf16[16,1024]{1,0:T(8,128)(2,1)S(1)} %get-tuple-element.36), channel_id=1, source_target_pairs={{0,2},{1,3},{2,0},{3,1},{4,6},{5,7},{6,4},{7,5},{8,10},{9,11},{10,... | collective-permute-start | bytes 98312 | tf_op jit(solution)/shard_map/ppermute | solution.py:352
  13.9 2.1 %norms.1 = (bf16[8,192,1024]{2,1,0:T(8,128)(2,1)S(1)}, f32[192,128]{1,0:T(8,128)S(1)}, f32[24,128]{1,0:T(8,128)S(1)}, f32[8,128]{1,0:T(8,128)S(1)}) custom-call(s32[1]{0:T(128)S(6)} %copy.12.present, bf16[1,192,8192]{2,1,0:T(8,128)(2,1)} %targets.1, bf16[4,16,1024]{2,1,0:T(8,128)(2,1)S(1)} %get-tuple-element.20.payload.refs_0_, ...), custom_call_target="tpu_custom_call" | custom-call | flops 6291456 | bytes 6291456 | tf_op jit(solution)/shard_map/norms/pallas_call | solution.py:428
  16.0 0.7 %collective-permute-done.3.refs_4_ = bf16[16,1024]{1,0:T(8,128)(2,1)S(1)} collective-permute-done((bf16[16,1024]{1,0:T(8,128)(2,1)S(1)}, bf16[16,1024]{1,0:T(8,128)(2,1)S(1)}, u32[]{:S(2)}, u32[]{:S(2)}) %collective-permute-start.3) | collective-permute-done | bytes 32800 | tf_op jit(solution)/shard_map/ppermute | solution.py:352
  16.7 0.0 collective-permute-done.4.refs_5_
  16.7 0.5 %collective-permute-done.2.refs_3_ = bf16[32,1024]{1,0:T(8,128)(2,1)S(1)} collective-permute-done((bf16[32,1024]{1,0:T(8,128)(2,1)S(1)}, bf16[32,1024]{1,0:T(8,128)(2,1)S(1)}, u32[]{:S(2)}, u32[]{:S(2)}) %collective-permute-start.2) | collective-permute-done | bytes 65568 | tf_op jit(solution)/shard_map/ppermute | solution.py:352
  17.2 0.0 collective-permute-done.1.refs_2_
  17.2 1.6 %collective-permute-start.5 = (bf16[112,1024]{1,0:T(8,128)(2,1)S(1)}, bf16[112,1024]{1,0:T(8,128)(2,1)S(1)}, u32[]{:S(2)}, u32[]{:S(2)}) collective-permute-start(bf16[112,1024]{1,0:T(8,128)(2,1)S(1)} %pad_maximum_fusion), channel_id=1, source_target_pairs={{0,1},{1,0},{2,3},{3,2},{4,5},{5,4},{6,7},{7,6},{8,9},{9,8},{10,11... | collective-permute-start | bytes 688136 | tf_op jit(solution)/shard_map/ppermute | solution.py:354
  18.8 1.1 %collective-permute-done.5.refs_6_ = bf16[112,1024]{1,0:T(8,128)(2,1)S(1)} collective-permute-done((bf16[112,1024]{1,0:T(8,128)(2,1)S(1)}, bf16[112,1024]{1,0:T(8,128)(2,1)S(1)}, u32[]{:S(2)}, u32[]{:S(2)}) %collective-permute-start.5) | collective-permute-done | bytes 229408 | tf_op jit(solution)/shard_map/ppermute | solution.py:354
  19.9 1.3 %score.1 = f32[16,1,128]{2,1,0:T(1,128)S(1)} custom-call(bf16[8,192,1024]{2,1,0:T(8,128)(2,1)S(1)} %get-tuple-element.28.stacked, f32[192,128]{1,0:T(8,128)S(1)} %get-tuple-element.29.inverse, f32[8,128]{1,0:T(8,128)S(1)} %get-tuple-element.30.counts, bf16[4,16,1024]{2,1,0:T(8,128)(2,1)S(1)} %get-tuple-element.20.payload.refs_0_, ...), custom_call_target="tpu_custom_call" | custom-call | tf_op jit(solution)/shard_map/score/pallas_call | solution.py:450
  21.3 0.4 %collective-permute-start.6 = (f32[16,1,128]{2,1,0:T(1,128)S(1)}, f32[16,1,128]{2,1,0:T(1,128)S(1)}, u32[]{:S(2)}, u32[]{:S(2)}) collective-permute-start(f32[16,1,128]{2,1,0:T(1,128)S(1)} %score.1), channel_id=1, source_target_pairs={{0,1},{1,0},{2,3},{3,2},{4,5},{5,4},{6,7},{7,6},{8,9},{9,8},{10,11... | collective-permute-start | bytes 24584 | tf_op jit(solution)/shard_map/ppermute | solution.py:340
  21.7 0.8 %collective-permute-done.6 = f32[16,1,128]{2,1,0:T(1,128)S(1)} collective-permute-done((f32[16,1,128]{2,1,0:T(1,128)S(1)}, f32[16,1,128]{2,1,0:T(1,128)S(1)}, u32[]{:S(2)}, u32[]{:S(2)}) %collective-permute-start.6) | collective-permute-done | bytes 8224 | tf_op jit(solution)/shard_map/ppermute | solution.py:340
  22.6 1.3 %collective-permute-start.10 = (f32[16,1,128]{2,1,0:T(1,128)S(1)}, f32[16,1,128]{2,1,0:T(1,128)S(1)}, u32[]{:S(2)}, u32[]{:S(2)}) collective-permute-start(f32[16,1,128]{2,1,0:T(1,128)S(1)} %broadcast_select_fusion.2.refs_0_), channel_id=1, source_target_pairs={{0,8},{1,11},{2,10},{3,9},{4,12},{5,15},{6,14},{7,13},{8,0},{9,3},... | collective-permute-start | bytes 24584 | tf_op jit(solution)/shard_map/ppermute | solution.py:342
  23.8 1.3 %collective-permute-start.8 = (f32[16,1,128]{2,1,0:T(1,128)S(1)}, f32[16,1,128]{2,1,0:T(1,128)S(1)}, u32[]{:S(2)}, u32[]{:S(2)}) collective-permute-start(f32[16,1,128]{2,1,0:T(1,128)S(1)} %broadcast_select_fusion.2.refs_0_), channel_id=1, source_target_pairs={{0,12},{1,15},{2,14},{3,13},{4,8},{5,11},{6,10},{7,9},{8,4},{9,7},... | collective-permute-start | bytes 24584 | tf_op jit(solution)/shard_map/ppermute | solution.py:342
  25.2 0.9 %collective-permute-start.9 = (f32[16,1,128]{2,1,0:T(1,128)S(1)}, f32[16,1,128]{2,1,0:T(1,128)S(1)}, u32[]{:S(2)}, u32[]{:S(2)}) collective-permute-start(f32[16,1,128]{2,1,0:T(1,128)S(1)} %broadcast_select_fusion.2.refs_0_), channel_id=1, source_target_pairs={{0,4},{1,7},{2,6},{3,5},{4,0},{5,3},{6,2},{7,1},{8,12},{9,15},{10,... | collective-permute-start | bytes 24584 | tf_op jit(solution)/shard_map/ppermute | solution.py:342
  26.1 1.3 %collective-permute-start.7 = (f32[16,1,128]{2,1,0:T(1,128)S(1)}, f32[16,1,128]{2,1,0:T(1,128)S(1)}, u32[]{:S(2)}, u32[]{:S(2)}) collective-permute-start(f32[16,1,128]{2,1,0:T(1,128)S(1)} %broadcast_select_fusion.2.refs_0_), channel_id=1, source_target_pairs={{0,2},{1,3},{2,0},{3,1},{4,6},{5,7},{6,4},{7,5},{8,10},{9,11},{10,... | collective-permute-start | bytes 24584 | tf_op jit(solution)/shard_map/ppermute | solution.py:342
  27.4 0.0 collective-permute-done.10
  27.4 1.9 %collective-permute-done.8 = f32[16,1,128]{2,1,0:T(1,128)S(1)} collective-permute-done((f32[16,1,128]{2,1,0:T(1,128)S(1)}, f32[16,1,128]{2,1,0:T(1,128)S(1)}, u32[]{:S(2)}, u32[]{:S(2)}) %collective-permute-start.8) | collective-permute-done | bytes 8224 | tf_op jit(solution)/shard_map/ppermute | solution.py:342
  29.3 0.0 collective-permute-done.9
  29.4 0.4 %collective-permute-start.11 = (f32[16,1,128]{2,1,0:T(1,128)S(1)}, f32[16,1,128]{2,1,0:T(1,128)S(1)}, u32[]{:S(2)}, u32[]{:S(2)}) collective-permute-start(f32[16,1,128]{2,1,0:T(1,128)S(1)} %broadcast_select_fusion.refs_2_), channel_id=1, source_target_pairs={{0,1},{1,0},{2,3},{3,2},{4,5},{5,4},{6,7},{7,6},{8,9},{9,8},{10,11... | collective-permute-start | bytes 24584 | tf_op jit(solution)/shard_map/ppermute | solution.py:344
  29.7 0.2 collective-permute-done.7.refs_1_
  29.9 0.7 %collective-permute-done.11.refs_3_ = f32[16,1,128]{2,1,0:T(1,128)S(1)} collective-permute-done((f32[16,1,128]{2,1,0:T(1,128)S(1)}, f32[16,1,128]{2,1,0:T(1,128)S(1)}, u32[]{:S(2)}, u32[]{:S(2)}) %collective-permute-start.11) | collective-permute-done | bytes 8224 | tf_op jit(solution)/shard_map/ppermute | solution.py:344
  30.6 0.6 %finish.1 = f32[24]{0:T(128)} custom-call(f32[24,128]{1,0:T(8,128)S(1)} %get-tuple-element.27.picks, f32[24,128]{1,0:T(8,128)S(1)} %get-tuple-element.22.member, f32[16,1,128]{2,1,0:T(1,128)S(1)} %broadcast_select_fusion.2.refs_0_, f32[16,1,128]{2,1,0:T(1,128)S(1)} %collective-permute-done.7.refs_1_, f32[16,1,128]{2,1,0:T(1,128)S(1)} %broadcast_select_fusion.refs_2_, ...), custom_call_target="tpu_custom_call" | custom-call | tf_op jit(solution)/shard_map/finish/pallas_call | solution.py:464
  (9 shorter events, 0.1 us)
Async XLA Ops:
  4.5 1.5 %collective-permute-start = (bf16[4,16,1024]{2,1,0:T(8,128)(2,1)S(1)}, bf16[4,16,1024]{2,1,0:T(8,128)(2,1)S(1)}, u32[]{:S(2)}, u32[]{:S(2)}) collective-permute-start(bf16[4,16,1024]{2,1,0:T(8,128)(2,1)S(1)} %get-tuple-element.20.payload.refs_0_), channel_id=1, source_target_pairs={{0,1},{1,0},{2,3},{3,2},{4,5},{5,4},{6,7},{7,6},{8,9},{9,8},{10,11... | collective-permute-start | bytes 393224 | tf_op jit(solution)/shard_map/ppermute | solution.py:348
  6.0 10.7 %collective-permute-start.4 = (bf16[32,1024]{1,0:T(8,128)(2,1)S(1)}, bf16[32,1024]{1,0:T(8,128)(2,1)S(1)}, u32[]{:S(2)}, u32[]{:S(2)}) collective-permute-start(bf16[32,1024]{1,0:T(8,128)(2,1)S(1)} %pad_maximum_fusion.3), channel_id=1, source_target_pairs={{0,12},{1,15},{2,14},{3,13},{4,8},{5,11},{6,10},{7,9},{8,4},{9,7},... | collective-permute-start | bytes 196616 | tf_op jit(solution)/shard_map/ppermute | solution.py:352
  11.0 6.2 %collective-permute-start.2 = (bf16[32,1024]{1,0:T(8,128)(2,1)S(1)}, bf16[32,1024]{1,0:T(8,128)(2,1)S(1)}, u32[]{:S(2)}, u32[]{:S(2)}) collective-permute-start(bf16[32,1024]{1,0:T(8,128)(2,1)S(1)} %pad_maximum_fusion.2), channel_id=1, source_target_pairs={{0,4},{1,7},{2,6},{3,5},{4,0},{5,3},{6,2},{7,1},{8,12},{9,15},{10,... | collective-permute-start | bytes 196616 | tf_op jit(solution)/shard_map/ppermute | solution.py:352
  11.0 6.1 %collective-permute-start.1 = (bf16[32,1024]{1,0:T(8,128)(2,1)S(1)}, bf16[32,1024]{1,0:T(8,128)(2,1)S(1)}, u32[]{:S(2)}, u32[]{:S(2)}) collective-permute-start(bf16[32,1024]{1,0:T(8,128)(2,1)S(1)} %pad_maximum_fusion.1), channel_id=1, source_target_pairs={{0,8},{1,11},{2,10},{3,9},{4,12},{5,15},{6,14},{7,13},{8,0},{9,3},... | collective-permute-start | bytes 196616 | tf_op jit(solution)/shard_map/ppermute | solution.py:352
  11.7 5.0 %collective-permute-start.3 = (bf16[16,1024]{1,0:T(8,128)(2,1)S(1)}, bf16[16,1024]{1,0:T(8,128)(2,1)S(1)}, u32[]{:S(2)}, u32[]{:S(2)}) collective-permute-start(bf16[16,1024]{1,0:T(8,128)(2,1)S(1)} %get-tuple-element.36), channel_id=1, source_target_pairs={{0,2},{1,3},{2,0},{3,1},{4,6},{5,7},{6,4},{7,5},{8,10},{9,11},{10,... | collective-permute-start | bytes 98312 | tf_op jit(solution)/shard_map/ppermute | solution.py:352
  17.2 2.7 %collective-permute-start.5 = (bf16[112,1024]{1,0:T(8,128)(2,1)S(1)}, bf16[112,1024]{1,0:T(8,128)(2,1)S(1)}, u32[]{:S(2)}, u32[]{:S(2)}) collective-permute-start(bf16[112,1024]{1,0:T(8,128)(2,1)S(1)} %pad_maximum_fusion), channel_id=1, source_target_pairs={{0,1},{1,0},{2,3},{3,2},{4,5},{5,4},{6,7},{7,6},{8,9},{9,8},{10,11... | collective-permute-start | bytes 688136 | tf_op jit(solution)/shard_map/ppermute | solution.py:354
  21.3 1.3 %collective-permute-start.6 = (f32[16,1,128]{2,1,0:T(1,128)S(1)}, f32[16,1,128]{2,1,0:T(1,128)S(1)}, u32[]{:S(2)}, u32[]{:S(2)}) collective-permute-start(f32[16,1,128]{2,1,0:T(1,128)S(1)} %score.1), channel_id=1, source_target_pairs={{0,1},{1,0},{2,3},{3,2},{4,5},{5,4},{6,7},{7,6},{8,9},{9,8},{10,11... | collective-permute-start | bytes 24584 | tf_op jit(solution)/shard_map/ppermute | solution.py:340
  22.6 4.9 %collective-permute-start.10 = (f32[16,1,128]{2,1,0:T(1,128)S(1)}, f32[16,1,128]{2,1,0:T(1,128)S(1)}, u32[]{:S(2)}, u32[]{:S(2)}) collective-permute-start(f32[16,1,128]{2,1,0:T(1,128)S(1)} %broadcast_select_fusion.2.refs_0_), channel_id=1, source_target_pairs={{0,8},{1,11},{2,10},{3,9},{4,12},{5,15},{6,14},{7,13},{8,0},{9,3},... | collective-permute-start | bytes 24584 | tf_op jit(solution)/shard_map/ppermute | solution.py:342
  23.8 5.5 %collective-permute-start.8 = (f32[16,1,128]{2,1,0:T(1,128)S(1)}, f32[16,1,128]{2,1,0:T(1,128)S(1)}, u32[]{:S(2)}, u32[]{:S(2)}) collective-permute-start(f32[16,1,128]{2,1,0:T(1,128)S(1)} %broadcast_select_fusion.2.refs_0_), channel_id=1, source_target_pairs={{0,12},{1,15},{2,14},{3,13},{4,8},{5,11},{6,10},{7,9},{8,4},{9,7},... | collective-permute-start | bytes 24584 | tf_op jit(solution)/shard_map/ppermute | solution.py:342
  25.2 4.2 %collective-permute-start.9 = (f32[16,1,128]{2,1,0:T(1,128)S(1)}, f32[16,1,128]{2,1,0:T(1,128)S(1)}, u32[]{:S(2)}, u32[]{:S(2)}) collective-permute-start(f32[16,1,128]{2,1,0:T(1,128)S(1)} %broadcast_select_fusion.2.refs_0_), channel_id=1, source_target_pairs={{0,4},{1,7},{2,6},{3,5},{4,0},{5,3},{6,2},{7,1},{8,12},{9,15},{10,... | collective-permute-start | bytes 24584 | tf_op jit(solution)/shard_map/ppermute | solution.py:342
  26.1 3.8 %collective-permute-start.7 = (f32[16,1,128]{2,1,0:T(1,128)S(1)}, f32[16,1,128]{2,1,0:T(1,128)S(1)}, u32[]{:S(2)}, u32[]{:S(2)}) collective-permute-start(f32[16,1,128]{2,1,0:T(1,128)S(1)} %broadcast_select_fusion.2.refs_0_), channel_id=1, source_target_pairs={{0,2},{1,3},{2,0},{3,1},{4,6},{5,7},{6,4},{7,5},{8,10},{9,11},{10,... | collective-permute-start | bytes 24584 | tf_op jit(solution)/shard_map/ppermute | solution.py:342
  29.4 1.2 %collective-permute-start.11 = (f32[16,1,128]{2,1,0:T(1,128)S(1)}, f32[16,1,128]{2,1,0:T(1,128)S(1)}, u32[]{:S(2)}, u32[]{:S(2)}) collective-permute-start(f32[16,1,128]{2,1,0:T(1,128)S(1)} %broadcast_select_fusion.refs_2_), channel_id=1, source_target_pairs={{0,1},{1,0},{2,3},{3,2},{4,5},{5,4},{6,7},{7,6},{8,9},{9,8},{10,11... | collective-permute-start | bytes 24584 | tf_op jit(solution)/shard_map/ppermute | solution.py:344

commit v8 on v7

--- a/solution.py
+++ b/solution.py
@@ -220,26 +220,22 @@
 
 
 def direct_groups(payload, other, *arrived):
-    d, x, core = (lax.axis_index(name) for name in ("dp", "x", "core"))
-    columns = lax.axis_size("x")
-
-    def place(k, across, on):
-        return (jnp.bitwise_xor(d, k) * columns + jnp.bitwise_xor(x, across)) * CORES + on
-
+    core = lax.axis_index("core")
     pieces = CAP * PIECES
-    groups = [(payload[0], place(0, 0, core)), (other[0], place(0, 0, 1 - core))]
+    home = lambda n, on: [(0, (n, on)), (1, (n, on))]
+    groups = [(payload[0], home(0, core)), (other[0], home(0, 1 - core))]
     arrived, from_core = arrived[:-1], arrived[-1]
-    for on, mine in ((core, True), (1 - core, False)):
+    for out, on in ((0, core), (1, 1 - core)):
         start = 0
         for k, ref in zip(direct_order(lax.axis_size("dp")), arrived):
             span = ref.shape[0]
-            rows = ref[...] if mine else from_core[start : start + span]
+            rows = from_core[start : start + span] if out else ref[...]
             start += span
             if k == 0:
-                groups.append((rows, place(0, 1, on)))
+                groups.append((rows, home(1, on)))
             else:
-                groups.append((rows[:pieces], place(k, on, on)))
-                groups.append((rows[pieces:], place(k, on, 1 - on)))
+                groups.append((rows[:pieces], [(out, (1 + k, on))]))
+                groups.append((rows[pieces:], [(out, (1 + k, 1 - on))]))
     return groups
 
 
@@ -249,13 +245,13 @@
     groups = []
     step = LANES // (CAP * PIECES)
     for b in range(0, sources, step):
-        groups += [(mine[n], n * CORES + core) for n in range(b, b + step)]
-        groups += [(other[n], n * CORES + 1 - core) for n in range(b, b + step)]
+        groups += [(mine[n], [(0, (n * CORES + core,))]) for n in range(b, b + step)]
+        groups += [(other[n], [(0, (n * CORES + 1 - core,))]) for n in range(b, b + step)]
     return groups
 
 
-def score_kernel(groups_of, stacked, inverse, counts, *refs):
-    back = refs[-1]
+def score_kernel(groups_of, outs, stacked, inverse, counts, *refs):
+    rows, back = refs[:-outs], refs[-outs:]
     per_task = TGT // TASKS
     half = PIECES // 2
     first = lax.axis_index("dp") * CAP
@@ -267,9 +263,9 @@
     per_block = CORES * LANES // pieces
     source = iota((per_block, LANES), 0)
     lane = iota((per_block, LANES), 1)
-    groups = groups_of(*refs[:-1])
+    groups = groups_of(*rows)
     for b in range(0, len(groups), per_block):
-        block = jnp.concatenate([rows for rows, _ in groups[b : b + per_block]], axis=0)
+        block = jnp.concatenate([part for part, _ in groups[b : b + per_block]], axis=0)
         whole = nt(stacked[...].reshape(PIECES * share, ROW), block)
         products = whole[:share]
         for n in range(1, PIECES):
@@ -293,15 +289,15 @@
             column = jnp.sum(jnp.where(at, table, 0.0), axis=1, keepdims=True)
             scores = jnp.where(iota(scores.shape, 1) == first + n, column, scores)
         for n in range(per_block):
-            back[groups[b + n][1]] = scores[n : n + 1]
+            for out, at in groups[b + n][1]:
+                back[out][at] = scores[n : n + 1]
 
 
 def finish_kernel(slots, strata_total, direct, picks, member, *refs):
     returned, out = refs[:-1], refs[-1]
     if direct:
-        d, x, core = (lax.axis_index(name) for name in ("dp", "x", "core"))
-        place = (d * lax.axis_size("x") + x) * CORES + core
-        values = jnp.concatenate([ref[place] for ref in returned], axis=0)
+        core = lax.axis_index("core")
+        values = jnp.concatenate([ref[core] for ref in returned], axis=0)
     else:
         values = returned[0][:, 0, :]
     raw = jnp.max(values, axis=0, keepdims=True)
@@ -333,15 +329,17 @@
     return pairs
 
 
-def direct_return(back, owners, columns, slots):
+def direct_return(mine, theirs, owners, columns, slots):
     def merge(a, b):
-        return jnp.where(iota(a.shape, 2) < slots, jnp.maximum(a, b), a + b)
-
-    chip = merge(back, lax.ppermute(back, "core", SWAP))
-    order = [3, 1, 2, 0] if owners == 4 else [1, 0]
-    got = [lax.ppermute(chip, ("dp", "x", "core"), direct_pairs(k, owners, columns)) for k in order]
+        return jnp.where(iota(a.shape, a.ndim - 1) < slots, jnp.maximum(a, b), a + b)
+
+    chip = merge(mine, lax.ppermute(theirs, "core", SWAP))
+    order = direct_order(owners)
+    got = [
+        lax.ppermute(chip[1 + k], ("dp", "x", "core"), direct_pairs(k, owners, columns)) for k in order
+    ]
     far = functools.reduce(merge, [part for k, part in zip(order, got) if k > 0])
-    return [chip, got[order.index(0)], far, lax.ppermute(far, "core", SWAP)]
+    return [chip[0], got[order.index(0)], far, lax.ppermute(far, "core", SWAP)]
 
 
 def direct_rows(payload, owners, columns, norms):
@@ -447,19 +445,20 @@
     else:
         mine = lax.all_to_all(payload, ("dp", "x"), split_axis=0, concat_axis=0, tiled=True)
         rows = [mine, lax.ppermute(mine, "core", SWAP)]
+    places_back = [(owners + 1, CORES)] * 2 if direct else [(chips * CORES,)]
     back = pl.pallas_call(
-        functools.partial(score_kernel, direct_groups if direct else gathered_groups),
-        out_shape=jax.ShapeDtypeStruct((chips * CORES, 1, lanes), f32),
+        functools.partial(score_kernel, direct_groups if direct else gathered_groups, len(places_back)),
+        out_shape=[jax.ShapeDtypeStruct((*place, 1, lanes), f32) for place in places_back],
         in_specs=[VMEM] * (3 + len(rows)),
-        out_specs=VMEM,
+        out_specs=[VMEM] * len(places_back),
         compiler_params=pltpu.CompilerParams(vmem_limit_bytes=40 * 2**20),
         name="score",
     )(stacked, inverse, counts, *rows)
     if direct:
-        returned = direct_return(back, owners, columns, slots)
+        returned = direct_return(*back, owners, columns, slots)
     else:
         returned = [
-            lax.all_to_all(back, ("dp", "x", "core"), split_axis=0, concat_axis=0, tiled=True)
+            lax.all_to_all(back[0], ("dp", "x", "core"), split_axis=0, concat_axis=0, tiled=True)
         ]
     return pl.pallas_call(
         functools.partial(finish_kernel, slots, strata_total, direct),

time: 31.4 us -> 30.9 us (0.984)
  starting transfers between devices: 15.1 us -> 14.1 us
  waiting for transfers between devices: 6.84 us -> 7.38 us
    ppermute x1, starting transfers between devices: 1.62 us -> 0.2 us  [direct_rows(): from_core = lax.ppermute(jnp.concatenate(arrived, axis=0), 'core', SWAP)]
    ppermute x4, waiting for transfers between devices: 1.14 us -> 1.96 us  [direct_rows(): lax.ppermute(rows, ('dp', 'x', 'core'), direct_pairs(k, owners, columns))]
    ppermute x6, waiting for transfers between devices: 3.61 us -> 3.09 us  [the longest x4 2.07 us: direct_return(): lax.ppermute(chip[1 + k], ('dp', 'x', 'core'), direct_pairs(k, owners, co...]
    ppermute x6, starting transfers between devices: 5.68 us -> 6.08 us  [the longest x4 5.79 us: direct_return(): lax.ppermute(chip[1 + k], ('dp', 'x', 'core'), direct_pairs(k, owners, co...]
  transfers between devices with their start and end apart: 12 -> 12, of which waited for: 8 -> 6; matrix products, arithmetic and copies ran while one was open for 0% -> 0% of each run, Pallas kernels for 7% -> 7%
where the time goes in v8:
time: 30.9 us; the launch traced here: 30.7 us
  starting transfers between devices  14.1 us (46%)
  Pallas kernels  8.49 us (27%)
  waiting for transfers between devices  7.38 us (24%)
  between operations  0.7 us (2%)
    ppermute x4, starting transfers between devices, direct_rows(): lax.ppermute(rows, ('dp', 'x', 'core'), direct_pairs(k, owners, columns))  7.22 us
    ppermute x4, starting transfers between devices, direct_return(): lax.ppermute(chip[1 + k], ('dp', 'x', 'core'), direct_pairs(k, owners, co...  5.79 us
    pallas_call x1, Pallas kernels, shards(): pl.pallas_call(functools.partial(project_kernel, places), out_shape=(jax....  4.45 us
    pallas_call x1, Pallas kernels, shards(): pl.pallas_call(functools.partial(norm_kernel, slots, direct), out_shape=(...  2.09 us
    ppermute x4, waiting for transfers between devices, direct_return(): lax.ppermute(chip[1 + k], ('dp', 'x', 'core'), direct_pairs(k, owners, co...  2.07 us
    ppermute x4, waiting for transfers between devices, direct_rows(): lax.ppermute(rows, ('dp', 'x', 'core'), direct_pairs(k, owners, columns))  1.96 us
    ppermute x1, waiting for transfers between devices, direct_rows(): from_core = lax.ppermute(jnp.concatenate(arrived, axis=0), 'core', SWAP)  1.35 us
    pallas_call x1, Pallas kernels, shards(): pl.pallas_call(functools.partial(score_kernel, direct_groups if direct el...  1.33 us
  transfers between devices with their start and end apart: 12, of which 6 were waited for; matrix products, arithmetic and copies ran while one was open for 0% of the time, Pallas kernels for 7%

profile of v8, /device:TPU:0, one launch (start us, length us, event | category | flops | bytes accessed | tf_op | source)
XLA Modules:
  0.0 30.7 jit_solution(13568269565337175442)
XLA Ops:
  0.0 4.5 %project.1 = (bf16[4,16,1024]{2,1,0:T(8,128)(2,1)S(1)}, f32[24,128]{1,0:T(8,128)S(1)}, f32[24,128]{1,0:T(8,128)S(1)}) custom-call(s32[24]{0:T(128)} %strata.1, s32[24]{0:T(128)} %keep.1, s32[32]{0:T(128)} %table.1, bf16[24,8,4096]{2,1,0:T(8,128)(2,1)} %bitcast.37, bf16[24,8,4096]{2,1,0:T(8,128)(2,1)} %bitcast.38, bf16[64,4096]{1,0:T(8,128)(2,1)} %bitcast.39, ...), custom_call_target="tpu_custom_call" | custom-call | tf_op jit(solution)/shard_map/project/pallas_call | solution.py:386
  4.5 0.6 %collective-permute-start = (bf16[4,16,1024]{2,1,0:T(8,128)(2,1)S(1)}, bf16[4,16,1024]{2,1,0:T(8,128)(2,1)S(1)}, u32[]{:S(2)}, u32[]{:S(2)}) collective-permute-start(bf16[4,16,1024]{2,1,0:T(8,128)(2,1)S(1)} %get-tuple-element.22.payload.refs_0_), channel_id=1, source_target_pairs={{0,1},{1,0},{2,3},{3,2},{4,5},{5,4},{6,7},{7,6},{8,9},{9,8},{10,11... | collective-permute-start | bytes 393224 | tf_op jit(solution)/shard_map/ppermute | solution.py:346
  5.1 1.0 %collective-permute-done.refs_1_ = bf16[4,16,1024]{2,1,0:T(8,128)(2,1)S(1)} collective-permute-done((bf16[4,16,1024]{2,1,0:T(8,128)(2,1)S(1)}, bf16[4,16,1024]{2,1,0:T(8,128)(2,1)S(1)}, u32[]{:S(2)}, u32[]{:S(2)}) %collective-permute-start) | collective-permute-done | bytes 131104 | tf_op jit(solution)/shard_map/ppermute | solution.py:346
  6.1 3.9 %collective-permute-start.1 = (bf16[32,1024]{1,0:T(8,128)(2,1)S(1)}, bf16[32,1024]{1,0:T(8,128)(2,1)S(1)}, u32[]{:S(2)}, u32[]{:S(2)}) collective-permute-start(bf16[32,1024]{1,0:T(8,128)(2,1)S(1)} %pad_maximum_fusion.1), channel_id=1, source_target_pairs={{0,8},{1,11},{2,10},{3,9},{4,12},{5,15},{6,14},{7,13},{8,0},{9,3},... | collective-permute-start | bytes 196616 | tf_op jit(solution)/shard_map/ppermute | solution.py:350
  10.0 1.6 %collective-permute-start.2 = (bf16[32,1024]{1,0:T(8,128)(2,1)S(1)}, bf16[32,1024]{1,0:T(8,128)(2,1)S(1)}, u32[]{:S(2)}, u32[]{:S(2)}) collective-permute-start(bf16[32,1024]{1,0:T(8,128)(2,1)S(1)} %pad_maximum_fusion.2), channel_id=1, source_target_pairs={{0,4},{1,7},{2,6},{3,5},{4,0},{5,3},{6,2},{7,1},{8,12},{9,15},{10,... | collective-permute-start | bytes 196616 | tf_op jit(solution)/shard_map/ppermute | solution.py:350
  11.6 0.0 collective-permute-start.4
  11.6 1.7 %collective-permute-start.3 = (bf16[16,1024]{1,0:T(8,128)(2,1)S(1)}, bf16[16,1024]{1,0:T(8,128)(2,1)S(1)}, u32[]{:S(2)}, u32[]{:S(2)}) collective-permute-start(bf16[16,1024]{1,0:T(8,128)(2,1)S(1)} %get-tuple-element.40), channel_id=1, source_target_pairs={{0,2},{1,3},{2,0},{3,1},{4,6},{5,7},{6,4},{7,5},{8,10},{9,11},{10,... | collective-permute-start | bytes 98312 | tf_op jit(solution)/shard_map/ppermute | solution.py:350
  13.9 2.1 %norms.1 = (bf16[8,192,1024]{2,1,0:T(8,128)(2,1)S(1)}, f32[192,128]{1,0:T(8,128)S(1)}, f32[24,128]{1,0:T(8,128)S(1)}, f32[8,128]{1,0:T(8,128)S(1)}) custom-call(s32[1]{0:T(128)S(6)} %copy.19.present, bf16[1,192,8192]{2,1,0:T(8,128)(2,1)} %targets.1, bf16[4,16,1024]{2,1,0:T(8,128)(2,1)S(1)} %get-tuple-element.22.payload.refs_0_, ...), custom_call_target="tpu_custom_call" | custom-call | flops 6291456 | bytes 6291456 | tf_op jit(solution)/shard_map/norms/pallas_call | solution.py:426
  16.0 0.0 collective-permute-done.3.refs_4_
  16.1 0.0 collective-permute-done.1.refs_2_
  16.1 0.0 collective-permute-done.2.refs_3_
  16.1 1.9 %collective-permute-done.4.refs_5_ = bf16[32,1024]{1,0:T(8,128)(2,1)S(1)} collective-permute-done((bf16[32,1024]{1,0:T(8,128)(2,1)S(1)}, bf16[32,1024]{1,0:T(8,128)(2,1)S(1)}, u32[]{:S(2)}, u32[]{:S(2)}) %collective-permute-start.4) | collective-permute-done | bytes 65568 | tf_op jit(solution)/shard_map/ppermute | solution.py:350
  18.0 0.2 collective-permute-start.5
  18.2 1.4 %collective-permute-done.5.refs_6_ = bf16[112,1024]{1,0:T(8,128)(2,1)S(1)} collective-permute-done((bf16[112,1024]{1,0:T(8,128)(2,1)S(1)}, bf16[112,1024]{1,0:T(8,128)(2,1)S(1)}, u32[]{:S(2)}, u32[]{:S(2)}) %collective-permute-start.5) | collective-permute-done | bytes 229408 | tf_op jit(solution)/shard_map/ppermute | solution.py:352
  19.6 1.3 %score.1 = (f32[5,2,1,128]{3,2,1,0:T(1,128)S(1)}, f32[5,2,1,128]{3,2,1,0:T(1,128)S(1)}) custom-call(bf16[8,192,1024]{2,1,0:T(8,128)(2,1)S(1)} %get-tuple-element.30.stacked, f32[192,128]{1,0:T(8,128)S(1)} %get-tuple-element.31.inverse, f32[8,128]{1,0:T(8,128)S(1)} %get-tuple-element.32.counts, bf16[4,16,1024]{2,1,0:T(8,128)(2,1)S(1)} %get-tuple-element.22.payload.refs_0_, ...), custom_call_target="tpu_custom_call" | custom-call | tf_op jit(solution)/shard_map/score/pallas_call | solution.py:449
  20.9 0.1 collective-permute-start.6
  21.1 1.0 %collective-permute-done.6 = f32[5,2,1,128]{3,1,2,0:T(2,128)S(1)} collective-permute-done((f32[5,2,1,128]{3,1,2,0:T(2,128)S(1)}, f32[5,2,1,128]{3,1,2,0:T(2,128)S(1)}, u32[]{:S(2)}, u32[]{:S(2)}) %collective-permute-start.6) | collective-permute-done | bytes 5152 | tf_op jit(solution)/shard_map/ppermute | solution.py:336
  22.1 2.2 %collective-permute-start.10 = (f32[2,1,128]{2,1,0:T(1,128)S(1)}, f32[2,1,128]{2,1,0:T(1,128)S(1)}, u32[]{:S(2)}, u32[]{:S(2)}) collective-permute-start(f32[2,1,128]{2,1,0:T(1,128)S(1)} %bitcast.43), channel_id=1, source_target_pairs={{0,12},{1,15},{2,14},{3,13},{4,8},{5,11},{6,10},{7,9},{8,4},{9,7},... | collective-permute-start | bytes 3080 | tf_op jit(solution)/shard_map/ppermute | solution.py:339
  24.3 0.0 collective-permute-start.8
  24.3 2.2 %collective-permute-start.9 = (f32[2,1,128]{2,1,0:T(1,128)S(1)}, f32[2,1,128]{2,1,0:T(1,128)S(1)}, u32[]{:S(2)}, u32[]{:S(2)}) collective-permute-start(f32[2,1,128]{2,1,0:T(1,128)S(1)} %bitcast.41), channel_id=1, source_target_pairs={{0,4},{1,7},{2,6},{3,5},{4,0},{5,3},{6,2},{7,1},{8,12},{9,15},{10,... | collective-permute-start | bytes 3080 | tf_op jit(solution)/shard_map/ppermute | solution.py:339
  26.5 1.3 %collective-permute-start.7 = (f32[2,1,128]{2,0,1:T(2,128)S(1)}, f32[2,1,128]{2,0,1:T(2,128)S(1)}, u32[]{:S(2)}, u32[]{:S(2)}) collective-permute-start(f32[2,1,128]{2,0,1:T(2,128)S(1)} %get-tuple-element.49), channel_id=1, source_target_pairs={{0,2},{1,3},{2,0},{3,1},{4,6},{5,7},{6,4},{7,5},{8,10},{9,11},{10,... | collective-permute-start | bytes 3080 | tf_op jit(solution)/shard_map/ppermute | solution.py:339
  27.9 0.0 collective-permute-done.10
  27.9 0.9 %collective-permute-done.8 = f32[2,1,128]{2,1,0:T(1,128)S(1)} collective-permute-done((f32[2,1,128]{2,1,0:T(1,128)S(1)}, f32[2,1,128]{2,1,0:T(1,128)S(1)}, u32[]{:S(2)}, u32[]{:S(2)}) %collective-permute-start.8) | collective-permute-done | bytes 1056 | tf_op jit(solution)/shard_map/ppermute | solution.py:339
  28.8 0.0 collective-permute-done.9
  28.8 0.1 collective-permute-start.11
  28.9 1.2 %collective-permute-done.7 = f32[2,1,128]{2,0,1:T(2,128)S(1)} collective-permute-done((f32[2,1,128]{2,0,1:T(2,128)S(1)}, f32[2,1,128]{2,0,1:T(2,128)S(1)}, u32[]{:S(2)}, u32[]{:S(2)}) %collective-permute-start.7) | collective-permute-done | bytes 1056 | tf_op jit(solution)/shard_map/ppermute | solution.py:339
  30.1 0.0 collective-permute-done.11.refs_3_
  30.1 0.6 %finish.1 = f32[24]{0:T(128)} custom-call(f32[24,128]{1,0:T(8,128)S(1)} %get-tuple-element.29.picks, f32[24,128]{1,0:T(8,128)S(1)} %get-tuple-element.24.member, f32[2,1,128]{2,1,0:T(1,128)S(1)} %bitcast.34, f32[2,1,128]{2,1,0:T(1,128)S(1)} %bitcast.35, f32[2,1,128]{2,1,0:T(1,128)S(1)} %broadcast_select_fusion.refs_2_, ...), custom_call_target="tpu_custom_call" | custom-call | tf_op jit(solution)/shard_map/finish/pallas_call | solution.py:463
  (10 shorter events, 0.1 us)
Async XLA Ops:
  4.5 1.6 %collective-permute-start = (bf16[4,16,1024]{2,1,0:T(8,128)(2,1)S(1)}, bf16[4,16,1024]{2,1,0:T(8,128)(2,1)S(1)}, u32[]{:S(2)}, u32[]{:S(2)}) collective-permute-start(bf16[4,16,1024]{2,1,0:T(8,128)(2,1)S(1)} %get-tuple-element.22.payload.refs_0_), channel_id=1, source_target_pairs={{0,1},{1,0},{2,3},{3,2},{4,5},{5,4},{6,7},{7,6},{8,9},{9,8},{10,11... | collective-permute-start | bytes 393224 | tf_op jit(solution)/shard_map/ppermute | solution.py:346
  6.1 10.0 %collective-permute-start.1 = (bf16[32,1024]{1,0:T(8,128)(2,1)S(1)}, bf16[32,1024]{1,0:T(8,128)(2,1)S(1)}, u32[]{:S(2)}, u32[]{:S(2)}) collective-permute-start(bf16[32,1024]{1,0:T(8,128)(2,1)S(1)} %pad_maximum_fusion.1), channel_id=1, source_target_pairs={{0,8},{1,11},{2,10},{3,9},{4,12},{5,15},{6,14},{7,13},{8,0},{9,3},... | collective-permute-start | bytes 196616 | tf_op jit(solution)/shard_map/ppermute | solution.py:350
  10.0 6.1 %collective-permute-start.2 = (bf16[32,1024]{1,0:T(8,128)(2,1)S(1)}, bf16[32,1024]{1,0:T(8,128)(2,1)S(1)}, u32[]{:S(2)}, u32[]{:S(2)}) collective-permute-start(bf16[32,1024]{1,0:T(8,128)(2,1)S(1)} %pad_maximum_fusion.2), channel_id=1, source_target_pairs={{0,4},{1,7},{2,6},{3,5},{4,0},{5,3},{6,2},{7,1},{8,12},{9,15},{10,... | collective-permute-start | bytes 196616 | tf_op jit(solution)/shard_map/ppermute | solution.py:350
  11.6 6.4 %collective-permute-start.4 = (bf16[32,1024]{1,0:T(8,128)(2,1)S(1)}, bf16[32,1024]{1,0:T(8,128)(2,1)S(1)}, u32[]{:S(2)}, u32[]{:S(2)}) collective-permute-start(bf16[32,1024]{1,0:T(8,128)(2,1)S(1)} %pad_maximum_fusion.3), channel_id=1, source_target_pairs={{0,12},{1,15},{2,14},{3,13},{4,8},{5,11},{6,10},{7,9},{8,4},{9,7},... | collective-permute-start | bytes 196616 | tf_op jit(solution)/shard_map/ppermute | solution.py:350
  11.6 4.5 %collective-permute-start.3 = (bf16[16,1024]{1,0:T(8,128)(2,1)S(1)}, bf16[16,1024]{1,0:T(8,128)(2,1)S(1)}, u32[]{:S(2)}, u32[]{:S(2)}) collective-permute-start(bf16[16,1024]{1,0:T(8,128)(2,1)S(1)} %get-tuple-element.40), channel_id=1, source_target_pairs={{0,2},{1,3},{2,0},{3,1},{4,6},{5,7},{6,4},{7,5},{8,10},{9,11},{10,... | collective-permute-start | bytes 98312 | tf_op jit(solution)/shard_map/ppermute | solution.py:350
  18.0 1.6 %collective-permute-start.5 = (bf16[112,1024]{1,0:T(8,128)(2,1)S(1)}, bf16[112,1024]{1,0:T(8,128)(2,1)S(1)}, u32[]{:S(2)}, u32[]{:S(2)}) collective-permute-start(bf16[112,1024]{1,0:T(8,128)(2,1)S(1)} %pad_maximum_fusion), channel_id=1, source_target_pairs={{0,1},{1,0},{2,3},{3,2},{4,5},{5,4},{6,7},{7,6},{8,9},{9,8},{10,11... | collective-permute-start | bytes 688136 | tf_op jit(solution)/shard_map/ppermute | solution.py:352
  20.9 1.2 %collective-permute-start.6 = (f32[5,2,1,128]{3,1,2,0:T(2,128)S(1)}, f32[5,2,1,128]{3,1,2,0:T(2,128)S(1)}, u32[]{:S(2)}, u32[]{:S(2)}) collective-permute-start(f32[5,2,1,128]{3,1,2,0:T(2,128)S(1)} %bitcast.36), channel_id=1, source_target_pairs={{0,1},{1,0},{2,3},{3,2},{4,5},{5,4},{6,7},{7,6},{8,9},{9,8},{10,11... | collective-permute-start | bytes 15368 | tf_op jit(solution)/shard_map/ppermute | solution.py:336
  22.1 5.8 %collective-permute-start.10 = (f32[2,1,128]{2,1,0:T(1,128)S(1)}, f32[2,1,128]{2,1,0:T(1,128)S(1)}, u32[]{:S(2)}, u32[]{:S(2)}) collective-permute-start(f32[2,1,128]{2,1,0:T(1,128)S(1)} %bitcast.43), channel_id=1, source_target_pairs={{0,12},{1,15},{2,14},{3,13},{4,8},{5,11},{6,10},{7,9},{8,4},{9,7},... | collective-permute-start | bytes 3080 | tf_op jit(solution)/shard_map/ppermute | solution.py:339
  24.3 4.5 %collective-permute-start.8 = (f32[2,1,128]{2,1,0:T(1,128)S(1)}, f32[2,1,128]{2,1,0:T(1,128)S(1)}, u32[]{:S(2)}, u32[]{:S(2)}) collective-permute-start(f32[2,1,128]{2,1,0:T(1,128)S(1)} %bitcast.42), channel_id=1, source_target_pairs={{0,8},{1,11},{2,10},{3,9},{4,12},{5,15},{6,14},{7,13},{8,0},{9,3},... | collective-permute-start | bytes 3080 | tf_op jit(solution)/shard_map/ppermute | solution.py:339
  24.3 4.5 %collective-permute-start.9 = (f32[2,1,128]{2,1,0:T(1,128)S(1)}, f32[2,1,128]{2,1,0:T(1,128)S(1)}, u32[]{:S(2)}, u32[]{:S(2)}) collective-permute-start(f32[2,1,128]{2,1,0:T(1,128)S(1)} %bitcast.41), channel_id=1, source_target_pairs={{0,4},{1,7},{2,6},{3,5},{4,0},{5,3},{6,2},{7,1},{8,12},{9,15},{10,... | collective-permute-start | bytes 3080 | tf_op jit(solution)/shard_map/ppermute | solution.py:339
  26.5 3.6 %collective-permute-start.7 = (f32[2,1,128]{2,0,1:T(2,128)S(1)}, f32[2,1,128]{2,0,1:T(2,128)S(1)}, u32[]{:S(2)}, u32[]{:S(2)}) collective-permute-start(f32[2,1,128]{2,0,1:T(2,128)S(1)} %get-tuple-element.49), channel_id=1, source_target_pairs={{0,2},{1,3},{2,0},{3,1},{4,6},{5,7},{6,4},{7,5},{8,10},{9,11},{10,... | collective-permute-start | bytes 3080 | tf_op jit(solution)/shard_map/ppermute | solution.py:339
  28.8 1.3 %collective-permute-start.11 = (f32[2,1,128]{2,1,0:T(1,128)S(1)}, f32[2,1,128]{2,1,0:T(1,128)S(1)}, u32[]{:S(2)}, u32[]{:S(2)}) collective-permute-start(f32[2,1,128]{2,1,0:T(1,128)S(1)} %broadcast_select_fusion.refs_2_), channel_id=1, source_target_pairs={{0,1},{1,0},{2,3},{3,2},{4,5},{5,4},{6,7},{7,6},{8,9},{9,8},{10,11... | collective-permute-start | bytes 3080 | tf_op jit(solution)/shard_map/ppermute | solution.py:342

commit v9 on v8

--- a/solution.py
+++ b/solution.py
@@ -142,7 +142,10 @@
             if g == 0:
                 weights[3 + n].wait()
             span = pl.ds(n * depth, depth)
-            part = nn(both(n * depth, depth), width_v[span, :])
+            lines_in = both(n * depth, depth)
+            part = jnp.concatenate(
+                [nn(lines_in, width_v[span, m : m + wide // 2]) for m in (0, wide // 2)], axis=1
+            )
             projected = part if n == 0 else projected + part
             if n == 0:
                 adapted = nn(both(0, model), adapters_t[...])

time: 30.9 us -> 30.7 us (level)
  waiting for transfers between devices: 7.38 us -> 6.79 us
  starting transfers between devices: 14.1 us -> 14.5 us
    ppermute x4, waiting for transfers between devices: 2.07 us -> 1.63 us  [direct_return(): lax.ppermute(chip[1 + k], ('dp', 'x', 'core'), direct_pairs(k, owners, co...]
  transfers between devices with their start and end apart: 12 -> 12, of which waited for: 6 -> 7; matrix products, arithmetic and copies ran while one was open for 0% -> 0% of each run, Pallas kernels for 7% -> 7%
where the time goes in v9:
time: 30.7 us; the launch traced here: 30.5 us
  starting transfers between devices  14.5 us (47%)
  Pallas kernels  8.39 us (27%)
  waiting for transfers between devices  6.79 us (22%)
  between operations  0.7 us (2%)
    ppermute x4, starting transfers between devices, direct_rows(): lax.ppermute(rows, ('dp', 'x', 'core'), direct_pairs(k, owners, columns))  7.22 us
    ppermute x4, starting transfers between devices, direct_return(): lax.ppermute(chip[1 + k], ('dp', 'x', 'core'), direct_pairs(k, owners, co...  5.93 us
    pallas_call x1, Pallas kernels, shards(): pl.pallas_call(functools.partial(project_kernel, places), out_shape=(jax....  4.34 us
    pallas_call x1, Pallas kernels, shards(): pl.pallas_call(functools.partial(norm_kernel, slots, direct), out_shape=(...  2.09 us
    ppermute x4, waiting for transfers between devices, direct_rows(): lax.ppermute(rows, ('dp', 'x', 'core'), direct_pairs(k, owners, columns))  1.78 us
    ppermute x4, waiting for transfers between devices, direct_return(): lax.ppermute(chip[1 + k], ('dp', 'x', 'core'), direct_pairs(k, owners, co...  1.63 us
    ppermute x1, waiting for transfers between devices, direct_rows(): from_core = lax.ppermute(jnp.concatenate(arrived, axis=0), 'core', SWAP)  1.36 us
    pallas_call x1, Pallas kernels, shards(): pl.pallas_call(functools.partial(score_kernel, direct_groups if direct el...  1.35 us
  transfers between devices with their start and end apart: 12, of which 7 were waited for; matrix products, arithmetic and copies ran while one was open for 0% of the time, Pallas kernels for 7%

profile of v9, /device:TPU:0, one launch (start us, length us, event | category | flops | bytes accessed | tf_op | source)
XLA Modules:
  0.0 30.5 jit_solution(14313694510162017466)
XLA Ops:
  0.0 4.3 %project.1 = (bf16[4,16,1024]{2,1,0:T(8,128)(2,1)S(1)}, f32[24,128]{1,0:T(8,128)S(1)}, f32[24,128]{1,0:T(8,128)S(1)}) custom-call(s32[24]{0:T(128)} %strata.1, s32[24]{0:T(128)} %keep.1, s32[32]{0:T(128)} %table.1, bf16[24,8,4096]{2,1,0:T(8,128)(2,1)} %bitcast.37, bf16[24,8,4096]{2,1,0:T(8,128)(2,1)} %bitcast.38, bf16[64,4096]{1,0:T(8,128)(2,1)} %bitcast.39, ...), custom_call_target="tpu_custom_call" | custom-call | tf_op jit(solution)/shard_map/project/pallas_call | solution.py:389
  4.3 0.6 %collective-permute-start = (bf16[4,16,1024]{2,1,0:T(8,128)(2,1)S(1)}, bf16[4,16,1024]{2,1,0:T(8,128)(2,1)S(1)}, u32[]{:S(2)}, u32[]{:S(2)}) collective-permute-start(bf16[4,16,1024]{2,1,0:T(8,128)(2,1)S(1)} %get-tuple-element.22.payload.refs_0_), channel_id=1, source_target_pairs={{0,1},{1,0},{2,3},{3,2},{4,5},{5,4},{6,7},{7,6},{8,9},{9,8},{10,11... | collective-permute-start | bytes 393224 | tf_op jit(solution)/shard_map/ppermute | solution.py:349
  5.0 1.0 %collective-permute-done.refs_1_ = bf16[4,16,1024]{2,1,0:T(8,128)(2,1)S(1)} collective-permute-done((bf16[4,16,1024]{2,1,0:T(8,128)(2,1)S(1)}, bf16[4,16,1024]{2,1,0:T(8,128)(2,1)S(1)}, u32[]{:S(2)}, u32[]{:S(2)}) %collective-permute-start) | collective-permute-done | bytes 131104 | tf_op jit(solution)/shard_map/ppermute | solution.py:349
  6.0 4.0 %collective-permute-start.1 = (bf16[32,1024]{1,0:T(8,128)(2,1)S(1)}, bf16[32,1024]{1,0:T(8,128)(2,1)S(1)}, u32[]{:S(2)}, u32[]{:S(2)}) collective-permute-start(bf16[32,1024]{1,0:T(8,128)(2,1)S(1)} %pad_maximum_fusion.1), channel_id=1, source_target_pairs={{0,8},{1,11},{2,10},{3,9},{4,12},{5,15},{6,14},{7,13},{8,0},{9,3},... | collective-permute-start | bytes 196616 | tf_op jit(solution)/shard_map/ppermute | solution.py:353
  10.0 1.5 %collective-permute-start.2 = (bf16[32,1024]{1,0:T(8,128)(2,1)S(1)}, bf16[32,1024]{1,0:T(8,128)(2,1)S(1)}, u32[]{:S(2)}, u32[]{:S(2)}) collective-permute-start(bf16[32,1024]{1,0:T(8,128)(2,1)S(1)} %pad_maximum_fusion.2), channel_id=1, source_target_pairs={{0,4},{1,7},{2,6},{3,5},{4,0},{5,3},{6,2},{7,1},{8,12},{9,15},{10,... | collective-permute-start | bytes 196616 | tf_op jit(solution)/shard_map/ppermute | solution.py:353
  11.5 0.1 collective-permute-start.4
  11.6 1.6 %collective-permute-start.3 = (bf16[16,1024]{1,0:T(8,128)(2,1)S(1)}, bf16[16,1024]{1,0:T(8,128)(2,1)S(1)}, u32[]{:S(2)}, u32[]{:S(2)}) collective-permute-start(bf16[16,1024]{1,0:T(8,128)(2,1)S(1)} %get-tuple-element.40), channel_id=1, source_target_pairs={{0,2},{1,3},{2,0},{3,1},{4,6},{5,7},{6,4},{7,5},{8,10},{9,11},{10,... | collective-permute-start | bytes 98312 | tf_op jit(solution)/shard_map/ppermute | solution.py:353
  13.8 2.1 %norms.1 = (bf16[8,192,1024]{2,1,0:T(8,128)(2,1)S(1)}, f32[192,128]{1,0:T(8,128)S(1)}, f32[24,128]{1,0:T(8,128)S(1)}, f32[8,128]{1,0:T(8,128)S(1)}) custom-call(s32[1]{0:T(128)S(6)} %copy.19.present, bf16[1,192,8192]{2,1,0:T(8,128)(2,1)} %targets.1, bf16[4,16,1024]{2,1,0:T(8,128)(2,1)S(1)} %get-tuple-element.22.payload.refs_0_, ...), custom_call_target="tpu_custom_call" | custom-call | flops 6291456 | bytes 6291456 | tf_op jit(solution)/shard_map/norms/pallas_call | solution.py:429
  15.9 0.1 collective-permute-done.3.refs_4_
  16.0 0.0 collective-permute-done.1.refs_2_
  16.0 0.0 collective-permute-done.2.refs_3_
  16.0 1.7 %collective-permute-done.4.refs_5_ = bf16[32,1024]{1,0:T(8,128)(2,1)S(1)} collective-permute-done((bf16[32,1024]{1,0:T(8,128)(2,1)S(1)}, bf16[32,1024]{1,0:T(8,128)(2,1)S(1)}, u32[]{:S(2)}, u32[]{:S(2)}) %collective-permute-start.4) | collective-permute-done | bytes 65568 | tf_op jit(solution)/shard_map/ppermute | solution.py:353
  17.7 0.2 collective-permute-start.5
  17.9 1.4 %collective-permute-done.5.refs_6_ = bf16[112,1024]{1,0:T(8,128)(2,1)S(1)} collective-permute-done((bf16[112,1024]{1,0:T(8,128)(2,1)S(1)}, bf16[112,1024]{1,0:T(8,128)(2,1)S(1)}, u32[]{:S(2)}, u32[]{:S(2)}) %collective-permute-start.5) | collective-permute-done | bytes 229408 | tf_op jit(solution)/shard_map/ppermute | solution.py:355
  19.3 1.3 %score.1 = (f32[5,2,1,128]{3,2,1,0:T(1,128)S(1)}, f32[5,2,1,128]{3,2,1,0:T(1,128)S(1)}) custom-call(bf16[8,192,1024]{2,1,0:T(8,128)(2,1)S(1)} %get-tuple-element.30.stacked, f32[192,128]{1,0:T(8,128)S(1)} %get-tuple-element.31.inverse, f32[8,128]{1,0:T(8,128)S(1)} %get-tuple-element.32.counts, bf16[4,16,1024]{2,1,0:T(8,128)(2,1)S(1)} %get-tuple-element.22.payload.refs_0_, ...), custom_call_target="tpu_custom_call" | custom-call | tf_op jit(solution)/shard_map/score/pallas_call | solution.py:452
  20.6 0.1 collective-permute-start.6
  20.8 1.0 %collective-permute-done.6 = f32[5,2,1,128]{3,1,2,0:T(2,128)S(1)} collective-permute-done((f32[5,2,1,128]{3,1,2,0:T(2,128)S(1)}, f32[5,2,1,128]{3,1,2,0:T(2,128)S(1)}, u32[]{:S(2)}, u32[]{:S(2)}) %collective-permute-start.6) | collective-permute-done | bytes 5152 | tf_op jit(solution)/shard_map/ppermute | solution.py:339
  21.8 2.2 %collective-permute-start.10 = (f32[2,1,128]{2,1,0:T(1,128)S(1)}, f32[2,1,128]{2,1,0:T(1,128)S(1)}, u32[]{:S(2)}, u32[]{:S(2)}) collective-permute-start(f32[2,1,128]{2,1,0:T(1,128)S(1)} %bitcast.43), channel_id=1, source_target_pairs={{0,12},{1,15},{2,14},{3,13},{4,8},{5,11},{6,10},{7,9},{8,4},{9,7},... | collective-permute-start | bytes 3080 | tf_op jit(solution)/shard_map/ppermute | solution.py:342
  24.0 0.3 collective-permute-start.8
  24.3 2.0 %collective-permute-start.9 = (f32[2,1,128]{2,1,0:T(1,128)S(1)}, f32[2,1,128]{2,1,0:T(1,128)S(1)}, u32[]{:S(2)}, u32[]{:S(2)}) collective-permute-start(f32[2,1,128]{2,1,0:T(1,128)S(1)} %bitcast.41), channel_id=1, source_target_pairs={{0,4},{1,7},{2,6},{3,5},{4,0},{5,3},{6,2},{7,1},{8,12},{9,15},{10,... | collective-permute-start | bytes 3080 | tf_op jit(solution)/shard_map/ppermute | solution.py:342
  26.3 1.5 %collective-permute-start.7 = (f32[2,1,128]{2,0,1:T(2,128)S(1)}, f32[2,1,128]{2,0,1:T(2,128)S(1)}, u32[]{:S(2)}, u32[]{:S(2)}) collective-permute-start(f32[2,1,128]{2,0,1:T(2,128)S(1)} %get-tuple-element.49), channel_id=1, source_target_pairs={{0,2},{1,3},{2,0},{3,1},{4,6},{5,7},{6,4},{7,5},{8,10},{9,11},{10,... | collective-permute-start | bytes 3080 | tf_op jit(solution)/shard_map/ppermute | solution.py:342
  27.8 0.0 collective-permute-done.10
  27.8 0.7 %collective-permute-done.8 = f32[2,1,128]{2,1,0:T(1,128)S(1)} collective-permute-done((f32[2,1,128]{2,1,0:T(1,128)S(1)}, f32[2,1,128]{2,1,0:T(1,128)S(1)}, u32[]{:S(2)}, u32[]{:S(2)}) %collective-permute-start.8) | collective-permute-done | bytes 1056 | tf_op jit(solution)/shard_map/ppermute | solution.py:342
  28.5 0.0 collective-permute-done.9
  28.5 0.4 %collective-permute-start.11 = (f32[2,1,128]{2,1,0:T(1,128)S(1)}, f32[2,1,128]{2,1,0:T(1,128)S(1)}, u32[]{:S(2)}, u32[]{:S(2)}) collective-permute-start(f32[2,1,128]{2,1,0:T(1,128)S(1)} %broadcast_select_fusion.refs_2_), channel_id=1, source_target_pairs={{0,1},{1,0},{2,3},{3,2},{4,5},{5,4},{6,7},{7,6},{8,9},{9,8},{10,11... | collective-permute-start | bytes 3080 | tf_op jit(solution)/shard_map/ppermute | solution.py:345
  28.9 0.9 %collective-permute-done.7 = f32[2,1,128]{2,0,1:T(2,128)S(1)} collective-permute-done((f32[2,1,128]{2,0,1:T(2,128)S(1)}, f32[2,1,128]{2,0,1:T(2,128)S(1)}, u32[]{:S(2)}, u32[]{:S(2)}) %collective-permute-start.7) | collective-permute-done | bytes 1056 | tf_op jit(solution)/shard_map/ppermute | solution.py:342
  29.8 0.0 collective-permute-done.11.refs_3_
  29.9 0.6 %finish.1 = f32[24]{0:T(128)} custom-call(f32[24,128]{1,0:T(8,128)S(1)} %get-tuple-element.29.picks, f32[24,128]{1,0:T(8,128)S(1)} %get-tuple-element.24.member, f32[2,1,128]{2,1,0:T(1,128)S(1)} %bitcast.34, f32[2,1,128]{2,1,0:T(1,128)S(1)} %bitcast.35, f32[2,1,128]{2,1,0:T(1,128)S(1)} %broadcast_select_fusion.refs_2_, ...), custom_call_target="tpu_custom_call" | custom-call | tf_op jit(solution)/shard_map/finish/pallas_call | solution.py:466
  (10 shorter events, 0.1 us)
Async XLA Ops:
  4.3 1.6 %collective-permute-start = (bf16[4,16,1024]{2,1,0:T(8,128)(2,1)S(1)}, bf16[4,16,1024]{2,1,0:T(8,128)(2,1)S(1)}, u32[]{:S(2)}, u32[]{:S(2)}) collective-permute-start(bf16[4,16,1024]{2,1,0:T(8,128)(2,1)S(1)} %get-tuple-element.22.payload.refs_0_), channel_id=1, source_target_pairs={{0,1},{1,0},{2,3},{3,2},{4,5},{5,4},{6,7},{7,6},{8,9},{9,8},{10,11... | collective-permute-start | bytes 393224 | tf_op jit(solution)/shard_map/ppermute | solution.py:349
  6.0 10.0 %collective-permute-start.1 = (bf16[32,1024]{1,0:T(8,128)(2,1)S(1)}, bf16[32,1024]{1,0:T(8,128)(2,1)S(1)}, u32[]{:S(2)}, u32[]{:S(2)}) collective-permute-start(bf16[32,1024]{1,0:T(8,128)(2,1)S(1)} %pad_maximum_fusion.1), channel_id=1, source_target_pairs={{0,8},{1,11},{2,10},{3,9},{4,12},{5,15},{6,14},{7,13},{8,0},{9,3},... | collective-permute-start | bytes 196616 | tf_op jit(solution)/shard_map/ppermute | solution.py:353
  10.0 6.0 %collective-permute-start.2 = (bf16[32,1024]{1,0:T(8,128)(2,1)S(1)}, bf16[32,1024]{1,0:T(8,128)(2,1)S(1)}, u32[]{:S(2)}, u32[]{:S(2)}) collective-permute-start(bf16[32,1024]{1,0:T(8,128)(2,1)S(1)} %pad_maximum_fusion.2), channel_id=1, source_target_pairs={{0,4},{1,7},{2,6},{3,5},{4,0},{5,3},{6,2},{7,1},{8,12},{9,15},{10,... | collective-permute-start | bytes 196616 | tf_op jit(solution)/shard_map/ppermute | solution.py:353
  11.5 6.3 %collective-permute-start.4 = (bf16[32,1024]{1,0:T(8,128)(2,1)S(1)}, bf16[32,1024]{1,0:T(8,128)(2,1)S(1)}, u32[]{:S(2)}, u32[]{:S(2)}) collective-permute-start(bf16[32,1024]{1,0:T(8,128)(2,1)S(1)} %pad_maximum_fusion.3), channel_id=1, source_target_pairs={{0,12},{1,15},{2,14},{3,13},{4,8},{5,11},{6,10},{7,9},{8,4},{9,7},... | collective-permute-start | bytes 196616 | tf_op jit(solution)/shard_map/ppermute | solution.py:353
  11.6 4.4 %collective-permute-start.3 = (bf16[16,1024]{1,0:T(8,128)(2,1)S(1)}, bf16[16,1024]{1,0:T(8,128)(2,1)S(1)}, u32[]{:S(2)}, u32[]{:S(2)}) collective-permute-start(bf16[16,1024]{1,0:T(8,128)(2,1)S(1)} %get-tuple-element.40), channel_id=1, source_target_pairs={{0,2},{1,3},{2,0},{3,1},{4,6},{5,7},{6,4},{7,5},{8,10},{9,11},{10,... | collective-permute-start | bytes 98312 | tf_op jit(solution)/shard_map/ppermute | solution.py:353
  17.7 1.6 %collective-permute-start.5 = (bf16[112,1024]{1,0:T(8,128)(2,1)S(1)}, bf16[112,1024]{1,0:T(8,128)(2,1)S(1)}, u32[]{:S(2)}, u32[]{:S(2)}) collective-permute-start(bf16[112,1024]{1,0:T(8,128)(2,1)S(1)} %pad_maximum_fusion), channel_id=1, source_target_pairs={{0,1},{1,0},{2,3},{3,2},{4,5},{5,4},{6,7},{7,6},{8,9},{9,8},{10,11... | collective-permute-start | bytes 688136 | tf_op jit(solution)/shard_map/ppermute | solution.py:355
  20.6 1.2 %collective-permute-start.6 = (f32[5,2,1,128]{3,1,2,0:T(2,128)S(1)}, f32[5,2,1,128]{3,1,2,0:T(2,128)S(1)}, u32[]{:S(2)}, u32[]{:S(2)}) collective-permute-start(f32[5,2,1,128]{3,1,2,0:T(2,128)S(1)} %bitcast.36), channel_id=1, source_target_pairs={{0,1},{1,0},{2,3},{3,2},{4,5},{5,4},{6,7},{7,6},{8,9},{9,8},{10,11... | collective-permute-start | bytes 15368 | tf_op jit(solution)/shard_map/ppermute | solution.py:339
  21.8 5.9 %collective-permute-start.10 = (f32[2,1,128]{2,1,0:T(1,128)S(1)}, f32[2,1,128]{2,1,0:T(1,128)S(1)}, u32[]{:S(2)}, u32[]{:S(2)}) collective-permute-start(f32[2,1,128]{2,1,0:T(1,128)S(1)} %bitcast.43), channel_id=1, source_target_pairs={{0,12},{1,15},{2,14},{3,13},{4,8},{5,11},{6,10},{7,9},{8,4},{9,7},... | collective-permute-start | bytes 3080 | tf_op jit(solution)/shard_map/ppermute | solution.py:342
  24.0 4.5 %collective-permute-start.8 = (f32[2,1,128]{2,1,0:T(1,128)S(1)}, f32[2,1,128]{2,1,0:T(1,128)S(1)}, u32[]{:S(2)}, u32[]{:S(2)}) collective-permute-start(f32[2,1,128]{2,1,0:T(1,128)S(1)} %bitcast.42), channel_id=1, source_target_pairs={{0,8},{1,11},{2,10},{3,9},{4,12},{5,15},{6,14},{7,13},{8,0},{9,3},... | collective-permute-start | bytes 3080 | tf_op jit(solution)/shard_map/ppermute | solution.py:342
  24.3 4.2 %collective-permute-start.9 = (f32[2,1,128]{2,1,0:T(1,128)S(1)}, f32[2,1,128]{2,1,0:T(1,128)S(1)}, u32[]{:S(2)}, u32[]{:S(2)}) collective-permute-start(f32[2,1,128]{2,1,0:T(1,128)S(1)} %bitcast.41), channel_id=1, source_target_pairs={{0,4},{1,7},{2,6},{3,5},{4,0},{5,3},{6,2},{7,1},{8,12},{9,15},{10,... | collective-permute-start | bytes 3080 | tf_op jit(solution)/shard_map/ppermute | solution.py:342
  26.3 3.6 %collective-permute-start.7 = (f32[2,1,128]{2,0,1:T(2,128)S(1)}, f32[2,1,128]{2,0,1:T(2,128)S(1)}, u32[]{:S(2)}, u32[]{:S(2)}) collective-permute-start(f32[2,1,128]{2,0,1:T(2,128)S(1)} %get-tuple-element.49), channel_id=1, source_target_pairs={{0,2},{1,3},{2,0},{3,1},{4,6},{5,7},{6,4},{7,5},{8,10},{9,11},{10,... | collective-permute-start | bytes 3080 | tf_op jit(solution)/shard_map/ppermute | solution.py:342
  28.5 1.4 %collective-permute-start.11 = (f32[2,1,128]{2,1,0:T(1,128)S(1)}, f32[2,1,128]{2,1,0:T(1,128)S(1)}, u32[]{:S(2)}, u32[]{:S(2)}) collective-permute-start(f32[2,1,128]{2,1,0:T(1,128)S(1)} %broadcast_select_fusion.refs_2_), channel_id=1, source_target_pairs={{0,1},{1,0},{2,3},{3,2},{4,5},{5,4},{6,7},{7,6},{8,9},{9,8},{10,11... | collective-permute-start | bytes 3080 | tf_op jit(solution)/shard_map/ppermute | solution.py:345

commit v10 on v9

--- a/solution.py
+++ b/solution.py
@@ -337,7 +337,7 @@
         return jnp.where(iota(a.shape, a.ndim - 1) < slots, jnp.maximum(a, b), a + b)
 
     chip = merge(mine, lax.ppermute(theirs, "core", SWAP))
-    order = direct_order(owners)
+    order = [2, 0, 1, 3] if owners == 4 else direct_order(owners)
     got = [
         lax.ppermute(chip[1 + k], ("dp", "x", "core"), direct_pairs(k, owners, columns)) for k in order
     ]

time: 30.7 us -> 30.7 us (level)
  waiting for transfers between devices: 6.79 us -> 7.35 us
  starting transfers between devices: 14.5 us -> 14.1 us
    ppermute x4, waiting for transfers between devices: 1.63 us -> 2.06 us  [direct_return(): lax.ppermute(chip[1 + k], ('dp', 'x', 'core'), direct_pairs(k, owners, co...]
  transfers between devices with their start and end apart: 12 -> 12, of which waited for: 7 -> 6; matrix products, arithmetic and copies ran while one was open for 0% -> 0% of each run, Pallas kernels for 7% -> 7%
where the time goes in v10:
time: 30.7 us; the launch traced here: 30.6 us
  starting transfers between devices  14.1 us (46%)
  Pallas kernels  8.37 us (27%)
  waiting for transfers between devices  7.35 us (24%)
  between operations  0.7 us (2%)
    ppermute x4, starting transfers between devices, direct_rows(): lax.ppermute(rows, ('dp', 'x', 'core'), direct_pairs(k, owners, columns))  7.3 us
    ppermute x4, starting transfers between devices, direct_return(): lax.ppermute(chip[1 + k], ('dp', 'x', 'core'), direct_pairs(k, owners, co...  5.8 us
    pallas_call x1, Pallas kernels, shards(): pl.pallas_call(functools.partial(project_kernel, places), out_shape=(jax....  4.34 us
    pallas_call x1, Pallas kernels, shards(): pl.pallas_call(functools.partial(norm_kernel, slots, direct), out_shape=(...  2.09 us
    ppermute x4, waiting for transfers between devices, direct_return(): lax.ppermute(chip[1 + k], ('dp', 'x', 'core'), direct_pairs(k, owners, co...  2.06 us
    ppermute x4, waiting for transfers between devices, direct_rows(): lax.ppermute(rows, ('dp', 'x', 'core'), direct_pairs(k, owners, columns))  1.93 us
    ppermute x1, waiting for transfers between devices, direct_rows(): from_core = lax.ppermute(jnp.concatenate(arrived, axis=0), 'core', SWAP)  1.36 us
    pallas_call x1, Pallas kernels, shards(): pl.pallas_call(functools.partial(score_kernel, direct_groups if direct el...  1.33 us
  transfers between devices with their start and end apart: 12, of which 6 were waited for; matrix products, arithmetic and copies ran while one was open for 0% of the time, Pallas kernels for 7%

profile of v10, /device:TPU:0, one launch (start us, length us, event | category | flops | bytes accessed | tf_op | source)
XLA Modules:
  0.0 30.6 jit_solution(14313694510162017466)
XLA Ops:
  0.0 4.3 %project.1 = (bf16[4,16,1024]{2,1,0:T(8,128)(2,1)S(1)}, f32[24,128]{1,0:T(8,128)S(1)}, f32[24,128]{1,0:T(8,128)S(1)}) custom-call(s32[24]{0:T(128)} %strata.1, s32[24]{0:T(128)} %keep.1, s32[32]{0:T(128)} %table.1, bf16[24,8,4096]{2,1,0:T(8,128)(2,1)} %bitcast.37, bf16[24,8,4096]{2,1,0:T(8,128)(2,1)} %bitcast.38, bf16[64,4096]{1,0:T(8,128)(2,1)} %bitcast.39, ...), custom_call_target="tpu_custom_call" | custom-call | tf_op jit(solution)/shard_map/project/pallas_call | solution.py:389
  4.3 0.5 %collective-permute-start = (bf16[4,16,1024]{2,1,0:T(8,128)(2,1)S(1)}, bf16[4,16,1024]{2,1,0:T(8,128)(2,1)S(1)}, u32[]{:S(2)}, u32[]{:S(2)}) collective-permute-start(bf16[4,16,1024]{2,1,0:T(8,128)(2,1)S(1)} %get-tuple-element.22.payload.refs_0_), channel_id=1, source_target_pairs={{0,1},{1,0},{2,3},{3,2},{4,5},{5,4},{6,7},{7,6},{8,9},{9,8},{10,11... | collective-permute-start | bytes 393224 | tf_op jit(solution)/shard_map/ppermute | solution.py:349
  4.9 1.0 %collective-permute-done.refs_1_ = bf16[4,16,1024]{2,1,0:T(8,128)(2,1)S(1)} collective-permute-done((bf16[4,16,1024]{2,1,0:T(8,128)(2,1)S(1)}, bf16[4,16,1024]{2,1,0:T(8,128)(2,1)S(1)}, u32[]{:S(2)}, u32[]{:S(2)}) %collective-permute-start) | collective-permute-done | bytes 131104 | tf_op jit(solution)/shard_map/ppermute | solution.py:349
  5.9 4.0 %collective-permute-start.1 = (bf16[32,1024]{1,0:T(8,128)(2,1)S(1)}, bf16[32,1024]{1,0:T(8,128)(2,1)S(1)}, u32[]{:S(2)}, u32[]{:S(2)}) collective-permute-start(bf16[32,1024]{1,0:T(8,128)(2,1)S(1)} %pad_maximum_fusion.1), channel_id=1, source_target_pairs={{0,8},{1,11},{2,10},{3,9},{4,12},{5,15},{6,14},{7,13},{8,0},{9,3},... | collective-permute-start | bytes 196616 | tf_op jit(solution)/shard_map/ppermute | solution.py:353
  9.9 1.6 %collective-permute-start.2 = (bf16[32,1024]{1,0:T(8,128)(2,1)S(1)}, bf16[32,1024]{1,0:T(8,128)(2,1)S(1)}, u32[]{:S(2)}, u32[]{:S(2)}) collective-permute-start(bf16[32,1024]{1,0:T(8,128)(2,1)S(1)} %pad_maximum_fusion.2), channel_id=1, source_target_pairs={{0,4},{1,7},{2,6},{3,5},{4,0},{5,3},{6,2},{7,1},{8,12},{9,15},{10,... | collective-permute-start | bytes 196616 | tf_op jit(solution)/shard_map/ppermute | solution.py:353
  11.5 0.0 collective-permute-start.4
  11.5 1.7 %collective-permute-start.3 = (bf16[16,1024]{1,0:T(8,128)(2,1)S(1)}, bf16[16,1024]{1,0:T(8,128)(2,1)S(1)}, u32[]{:S(2)}, u32[]{:S(2)}) collective-permute-start(bf16[16,1024]{1,0:T(8,128)(2,1)S(1)} %get-tuple-element.40), channel_id=1, source_target_pairs={{0,2},{1,3},{2,0},{3,1},{4,6},{5,7},{6,4},{7,5},{8,10},{9,11},{10,... | collective-permute-start | bytes 98312 | tf_op jit(solution)/shard_map/ppermute | solution.py:353
  13.8 2.1 %norms.1 = (bf16[8,192,1024]{2,1,0:T(8,128)(2,1)S(1)}, f32[192,128]{1,0:T(8,128)S(1)}, f32[24,128]{1,0:T(8,128)S(1)}, f32[8,128]{1,0:T(8,128)S(1)}) custom-call(s32[1]{0:T(128)S(6)} %copy.19.present, bf16[1,192,8192]{2,1,0:T(8,128)(2,1)} %targets.1, bf16[4,16,1024]{2,1,0:T(8,128)(2,1)S(1)} %get-tuple-element.22.payload.refs_0_, ...), custom_call_target="tpu_custom_call" | custom-call | flops 6291456 | bytes 6291456 | tf_op jit(solution)/shard_map/norms/pallas_call | solution.py:429
  15.9 0.0 collective-permute-done.3.refs_4_
  16.0 0.0 collective-permute-done.1.refs_2_
  16.0 0.0 collective-permute-done.2.refs_3_
  16.0 1.9 %collective-permute-done.4.refs_5_ = bf16[32,1024]{1,0:T(8,128)(2,1)S(1)} collective-permute-done((bf16[32,1024]{1,0:T(8,128)(2,1)S(1)}, bf16[32,1024]{1,0:T(8,128)(2,1)S(1)}, u32[]{:S(2)}, u32[]{:S(2)}) %collective-permute-start.4) | collective-permute-done | bytes 65568 | tf_op jit(solution)/shard_map/ppermute | solution.py:353
  17.9 0.2 collective-permute-start.5
  18.1 1.4 %collective-permute-done.5.refs_6_ = bf16[112,1024]{1,0:T(8,128)(2,1)S(1)} collective-permute-done((bf16[112,1024]{1,0:T(8,128)(2,1)S(1)}, bf16[112,1024]{1,0:T(8,128)(2,1)S(1)}, u32[]{:S(2)}, u32[]{:S(2)}) %collective-permute-start.5) | collective-permute-done | bytes 229408 | tf_op jit(solution)/shard_map/ppermute | solution.py:355
  19.4 1.3 %score.1 = (f32[5,2,1,128]{3,2,1,0:T(1,128)S(1)}, f32[5,2,1,128]{3,2,1,0:T(1,128)S(1)}) custom-call(bf16[8,192,1024]{2,1,0:T(8,128)(2,1)S(1)} %get-tuple-element.30.stacked, f32[192,128]{1,0:T(8,128)S(1)} %get-tuple-element.31.inverse, f32[8,128]{1,0:T(8,128)S(1)} %get-tuple-element.32.counts, bf16[4,16,1024]{2,1,0:T(8,128)(2,1)S(1)} %get-tuple-element.22.payload.refs_0_, ...), custom_call_target="tpu_custom_call" | custom-call | tf_op jit(solution)/shard_map/score/pallas_call | solution.py:452
  20.8 0.1 collective-permute-start.6
  20.9 1.0 %collective-permute-done.6 = f32[5,2,1,128]{3,1,2,0:T(2,128)S(1)} collective-permute-done((f32[5,2,1,128]{3,1,2,0:T(2,128)S(1)}, f32[5,2,1,128]{3,1,2,0:T(2,128)S(1)}, u32[]{:S(2)}, u32[]{:S(2)}) %collective-permute-start.6) | collective-permute-done | bytes 5152 | tf_op jit(solution)/shard_map/ppermute | solution.py:339
  22.0 2.2 %collective-permute-start.10 = (f32[2,1,128]{2,1,0:T(1,128)S(1)}, f32[2,1,128]{2,1,0:T(1,128)S(1)}, u32[]{:S(2)}, u32[]{:S(2)}) collective-permute-start(f32[2,1,128]{2,1,0:T(1,128)S(1)} %bitcast.43), channel_id=1, source_target_pairs={{0,12},{1,15},{2,14},{3,13},{4,8},{5,11},{6,10},{7,9},{8,4},{9,7},... | collective-permute-start | bytes 3080 | tf_op jit(solution)/shard_map/ppermute | solution.py:342
  24.2 0.0 collective-permute-start.8
  24.2 2.2 %collective-permute-start.9 = (f32[2,1,128]{2,1,0:T(1,128)S(1)}, f32[2,1,128]{2,1,0:T(1,128)S(1)}, u32[]{:S(2)}, u32[]{:S(2)}) collective-permute-start(f32[2,1,128]{2,1,0:T(1,128)S(1)} %bitcast.41), channel_id=1, source_target_pairs={{0,4},{1,7},{2,6},{3,5},{4,0},{5,3},{6,2},{7,1},{8,12},{9,15},{10,... | collective-permute-start | bytes 3080 | tf_op jit(solution)/shard_map/ppermute | solution.py:342
  26.4 1.4 %collective-permute-start.7 = (f32[2,1,128]{2,0,1:T(2,128)S(1)}, f32[2,1,128]{2,0,1:T(2,128)S(1)}, u32[]{:S(2)}, u32[]{:S(2)}) collective-permute-start(f32[2,1,128]{2,0,1:T(2,128)S(1)} %get-tuple-element.49), channel_id=1, source_target_pairs={{0,2},{1,3},{2,0},{3,1},{4,6},{5,7},{6,4},{7,5},{8,10},{9,11},{10,... | collective-permute-start | bytes 3080 | tf_op jit(solution)/shard_map/ppermute | solution.py:342
  27.8 0.0 collective-permute-done.10
  27.8 0.9 %collective-permute-done.8 = f32[2,1,128]{2,1,0:T(1,128)S(1)} collective-permute-done((f32[2,1,128]{2,1,0:T(1,128)S(1)}, f32[2,1,128]{2,1,0:T(1,128)S(1)}, u32[]{:S(2)}, u32[]{:S(2)}) %collective-permute-start.8) | collective-permute-done | bytes 1056 | tf_op jit(solution)/shard_map/ppermute | solution.py:342
  28.6 0.0 collective-permute-done.9
  28.7 0.1 collective-permute-start.11
  28.8 1.2 %collective-permute-done.7 = f32[2,1,128]{2,0,1:T(2,128)S(1)} collective-permute-done((f32[2,1,128]{2,0,1:T(2,128)S(1)}, f32[2,1,128]{2,0,1:T(2,128)S(1)}, u32[]{:S(2)}, u32[]{:S(2)}) %collective-permute-start.7) | collective-permute-done | bytes 1056 | tf_op jit(solution)/shard_map/ppermute | solution.py:342
  30.0 0.0 collective-permute-done.11.refs_3_
  30.0 0.6 %finish.1 = f32[24]{0:T(128)} custom-call(f32[24,128]{1,0:T(8,128)S(1)} %get-tuple-element.29.picks, f32[24,128]{1,0:T(8,128)S(1)} %get-tuple-element.24.member, f32[2,1,128]{2,1,0:T(1,128)S(1)} %bitcast.34, f32[2,1,128]{2,1,0:T(1,128)S(1)} %bitcast.35, f32[2,1,128]{2,1,0:T(1,128)S(1)} %broadcast_select_fusion.refs_2_, ...), custom_call_target="tpu_custom_call" | custom-call | tf_op jit(solution)/shard_map/finish/pallas_call | solution.py:466
  (10 shorter events, 0.1 us)
Async XLA Ops:
  4.3 1.5 %collective-permute-start = (bf16[4,16,1024]{2,1,0:T(8,128)(2,1)S(1)}, bf16[4,16,1024]{2,1,0:T(8,128)(2,1)S(1)}, u32[]{:S(2)}, u32[]{:S(2)}) collective-permute-start(bf16[4,16,1024]{2,1,0:T(8,128)(2,1)S(1)} %get-tuple-element.22.payload.refs_0_), channel_id=1, source_target_pairs={{0,1},{1,0},{2,3},{3,2},{4,5},{5,4},{6,7},{7,6},{8,9},{9,8},{10,11... | collective-permute-start | bytes 393224 | tf_op jit(solution)/shard_map/ppermute | solution.py:349
  5.9 10.1 %collective-permute-start.1 = (bf16[32,1024]{1,0:T(8,128)(2,1)S(1)}, bf16[32,1024]{1,0:T(8,128)(2,1)S(1)}, u32[]{:S(2)}, u32[]{:S(2)}) collective-permute-start(bf16[32,1024]{1,0:T(8,128)(2,1)S(1)} %pad_maximum_fusion.1), channel_id=1, source_target_pairs={{0,8},{1,11},{2,10},{3,9},{4,12},{5,15},{6,14},{7,13},{8,0},{9,3},... | collective-permute-start | bytes 196616 | tf_op jit(solution)/shard_map/ppermute | solution.py:353
  9.9 6.1 %collective-permute-start.2 = (bf16[32,1024]{1,0:T(8,128)(2,1)S(1)}, bf16[32,1024]{1,0:T(8,128)(2,1)S(1)}, u32[]{:S(2)}, u32[]{:S(2)}) collective-permute-start(bf16[32,1024]{1,0:T(8,128)(2,1)S(1)} %pad_maximum_fusion.2), channel_id=1, source_target_pairs={{0,4},{1,7},{2,6},{3,5},{4,0},{5,3},{6,2},{7,1},{8,12},{9,15},{10,... | collective-permute-start | bytes 196616 | tf_op jit(solution)/shard_map/ppermute | solution.py:353
  11.5 6.4 %collective-permute-start.4 = (bf16[32,1024]{1,0:T(8,128)(2,1)S(1)}, bf16[32,1024]{1,0:T(8,128)(2,1)S(1)}, u32[]{:S(2)}, u32[]{:S(2)}) collective-permute-start(bf16[32,1024]{1,0:T(8,128)(2,1)S(1)} %pad_maximum_fusion.3), channel_id=1, source_target_pairs={{0,12},{1,15},{2,14},{3,13},{4,8},{5,11},{6,10},{7,9},{8,4},{9,7},... | collective-permute-start | bytes 196616 | tf_op jit(solution)/shard_map/ppermute | solution.py:353
  11.5 4.5 %collective-permute-start.3 = (bf16[16,1024]{1,0:T(8,128)(2,1)S(1)}, bf16[16,1024]{1,0:T(8,128)(2,1)S(1)}, u32[]{:S(2)}, u32[]{:S(2)}) collective-permute-start(bf16[16,1024]{1,0:T(8,128)(2,1)S(1)} %get-tuple-element.40), channel_id=1, source_target_pairs={{0,2},{1,3},{2,0},{3,1},{4,6},{5,7},{6,4},{7,5},{8,10},{9,11},{10,... | collective-permute-start | bytes 98312 | tf_op jit(solution)/shard_map/ppermute | solution.py:353
  17.9 1.6 %collective-permute-start.5 = (bf16[112,1024]{1,0:T(8,128)(2,1)S(1)}, bf16[112,1024]{1,0:T(8,128)(2,1)S(1)}, u32[]{:S(2)}, u32[]{:S(2)}) collective-permute-start(bf16[112,1024]{1,0:T(8,128)(2,1)S(1)} %pad_maximum_fusion), channel_id=1, source_target_pairs={{0,1},{1,0},{2,3},{3,2},{4,5},{5,4},{6,7},{7,6},{8,9},{9,8},{10,11... | collective-permute-start | bytes 688136 | tf_op jit(solution)/shard_map/ppermute | solution.py:355
  20.8 1.2 %collective-permute-start.6 = (f32[5,2,1,128]{3,1,2,0:T(2,128)S(1)}, f32[5,2,1,128]{3,1,2,0:T(2,128)S(1)}, u32[]{:S(2)}, u32[]{:S(2)}) collective-permute-start(f32[5,2,1,128]{3,1,2,0:T(2,128)S(1)} %bitcast.36), channel_id=1, source_target_pairs={{0,1},{1,0},{2,3},{3,2},{4,5},{5,4},{6,7},{7,6},{8,9},{9,8},{10,11... | collective-permute-start | bytes 15368 | tf_op jit(solution)/shard_map/ppermute | solution.py:339
  22.0 5.8 %collective-permute-start.10 = (f32[2,1,128]{2,1,0:T(1,128)S(1)}, f32[2,1,128]{2,1,0:T(1,128)S(1)}, u32[]{:S(2)}, u32[]{:S(2)}) collective-permute-start(f32[2,1,128]{2,1,0:T(1,128)S(1)} %bitcast.43), channel_id=1, source_target_pairs={{0,12},{1,15},{2,14},{3,13},{4,8},{5,11},{6,10},{7,9},{8,4},{9,7},... | collective-permute-start | bytes 3080 | tf_op jit(solution)/shard_map/ppermute | solution.py:342
  24.2 4.5 %collective-permute-start.8 = (f32[2,1,128]{2,1,0:T(1,128)S(1)}, f32[2,1,128]{2,1,0:T(1,128)S(1)}, u32[]{:S(2)}, u32[]{:S(2)}) collective-permute-start(f32[2,1,128]{2,1,0:T(1,128)S(1)} %bitcast.42), channel_id=1, source_target_pairs={{0,8},{1,11},{2,10},{3,9},{4,12},{5,15},{6,14},{7,13},{8,0},{9,3},... | collective-permute-start | bytes 3080 | tf_op jit(solution)/shard_map/ppermute | solution.py:342
  24.2 4.4 %collective-permute-start.9 = (f32[2,1,128]{2,1,0:T(1,128)S(1)}, f32[2,1,128]{2,1,0:T(1,128)S(1)}, u32[]{:S(2)}, u32[]{:S(2)}) collective-permute-start(f32[2,1,128]{2,1,0:T(1,128)S(1)} %bitcast.41), channel_id=1, source_target_pairs={{0,4},{1,7},{2,6},{3,5},{4,0},{5,3},{6,2},{7,1},{8,12},{9,15},{10,... | collective-permute-start | bytes 3080 | tf_op jit(solution)/shard_map/ppermute | solution.py:342
  26.4 3.6 %collective-permute-start.7 = (f32[2,1,128]{2,0,1:T(2,128)S(1)}, f32[2,1,128]{2,0,1:T(2,128)S(1)}, u32[]{:S(2)}, u32[]{:S(2)}) collective-permute-start(f32[2,1,128]{2,0,1:T(2,128)S(1)} %get-tuple-element.49), channel_id=1, source_target_pairs={{0,2},{1,3},{2,0},{3,1},{4,6},{5,7},{6,4},{7,5},{8,10},{9,11},{10,... | collective-permute-start | bytes 3080 | tf_op jit(solution)/shard_map/ppermute | solution.py:342
  28.7 1.3 %collective-permute-start.11 = (f32[2,1,128]{2,1,0:T(1,128)S(1)}, f32[2,1,128]{2,1,0:T(1,128)S(1)}, u32[]{:S(2)}, u32[]{:S(2)}) collective-permute-start(f32[2,1,128]{2,1,0:T(1,128)S(1)} %broadcast_select_fusion.refs_2_), channel_id=1, source_target_pairs={{0,1},{1,0},{2,3},{3,2},{4,5},{5,4},{6,7},{7,6},{8,9},{9,8},{10,11... | collective-permute-start | bytes 3080 | tf_op jit(solution)/shard_map/ppermute | solution.py:345
